TPU v7x, 256 devices: a whole 4x4x8 slice. The times are simulated.
256 devices in a mesh: grp: 4 (over z_lo), seq: 64 (over x, y, z_hi, core).
Axes of the slice: x: 4, y: 4, z: 8 (z_hi: 2, z_lo: 4; z = z_hi * 4 + z_lo), core: 2. Of those that a mesh axis runs over, the one named last changes fastest.
Arguments:
- main_query: bfloat16 [64, 128, 2560], P('seq', 'grp'), may hold values from -150 to 150
- main_key: bfloat16 [64, 128, 2560], P('seq', 'grp'), may hold values from -4 to 4
- main_value: bfloat16 [64, 128, 2560], P('seq', 'grp'), may hold values from -240 to 240
- guide_query: bfloat16 [64, 128, 1024], P('seq', None, 'grp'), may hold values from -150 to 150
- guide_key: bfloat16 [64, 128, 1024], P('seq', None, 'grp'), may hold values from -4 to 4
- guide_value: bfloat16 [64, 128, 1024], P('seq', None, 'grp'), may hold values from -240 to 240
- latents: float32 [64, 128, 64], P('seq', 'grp'), may hold values from -6 to 6
- step_index: int32 [1], replicated, may hold values from 0 to 49
- main_mod: bfloat16 [50, 2, 2560], replicated, may hold values from -3 to 3
- guide_mod: bfloat16 [50, 2, 1024], replicated, may hold values from -3 to 3
- main_head: bfloat16 [2560, 64], replicated, may hold values from -0.125 to 0.125
- guide_head: bfloat16 [1024, 64], replicated, may hold values from -0.1875 to 0.1875
Outputs:
- velocity: float32 [64, 128, 64], P('seq', 'grp')
- next_latents: float32 [64, 128, 64], P('seq', 'grp')
All inputs are finite; a program needn't handle non-finite values.
Results may differ from a plain program's by a relative error of at most 0.012.
Values may be sent and summed in bfloat16 or wider, within the bound.
No kernel may reach another device: no remote copies, remote signals or barrier semaphores. Data moves between devices by JAX's collectives and lax.ppermute only.
A program may use at most 128 MiB of HBM per device.

v0:
```python
import math

import jax
import jax.numpy as jnp
from jax import lax
from jax.sharding import PartitionSpec as P

HD = 128
STEPS = 50


guidance = 2.5
flow_shift = 3.0
epsilon = 1e-06
very_low = -1e30


def sigma_at(index):
    remaining = 1.0 - index.astype(jnp.float32) / STEPS
    return flow_shift * remaining / (1.0 + (flow_shift - 1.0) * remaining)


def fresh_state(queries):
    rows, heads, depth = queries.shape
    return (
        jnp.full((heads, rows), very_low, jnp.float32),
        jnp.zeros((heads, rows), jnp.float32),
        jnp.zeros((rows, heads, depth), jnp.float32),
    )


def fold_keys(carried, queries, keys, values):
    rows, heads, depth = queries.shape
    length = keys.shape[1]
    block = math.gcd(length, 512)
    key_blocks = keys.reshape(length // block, block, heads, depth)
    value_blocks = values.reshape(length // block, block, heads, depth)
    factor = 1.0 / math.sqrt(depth)

    def one_block(running, blocks):
        highest, weight_sum, numerator = running
        key_block, value_block = blocks
        scores = (
            jnp.einsum("rhd,bhd->hrb", queries, key_block, preferred_element_type=jnp.float32)
            * factor
        )
        raised = jnp.maximum(highest, jnp.max(scores, axis=-1))
        shrink = jnp.exp(highest - raised)
        weights = jnp.exp(scores - raised[:, :, None])
        weight_sum = weight_sum * shrink + jnp.sum(weights, axis=-1)
        numerator = numerator * jnp.transpose(shrink)[:, :, None] + jnp.einsum(
            "hrb,bhd->rhd",
            weights.astype(jnp.bfloat16),
            value_block,
            preferred_element_type=jnp.float32,
        )
        return ((raised, weight_sum, numerator), None)

    carried, unused = lax.scan(one_block, carried, (key_blocks, value_blocks))
    return carried


def finish_state(carried):
    highest, weight_sum, numerator = carried
    rows, heads, depth = numerator.shape
    result = numerator / jnp.transpose(weight_sum)[:, :, None]
    return lax.optimization_barrier(result.reshape(rows, heads * depth).astype(jnp.bfloat16))


def table_row(table, step_now):
    return lax.dynamic_index_in_dim(table, step_now, 0, keepdims=False).astype(jnp.float32)


def project_whole(attended, table, step_now, weight):
    row_now = table_row(table, step_now)
    values = attended.astype(jnp.float32)
    center = jnp.mean(values, axis=-1, keepdims=True)
    centered = values - center
    spread = jnp.mean(centered * centered, axis=-1, keepdims=True)
    normed = centered * lax.rsqrt(spread + epsilon)
    modulated = normed * (1.0 + row_now[1]) + row_now[0]
    return jnp.dot(modulated, weight.astype(jnp.float32), precision=lax.Precision.HIGHEST)


def on_device(
    main_query,
    main_key,
    main_value,
    guide_query,
    guide_key,
    guide_value,
    latents,
    step_index,
    main_mod,
    guide_mod,
    main_head,
    guide_head,
):
    step_now = step_index[0]
    moved_query, moved_key, moved_value = (
        lax.all_to_all(main_query, "grp", split_axis=2, concat_axis=1, tiled=True),
        lax.all_to_all(main_key, "grp", split_axis=2, concat_axis=1, tiled=True),
        lax.all_to_all(main_value, "grp", split_axis=2, concat_axis=1, tiled=True),
    )
    rows = moved_query.shape[1]
    main_queries = moved_query[0].reshape(rows, moved_query.shape[2] // HD, HD)
    guide_queries = guide_query[0].reshape(rows, guide_query.shape[2] // HD, HD)
    pieces = (
        lax.all_gather(moved_key, "seq", axis=1, tiled=True),
        lax.all_gather(moved_value, "seq", axis=1, tiled=True),
    )
    main_state = fold_keys(fresh_state(main_queries), main_queries, pieces[0], pieces[1])
    pieces = (
        lax.all_gather(guide_key, "seq", axis=1, tiled=True),
        lax.all_gather(guide_value, "seq", axis=1, tiled=True),
    )
    guide_state = fold_keys(fresh_state(guide_queries), guide_queries, pieces[0], pieces[1])
    main_out = finish_state(main_state)
    guide_out = finish_state(guide_state)
    main_back, guide_back = (
        lax.all_to_all(main_out[None], "grp", split_axis=1, concat_axis=2, tiled=True),
        lax.all_to_all(guide_out[None], "grp", split_axis=1, concat_axis=2, tiled=True),
    )
    main_flow = project_whole(main_back[0], main_mod, step_now, main_head)[None]
    guide_flow = project_whole(guide_back[0], guide_mod, step_now, guide_head)[None]
    velocity = guide_flow + guidance * (main_flow - guide_flow)
    advanced = latents + (sigma_at(step_now + 1) - sigma_at(step_now)) * velocity
    return (velocity, advanced)


def solution(mesh):
    return jax.shard_map(
        on_device,
        mesh=mesh,
        in_specs=(
            P("seq", "grp", None),
            P("seq", "grp", None),
            P("seq", "grp", None),
            P("seq", None, "grp"),
            P("seq", None, "grp"),
            P("seq", None, "grp"),
            P("seq", "grp", None),
            P(),
            P(),
            P(),
            P(),
            P(),
        ),
        out_specs=(P("seq", "grp", None), P("seq", "grp", None)),
        check_vma=False,
    )
```

profile of v0, /device:TPU:24, one launch (start us, length us, event | category | flops | bytes accessed | tf_op | source)
XLA Modules:
  0.0 556.5 jit_solution(1689155577458871130)
XLA Ops:
  8.7 2.2 copy.93
  11.5 14.2 %reduce.17 = bf16[2560,32]{1,0:T(8,128)(2,1)S(1)} reduce(bf16[2560,1,32]{2,1,0:T(2,128)(2,1)S(1)} %bitcast.105, bf16[]{:T(256)} %broadcast.157), dimensions={1}, to_apply=%bitcast.62.reduce_sub_computation | reduce | bytes 327682
  26.4 12.6 %all_to_all.69 = bf16[4,2,10240]{2,1,0:T(2,128)(2,1)S(1)} all-to-all(bf16[4,2,10240]{2,1,0:T(2,128)(2,1)S(1)} %reshape.113), channel_id=1, replica_groups=mesh['grp'=4,'seq'=64] {'grp'}, dimensions={0} | all-to-all | bytes 327680 | tf_op jit(solution)/shard_map/all_to_all | solution.py:102
  42.3 14.3 %reduce.19 = bf16[2560,32]{1,0:T(8,128)(2,1)S(1)} reduce(bf16[2560,1,32]{2,1,0:T(2,128)(2,1)S(1)} %bitcast.109, bf16[]{:T(256)} %broadcast.157), dimensions={1}, to_apply=%bitcast.66.reduce_sub_computation | reduce | bytes 327682
  57.9 3.5 all-to-all-start.3
  63.7 14.3 %reduce.18 = bf16[2560,32]{1,0:T(8,128)(2,1)S(1)} reduce(bf16[2560,1,32]{2,1,0:T(2,128)(2,1)S(1)} %bitcast.110, bf16[]{:T(256)} %broadcast.157), dimensions={1}, to_apply=%bitcast.64.reduce_sub_computation | reduce | bytes 327682
  79.7 4.9 all-to-all-start.2
  87.6 17.8 %all-gather.5.cloned.1.call-done = bf16[1,8192,256]{2,1,0:T(8,128)(2,1)} async-done(((bf16[1,128,256]{2,1,0:T(8,128)(2,1)}), bf16[1,8192,256]{2,1,0:T(8,128)(2,1)}) %all-gather.5.cloned.1.call-update) | async-done | bytes 4194320 | tf_op jit(solution)/shard_map/all_gather | solution.py:114
  105.3 6.9 %reshape.105 = bf16[16,512,2,128]{3,2,1,0:T(2,128)(2,1)} reshape(bf16[1,8192,256]{2,1,0:T(8,128)(2,1)} %all-gather.5.cloned.1.call-done) | data formatting | bytes 8388608 | tf_op jit(solution)/shard_map/reshape | solution.py:36
  112.3 85.4 %all-gather.7.cloned.1.call-done = bf16[1,8192,256]{2,1,0:T(8,128)(2,1)} async-done(((bf16[1,128,256]{2,1,0:T(8,128)(2,1)}), bf16[1,8192,256]{2,1,0:T(8,128)(2,1)}) %all-gather.7.cloned.1.call-update) | async-done | bytes 4194320 | tf_op jit(solution)/shard_map/all_gather | solution.py:115
  197.7 6.9 %reshape.106 = bf16[16,512,2,128]{3,2,1,0:T(2,128)(2,1)} reshape(bf16[1,8192,256]{2,1,0:T(8,128)(2,1)} %all-gather.7.cloned.1.call-done) | data formatting | bytes 8388608 | tf_op jit(solution)/shard_map/reshape | solution.py:37
  204.6 35.6 %while.30 = (s32[]{:T(128)}, f32[2,128]{1,0:T(2,128)S(1)}, f32[2,128]{1,0:T(2,128)S(1)}, f32[128,2,128]{0,2,1:T(8,128)S(1)}, bf16[16,512,2,128]{3,2,1,0:T(2,128)...) while((s32[]{:T(128)}, f32[2,128]{1,0:T(2,128)S(1)}, ...), condition=%wide.region_3.4_spmd.clone, body=%wide.region_0.3_spmd.clone.sunk | while | flops 67995136 | bytes 4014189 | solution.py:59
  242.1 3.5 all-to-all-start
  247.5 3.6 all-to-all-done
  251.6 67.8 %all-gather.9.cloned.1.call-done = bf16[1,8192,640]{2,1,0:T(8,128)(2,1)} async-done(((bf16[1,128,640]{2,1,0:T(8,128)(2,1)}), bf16[1,8192,640]{2,1,0:T(8,128)(2,1)}) %all-gather.9.cloned.1.call-update) | async-done | bytes 10485776 | tf_op jit(solution)/shard_map/all_gather | solution.py:109
  319.4 23.6 %reshape.107 = bf16[16,512,5,128]{3,2,1,0:T(8,128)(2,1)} reshape(bf16[1,8192,640]{2,1,0:T(8,128)(2,1)} %all-gather.9.cloned.1.call-done) | data formatting | bytes 20971520 | tf_op jit(solution)/shard_map/reshape | solution.py:36
  342.9 12.4 %copy.104 = bf16[16,512,5,128]{3,1,2,0:T(8,128)(2,1)} copy(bf16[16,512,5,128]{3,2,1,0:T(8,128)(2,1)} %reshape.107) | data formatting | bytes 20971520
  355.4 84.5 %all-gather.11.cloned.1.call-done = bf16[1,8192,640]{2,1,0:T(8,128)(2,1)} async-done(((bf16[1,128,640]{2,1,0:T(8,128)(2,1)}), bf16[1,8192,640]{2,1,0:T(8,128)(2,1)}) %all-gather.11.cloned.1.call-update) | async-done | bytes 10485776 | tf_op jit(solution)/shard_map/all_gather | solution.py:110
  439.9 23.6 %reshape.108 = bf16[16,512,5,128]{3,2,1,0:T(8,128)(2,1)} reshape(bf16[1,8192,640]{2,1,0:T(8,128)(2,1)} %all-gather.11.cloned.1.call-done) | data formatting | bytes 20971520 | tf_op jit(solution)/shard_map/reshape | solution.py:37
  463.4 21.0 %copy.106 = bf16[16,512,5,128]{1,3,2,0:T(8,128)(2,1)} copy(bf16[16,512,5,128]{3,2,1,0:T(8,128)(2,1)} %reshape.108) | data formatting | bytes 20971520
  484.5 50.5 %while.31 = (s32[]{:T(128)}, f32[5,128]{1,0:T(8,128)S(1)}, f32[5,128]{1,0:T(8,128)S(1)}, f32[128,5,128]{0,2,1:T(8,128)S(1)}, bf16[16,512,5,128]{3,1,2,0:T(8,128)...) while((s32[]{:T(128)}, f32[5,128]{1,0:T(8,128)S(1)}, ...), condition=%wide.region_10.11_spmd.clone, body=%wide.region_7.0_spmd.clone.sunk | while | flops 169987840 | bytes 6104169 | solution.py:59
  489.1 1.5 fusion.84
  492.2 1.5 fusion.84
  498.6 1.5 fusion.84
  508.1 1.5 fusion.84
  511.2 1.5 fusion.84
  517.5 1.5 fusion.84
  520.7 1.5 fusion.84
  527.0 1.5 fusion.84
  535.3 1.6 reduce.20
  537.6 3.3 all-to-all-start.4
  541.4 6.5 %all-to-all-done.4 = bf16[4,2,10240]{2,1,0:T(2,128)(2,1)S(1)} async-done(((bf16[4,2,10240]{2,1,0:T(2,128)(2,1)}), bf16[4,2,10240]{2,1,0:T(2,128)(2,1)S(1)}, u32[]{:S(2)}, u32[]{:S(2)}) %all-to-all-start.4) | async-done | bytes 163872 | tf_op jit(solution)/shard_map/all_to_all | solution.py:121
  (300 shorter events, 93.6 us)
Async XLA Ops:
  7.2 541.7 %copy-start = (bf16[2560,64]{0,1:T(8,128)(2,1)S(1)}, bf16[2560,64]{0,1:T(8,128)(2,1)}, u32[]{:S(2)}) copy-start(bf16[2560,64]{0,1:T(8,128)(2,1)} %param.26) | copy-start | bytes 983044
  7.2 98.1 %all-gather.5.cloned.1.call-start = ((), (), s32[]{:S(2)}) async-start(), calls=%async_computation.5 | async-start | bytes 4259840 | tf_op jit(solution)/shard_map/all_gather | solution.py:114
  7.9 189.7 %all-gather.7.cloned.1.call-start = ((), (), s32[]{:S(2)}) async-start(), calls=%async_computation.6 | async-start | bytes 4259840 | tf_op jit(solution)/shard_map/all_gather | solution.py:115
  8.7 310.7 %all-gather.9.cloned.1.call-start = ((), (), s32[]{:S(2)}) async-start(), calls=%async_computation.7 | async-start | bytes 10649600 | tf_op jit(solution)/shard_map/all_gather | solution.py:109
  39.8 1.5 copy-start.1
  42.3 20.5 %copy-start.2 = (bf16[1,32,2560]{2,1,0:T(8,128)(2,1)S(1)}, bf16[1,32,2560]{2,1,0:T(8,128)(2,1)}, u32[]{:S(2)}) copy-start(bf16[1,32,2560]{2,1,0:T(8,128)(2,1)} %param.16) | copy-start | bytes 491524
  57.9 21.8 %all-to-all-start.3 = ((bf16[4,2,10240]{2,1,0:T(2,128)(2,1)}), bf16[4,2,10240]{2,1,0:T(2,128)(2,1)S(1)}, u32[]{:S(2)}, u32[]{:S(2)}) async-start(bf16[4,2,10240]{2,1,0:T(2,128)(2,1)} %reshape.117), calls=%async_computation.3 | async-start | bytes 327680 | tf_op jit(solution)/shard_map/all_to_all | solution.py:103
  63.7 15.6 %copy-start.4 = (bf16[1,128,256]{2,1,0:T(8,128)(2,1)S(1)}, bf16[1,128,256]{2,1,0:T(8,128)(2,1)}, u32[]{:S(2)}) copy-start(bf16[1,128,256]{2,1,0:T(8,128)(2,1)} %param.19) | copy-start | bytes 196612
  79.7 162.4 %all-to-all-start.2 = ((bf16[4,2,10240]{2,1,0:T(2,128)(2,1)}), bf16[4,2,10240]{2,1,0:T(2,128)(2,1)S(1)}, u32[]{:S(2)}, u32[]{:S(2)}) async-start(bf16[4,2,10240]{2,1,0:T(2,128)(2,1)} %reshape.115), calls=%async_computation.2 | async-start | bytes 327680 | tf_op jit(solution)/shard_map/all_to_all | solution.py:101
  84.6 355.3 %all-gather.11.cloned.1.call-start = ((), (), s32[]{:S(2)}) async-start(), calls=%async_computation.8 | async-start | bytes 10649600 | tf_op jit(solution)/shard_map/all_gather | solution.py:110
  242.1 9.0 %all-to-all-start = ((bf16[4,2,4096]{2,1,0:T(2,128)(2,1)}), bf16[4,2,4096]{2,1,0:T(2,128)(2,1)S(1)}, u32[]{:S(2)}, u32[]{:S(2)}) async-start(bf16[4,2,4096]{2,1,0:T(2,128)(2,1)} %reshape.111), calls=%async_computation | async-start | bytes 131072 | tf_op jit(solution)/shard_map/all_to_all | solution.py:122
  535.0 6.1 %copy-start.3 = (bf16[1024,64]{0,1:T(8,128)(2,1)S(1)}, bf16[1024,64]{0,1:T(8,128)(2,1)}, u32[]{:S(2)}) copy-start(bf16[1024,64]{0,1:T(8,128)(2,1)} %param.27) | copy-start | bytes 393220
  537.6 10.4 %all-to-all-start.4 = ((bf16[4,2,10240]{2,1,0:T(2,128)(2,1)}), bf16[4,2,10240]{2,1,0:T(2,128)(2,1)S(1)}, u32[]{:S(2)}, u32[]{:S(2)}) async-start(bf16[4,2,10240]{2,1,0:T(2,128)(2,1)} %reshape.119), calls=%async_computation.4 | async-start | bytes 327680 | tf_op jit(solution)/shard_map/all_to_all | solution.py:121
  548.1 0.8 copy-start.5
Sparse Core Ops, SparseCore 0:
  11.5 93.7 all-gather.4
  108.8 88.8 all-gather.6
  201.1 118.1 all-gather.8
  322.7 117.1 all-gather.10
where the time goes:
time: 562 us; the launch traced here: 557 us
  waiting for transfers between devices  267 us (48%)
  local copies, waits for them, and re-layouts  136 us (24%)
  matrix products  55.4 us (10%)
  other arithmetic  52.9 us (9%)
  starting transfers between devices  15.4 us (3%)
  between operations  15 us (3%)
  blocking collectives  12.6 us (2%)
    all_gather x1, waiting for transfers between devices, on_device(): lax.all_gather(guide_value, 'seq', axis=1, tiled=True)  85.4 us
    all_gather x1, waiting for transfers between devices, on_device(): lax.all_gather(moved_value, 'seq', axis=1, tiled=True)  84.5 us
    all_gather x1, waiting for transfers between devices, on_device(): lax.all_gather(moved_key, 'seq', axis=1, tiled=True)  67.8 us
    unnamed x33, local copies, waits for them, and re-layouts  45.6 us
    unnamed x11, other arithmetic  45.4 us
    reshape x2, local copies, waits for them, and re-layouts, fold_keys(): key_blocks = keys.reshape(length // block, block, heads, depth)  30.5 us
    reshape x2, local copies, waits for them, and re-layouts, fold_keys(): value_blocks = values.reshape(length // block, block, heads, depth)  30.5 us
    dot_general x32, matrix products, one_block(): jnp.einsum('hrb,bhd->rhd', weights.astype(jnp.bfloat16), value_block, pre...  27.2 us
  transfers between devices with their start and end apart: 8, of which 6 were waited for; matrix products, arithmetic and copies ran while one was open for 26% of the time, Pallas kernels for 0%

commit v1 on v0

v1 whole, which is shorter than its diff:
```python
import math

import jax
import jax.numpy as jnp
from jax import lax
from jax.experimental import pallas as pl
from jax.experimental.pallas import tpu as pltpu
from jax.sharding import Mesh, PartitionSpec as P

HD = 128
STEPS = 50
ZL, X, Y, ZH, CORE = 4, 4, 4, 2, 2
Z = ZL * ZH
ROWS = 32
TOKENS = ROWS * Z
BLOCK = 128
FULL = 3
HALF = TOKENS // 2
QROWS = FULL * TOKENS + HALF
STAT = 32
OROWS = QROWS + STAT
PIECES = Y * CORE
KEYS = PIECES * TOKENS

guidance = 2.5
flow_shift = 3.0
epsilon = 1e-06
score_scale = math.log2(math.e) / math.sqrt(HD)

f32 = jnp.float32
bf16 = jnp.bfloat16
VMEM = pl.BlockSpec(memory_space=pltpu.VMEM)
SMEM = pl.BlockSpec(memory_space=pltpu.SMEM)


def params(mib):
    return pltpu.CompilerParams(vmem_limit_bytes=mib * 1024 * 1024)


def head_of(zh, zl, slot):
    return zl * 5 + (4 if slot == 2 else 2 * zh + slot)


def pack_kernel(half, mq, mk, mv, gq, gk, gv, send, guide_send, guide_own):
    zh = half[0]
    for zh_to in range(ZH):
        for zl_to in range(ZL):
            to = zh_to * ZL + zl_to
            for kind, ref in enumerate((mq, mk, mv)):
                for slot in range(3):
                    head = head_of(zh_to, zl_to, slot)
                    send[to, kind * 3 + slot] = ref[0, :, head * HD : (head + 1) * HD]
    own = pl.ds(pl.multiple_of(zh * HD, HD), HD)
    other = pl.ds(pl.multiple_of((1 - zh) * HD, HD), HD)
    for kind, ref in enumerate((gq, gk, gv)):
        guide_own[kind] = ref[0, :, own]
        guide_send[kind] = ref[0, :, other]


def unpack_kernel(half, got, guide_own, guide_got, queries, pairs):
    zh = half[0]
    for source in range(Z):
        rows = pl.ds(source * ROWS, ROWS)
        for slot in range(2):
            queries[pl.ds(slot * TOKENS + source * ROWS, ROWS), :] = got[source, slot]
        for kind in range(2):
            for slot, place in ((0, 0), (1, 1), (2, 3)):
                pairs[kind * 4 + place, rows, :] = got[source, (kind + 1) * 3 + slot]
    for zl in range(ZL):
        queries[pl.ds(FULL * TOKENS + zl * ROWS, ROWS), :] = got[zh * ZL + zl, 2]
    for ref, place in ((guide_own, zh), (guide_got, 1 - zh)):
        at = pl.multiple_of(place * BLOCK, BLOCK)
        queries[pl.ds(2 * TOKENS + at, BLOCK), :] = ref[0]
        pairs[2, pl.ds(at, BLOCK), :] = ref[1]
        pairs[6, pl.ds(at, BLOCK), :] = ref[2]


def diagonal():
    return lax.broadcasted_iota(jnp.int32, (HD, HD), 0) == lax.broadcasted_iota(
        jnp.int32, (HD, HD), 1
    )


def attend_kernel(*refs):
    queries, pairs = refs[:X], refs[X : X + PIECES]
    outs = refs[X + PIECES : 2 * X + PIECES]
    keys, values, scores, weights, stats = refs[2 * X + PIECES :]
    for piece in range(PIECES):
        rows = pl.ds(piece * TOKENS, TOKENS)
        for head in range(4):
            keys[head, rows, :] = pairs[piece][head]
            values[head, rows, :HD] = pairs[piece][4 + head]
            values[head, rows, HD:] = jnp.ones((TOKENS, HD), bf16)
    on_diagonal = diagonal()

    def score_tile(place, query, head):
        size = query.shape[0]
        highest = None
        for piece in range(PIECES):
            part = lax.dot_general(
                query,
                keys[head, pl.ds(piece * TOKENS, TOKENS), :],
                (((1,), (1,)), ((), ())),
                preferred_element_type=f32,
            )
            scores[place, :size, pl.ds(piece * TOKENS, TOKENS)] = part
            here = jnp.maximum(part[:, :HD], part[:, HD:])
            highest = here if highest is None else jnp.maximum(highest, here)
        return jnp.max(highest, axis=1, keepdims=True) * score_scale

    def weight_tile(place, size, highest, head):
        for piece in range(PIECES):
            columns = pl.ds(piece * TOKENS, TOKENS)
            part = scores[place, :size, columns]
            weights[place, :size, columns] = jnp.exp2(part * score_scale - highest).astype(bf16)
        return jnp.dot(weights[place, :size, :], values[head], preferred_element_type=f32)

    def store_tile(source, start, size, highest, total, first_stat):
        weight_sum = total[:, HD:]
        outs[source][pl.ds(start, size), :] = (total[:, :HD] / weight_sum).astype(bf16)
        level = highest + jnp.log2(weight_sum)
        for part in range(size // HD):
            block = level[part * HD : (part + 1) * HD, :]
            row = jnp.sum(jnp.where(on_diagonal, block, 0.0), axis=0, keepdims=True)
            stats[source, pl.ds(first_stat + part, 1), :] = row

    def full_head(head, carry):
        start = pl.multiple_of(head * TOKENS, TOKENS)
        tops = [
            score_tile(source, queries[source][pl.ds(start, TOKENS), :], head)
            for source in range(X)
        ]
        for source in range(X):
            total = weight_tile(source, TOKENS, tops[source], head)
            store_tile(source, start, TOKENS, tops[source], total, head * 2)
        return carry

    stats[...] = jnp.zeros_like(stats)
    lax.fori_loop(0, FULL, full_head, 0)
    tops = [
        score_tile(source, queries[source][FULL * TOKENS :, :], FULL) for source in range(X)
    ]
    for source in range(X):
        total = weight_tile(source, HALF, tops[source], FULL)
        store_tile(source, FULL * TOKENS, HALF, tops[source], total, FULL * 2)
    for source in range(X):
        level = stats[source]
        high = level.astype(bf16).astype(f32)
        middle = (level - high).astype(bf16).astype(f32)
        low = level - high - middle
        block = jnp.concatenate([high, middle, low, jnp.zeros_like(low)], axis=0)
        outs[source][QROWS:, :] = block.astype(bf16)


def combine_kernel(*refs):
    parts, send = refs[:X], refs[X]
    on_diagonal = diagonal()
    levels = []
    for part in parts:
        block = part[QROWS:, :].astype(f32)
        levels.append(block[0:8] + block[8:16] + block[16:24])
    top = levels[0]
    for level in levels[1:]:
        top = jnp.maximum(top, level)
    shares = [jnp.exp2(level - top) for level in levels]
    whole = shares[0] + shares[1] + shares[2] + shares[3]
    shares = [share / whole for share in shares]
    for tile in range(QROWS // HD):
        total = None
        for part, share in zip(parts, shares):
            row = jnp.broadcast_to(share[tile : tile + 1, :], (HD, HD))
            column = jnp.sum(jnp.where(on_diagonal, row, 0.0), axis=1, keepdims=True)
            term = part[tile * HD : (tile + 1) * HD, :].astype(f32) * column
            total = term if total is None else total + term
        result = total.astype(bf16)
        for zl in range(ZL):
            rows = result[zl * ROWS : (zl + 1) * ROWS, :]
            if tile < FULL * 2:
                slot = (0, 1, 3)[tile // 2]
                send[(tile % 2) * ZL + zl, slot] = rows
            else:
                send[zl, 2] = rows
                send[ZL + zl, 2] = rows


def split_dot(left, weight):
    high = left.astype(bf16)
    low = (left - high.astype(f32)).astype(bf16)
    return jnp.dot(high, weight, preferred_element_type=f32) + jnp.dot(
        low, weight, preferred_element_type=f32
    )


def flow_of(heads, table, weight):
    width = len(heads) * HD
    center = sum(jnp.sum(h, axis=1, keepdims=True) for h in heads) / width
    centered = [h - center for h in heads]
    spread = sum(jnp.sum(h * h, axis=1, keepdims=True) for h in centered) / width
    shrink = lax.rsqrt(spread + epsilon)
    shift, scale = table[0, 0:1, :].astype(f32), table[0, 1:2, :].astype(f32)
    total = None
    for index, head in enumerate(centered):
        lanes = slice(index * HD, (index + 1) * HD)
        modulated = head * shrink * (1.0 + scale[:, lanes]) + shift[:, lanes]
        term = split_dot(modulated, weight[lanes, :])
        total = term if total is None else total + term
    return total


def sigma_at(index):
    remaining = 1.0 - index.astype(f32) / STEPS
    return flow_shift * remaining / (1.0 + (flow_shift - 1.0) * remaining)


def final_kernel(
    step, half, got, latents, main_mod, guide_mod, main_head, guide_head, velocity, advanced
):
    zh = half[0]
    main, guide = [], []
    for zl in range(ZL):
        main += [got[0 * ZL + zl, 0], got[0 * ZL + zl, 1]]
        main += [got[1 * ZL + zl, 0], got[1 * ZL + zl, 1]]
        main += [got[zh * ZL + zl, 2]]
        guide += [got[0 * ZL + zl, 3], got[1 * ZL + zl, 3]]
    main_flow = flow_of([h.astype(f32) for h in main], main_mod, main_head)
    guide_flow = flow_of([h.astype(f32) for h in guide], guide_mod, guide_head)
    result = guide_flow + guidance * (main_flow - guide_flow)
    now = jnp.full((1, 1), step[0], jnp.int32)
    velocity[0] = result
    advanced[0] = latents[0] + (sigma_at(now + 1) - sigma_at(now)) * result


def shifted(array, axis, size, by):
    return lax.ppermute(array, axis, [(i, (i + by) % size) for i in range(size)])


def on_device(
    main_query,
    main_key,
    main_value,
    guide_query,
    guide_key,
    guide_value,
    latents,
    step_index,
    main_mod,
    guide_mod,
    main_head,
    guide_head,
):
    half = lax.axis_index("zh").astype(jnp.int32).reshape(1)
    send, guide_send, guide_own = pl.pallas_call(
        pack_kernel,
        out_shape=(
            jax.ShapeDtypeStruct((Z, 9, ROWS, HD), bf16),
            jax.ShapeDtypeStruct((3, BLOCK, HD), bf16),
            jax.ShapeDtypeStruct((3, BLOCK, HD), bf16),
        ),
        in_specs=[SMEM] + [VMEM] * 6,
        out_specs=(VMEM,) * 3,
        compiler_params=params(16),
        name="pack",
    )(half, main_query, main_key, main_value, guide_query, guide_key, guide_value)
    guide_got = shifted(guide_send, "zh", ZH, 1)
    got = lax.all_to_all(send, ("zh", "zl"), split_axis=0, concat_axis=0, tiled=True)
    queries, pairs = pl.pallas_call(
        unpack_kernel,
        out_shape=(
            jax.ShapeDtypeStruct((QROWS, HD), bf16),
            jax.ShapeDtypeStruct((8, TOKENS, HD), bf16),
        ),
        in_specs=[SMEM] + [VMEM] * 3,
        out_specs=(VMEM,) * 2,
        compiler_params=params(16),
        name="unpack",
    )(half, got, guide_own, guide_got)

    own_pairs = [pairs] + [shifted(pairs, "y", Y, by) for by in (1, -1, 2)]
    all_queries = [queries] + [shifted(queries, "x", X, by) for by in (1, -1, 2)]
    all_pairs = own_pairs + [shifted(p, "core", CORE, 1) for p in own_pairs]
    parts = pl.pallas_call(
        attend_kernel,
        out_shape=(jax.ShapeDtypeStruct((OROWS, HD), bf16),) * X,
        in_specs=[VMEM] * (X + PIECES),
        out_specs=(VMEM,) * X,
        scratch_shapes=[
            pltpu.VMEM((4, KEYS, HD), bf16),
            pltpu.VMEM((4, KEYS, 2 * HD), bf16),
            pltpu.VMEM((X, TOKENS, KEYS), f32),
            pltpu.VMEM((X, TOKENS, KEYS), bf16),
            pltpu.VMEM((X, 8, HD), f32),
        ],
        compiler_params=params(48),
        name="attend",
    )(*all_queries, *all_pairs)
    back = [parts[0]] + [shifted(p, "x", X, -by) for p, by in zip(parts[1:], (1, -1, 2))]
    send = pl.pallas_call(
        combine_kernel,
        out_shape=jax.ShapeDtypeStruct((Z, 4, ROWS, HD), bf16),
        in_specs=[VMEM] * X,
        out_specs=VMEM,
        compiler_params=params(16),
        name="combine",
    )(*back)
    got = lax.all_to_all(send, ("zh", "zl"), split_axis=0, concat_axis=0, tiled=True)
    grid_spec = pltpu.PrefetchScalarGridSpec(
        num_scalar_prefetch=2,
        grid=(1,),
        in_specs=[
            pl.BlockSpec((Z, 4, ROWS, HD), lambda i, step, half: (0, 0, 0, 0)),
            pl.BlockSpec((1, ROWS, 64), lambda i, step, half: (0, 0, 0)),
            pl.BlockSpec((1, 2, 20 * HD), lambda i, step, half: (step[0], 0, 0)),
            pl.BlockSpec((1, 2, 8 * HD), lambda i, step, half: (step[0], 0, 0)),
            pl.BlockSpec((20 * HD, 64), lambda i, step, half: (0, 0)),
            pl.BlockSpec((8 * HD, 64), lambda i, step, half: (0, 0)),
        ],
        out_specs=[pl.BlockSpec((1, ROWS, 64), lambda i, step, half: (0, 0, 0))] * 2,
    )
    velocity, advanced = pl.pallas_call(
        final_kernel,
        out_shape=(jax.ShapeDtypeStruct((1, ROWS, 64), f32),) * 2,
        grid_spec=grid_spec,
        compiler_params=params(16),
        name="final",
    )(step_index, half, got, latents, main_mod, guide_mod, main_head, guide_head)
    return velocity, advanced


def solution(mesh):
    fine = Mesh(mesh.devices.reshape(ZL, X, Y, ZH, CORE), ("zl", "x", "y", "zh", "core"))
    seq = ("x", "y", "zh", "core")
    return jax.shard_map(
        on_device,
        mesh=fine,
        in_specs=(P(seq, "zl", None),) * 3
        + (P(seq, None, "zl"),) * 3
        + (P(seq, "zl", None),)
        + (P(),) * 5,
        out_specs=(P(seq, "zl", None),) * 2,
        check_vma=False,
    )
```

time: 562 us -> 126 us (0.22)
  waiting for transfers between devices: 267 us -> 70 us
  local copies, waits for them, and re-layouts: 136 us -> 6.32 us
  matrix products: 55.4 us -> 0 us
  other arithmetic: 52.9 us -> 0 us
  starting transfers between devices: 15.4 us -> 33.8 us
  Pallas kernels: 0 us -> 14 us
  between operations: 15 us -> 1.39 us
  blocking collectives: 12.6 us -> 0 us
    all_gather x4 -> x0, waiting for transfers between devices: 255 us -> none  [the longest x1 85.4 us: on_device(): lax.all_gather(guide_value, 'seq', axis=1, tiled=True)]
    ppermute x0 -> x14, waiting for transfers between devices: none -> 61.3 us  [shifted(): lax.ppermute(array, axis, [(i, (i + by) % size) for i in range(size)])]
    reshape x4 -> x0, local copies, waits for them, and re-layouts: 61 us -> none  [the longest x2 30.5 us: fold_keys(): key_blocks = keys.reshape(length // block, block, heads, depth)]
    dot_general x66 -> x0, matrix products: 55.4 us -> none  [the longest x32 27.2 us: one_block(): jnp.einsum('hrb,bhd->rhd', weights.astype(jnp.bfloat16), value_block, pre...]
    unnamed x11 -> x0, other arithmetic: 45.4 us -> none
    unnamed x33 -> x24, local copies, waits for them, and re-layouts: 45.6 us -> 6.32 us
    dynamic_slice x32 -> x0, local copies, waits for them, and re-layouts: 25 us -> none  [fold_keys(): carried, unused = lax.scan(one_block, carried, (key_blocks, value_blocks))]
    ppermute x0 -> x14, starting transfers between devices: none -> 21.8 us  [shifted(): lax.ppermute(array, axis, [(i, (i + by) % size) for i in range(size)])]
  transfers between devices with their start and end apart: 8 -> 16, of which waited for: 6 -> 9; matrix products, arithmetic and copies ran while one was open for 26% -> 0% of each run, Pallas kernels for 0% -> 0%
where the time goes in v1:
time: 126 us; the launch traced here: 125 us
  waiting for transfers between devices  70 us (56%)
  starting transfers between devices  33.8 us (27%)
  Pallas kernels  14 us (11%)
  local copies, waits for them, and re-layouts  6.32 us (5%)
  between operations  1.39 us (1%)
    ppermute x14, waiting for transfers between devices, shifted(): lax.ppermute(array, axis, [(i, (i + by) % size) for i in range(size)])  61.3 us
    ppermute x14, starting transfers between devices, shifted(): lax.ppermute(array, axis, [(i, (i + by) % size) for i in range(size)])  21.8 us
    all_to_all x2, starting transfers between devices, on_device(): lax.all_to_all(send, ('zh', 'zl'), split_axis=0, concat_axis=0, tiled=True)  12 us
    pallas_call x1, Pallas kernels, on_device(): pl.pallas_call(attend_kernel, out_shape=(jax.ShapeDtypeStruct((OROWS, HD)...  10.2 us
    all_to_all x2, waiting for transfers between devices, on_device(): lax.all_to_all(send, ('zh', 'zl'), split_axis=0, concat_axis=0, tiled=True)  8.64 us
    unnamed x24, local copies, waits for them, and re-layouts  6.32 us
  transfers between devices with their start and end apart: 16, of which 9 were waited for; matrix products, arithmetic and copies ran while one was open for 0% of the time, Pallas kernels for 0%

profile of v1, /device:TPU:24, one launch (start us, length us, event | category | flops | bytes accessed | tf_op | source)
XLA Modules:
  0.0 125.5 jit_solution(3725577880498790518)
XLA Ops:
  0.6 0.9 copy-done.2
  1.6 0.9 copy-done.3
  2.5 0.9 copy-done.4
  3.4 0.8 copy-done.5
  4.2 0.8 copy-done.6
  5.1 0.8 copy-done.7
  5.9 0.9 pack.1
  6.8 8.5 %all-to-all-start = ((bf16[8,9,32,128]{3,2,1,0:T(8,128)(2,1)}), bf16[8,9,32,128]{3,2,1,0:T(8,128)(2,1)S(1)}, u32[]{:S(2)}, u32[]{:S(2)}) async-start(bf16[8,9,32,128]{3,2,1,0:T(8,128)(2,1)} %get-tuple-element.11), calls=%async_computation | async-start | bytes 1179648 | tf_op jit(solution)/shard_map/all_to_all | solution.py:265
  15.3 5.9 %collective-permute-start = (bf16[3,128,128]{2,1,0:T(8,128)(2,1)S(1)}, bf16[3,128,128]{2,1,0:T(8,128)(2,1)S(1)}, u32[]{:S(2)}, u32[]{:S(2)}) collective-permute-start(bf16[3,128,128]{2,1,0:T(8,128)(2,1)S(1)} %get-tuple-element.13), channel_id=1, source_target_pairs={{0,2},{2,0},{1,3},{3,1},{4,6},{6,4},{5,7},{7,5},{8,10},{10,8},{9,1... | collective-permute-start | bytes 294920 | tf_op jit(solution)/shard_map/ppermute | solution.py:234
  21.2 17.2 %collective-permute-done.guide_got = bf16[3,128,128]{2,1,0:T(8,128)(2,1)S(1)} collective-permute-done((bf16[3,128,128]{2,1,0:T(8,128)(2,1)S(1)}, bf16[3,128,128]{2,1,0:T(8,128)(2,1)S(1)}, u32[]{:S(2)}, u32[]{:S(2)}) %collective-permute-start) | collective-permute-done | bytes 98336 | tf_op jit(solution)/shard_map/ppermute | solution.py:234
  38.5 1.3 %collective-permute-start.6 = (bf16[8,256,128]{2,1,0:T(8,128)(2,1)S(1)}, bf16[8,256,128]{2,1,0:T(8,128)(2,1)S(1)}, u32[]{:S(2)}, u32[]{:S(2)}) collective-permute-start(bf16[8,256,128]{2,1,0:T(8,128)(2,1)S(1)} %get-tuple-element.15.refs_4_), channel_id=1, source_target_pairs={{0,8},{4,12},{8,0},{12,4},{1,9},{5,13},{9,1},{13,5},{2,10},{6,14},... | collective-permute-start | bytes 1572872 | tf_op jit(solution)/shard_map/ppermute | solution.py:234
  39.8 2.2 %collective-permute-start.4 = (bf16[8,256,128]{2,1,0:T(8,128)(2,1)S(1)}, bf16[8,256,128]{2,1,0:T(8,128)(2,1)S(1)}, u32[]{:S(2)}, u32[]{:S(2)}) collective-permute-start(bf16[8,256,128]{2,1,0:T(8,128)(2,1)S(1)} %get-tuple-element.15.refs_4_), channel_id=1, source_target_pairs={{0,4},{4,8},{8,12},{12,0},{1,5},{5,9},{9,13},{13,1},{2,6},{6,10},{... | collective-permute-start | bytes 1572872 | tf_op jit(solution)/shard_map/ppermute | solution.py:234
  42.0 1.5 %collective-permute-start.1 = (bf16[896,128]{1,0:T(8,128)(2,1)S(1)}, bf16[896,128]{1,0:T(8,128)(2,1)S(1)}, u32[]{:S(2)}, u32[]{:S(2)}) collective-permute-start(bf16[896,128]{1,0:T(8,128)(2,1)S(1)} %get-tuple-element.14.refs_0_), channel_id=1, source_target_pairs={{0,16},{16,32},{32,48},{48,0},{1,17},{17,33},{33,49},{49,1},{2,18}... | collective-permute-start | bytes 688136 | tf_op jit(solution)/shard_map/ppermute | solution.py:234
  43.5 11.4 %collective-permute-done.6.refs_7_ = bf16[8,256,128]{2,1,0:T(8,128)(2,1)S(1)} collective-permute-done((bf16[8,256,128]{2,1,0:T(8,128)(2,1)S(1)}, bf16[8,256,128]{2,1,0:T(8,128)(2,1)S(1)}, u32[]{:S(2)}, u32[]{:S(2)}) %collective-permute-start.6) | collective-permute-done | bytes 524320 | tf_op jit(solution)/shard_map/ppermute | solution.py:234
  54.9 7.8 %collective-permute-done.4.refs_5_ = bf16[8,256,128]{2,1,0:T(8,128)(2,1)S(1)} collective-permute-done((bf16[8,256,128]{2,1,0:T(8,128)(2,1)S(1)}, bf16[8,256,128]{2,1,0:T(8,128)(2,1)S(1)}, u32[]{:S(2)}, u32[]{:S(2)}) %collective-permute-start.4) | collective-permute-done | bytes 524320 | tf_op jit(solution)/shard_map/ppermute | solution.py:234
  62.7 2.4 %collective-permute-done.5.refs_6_ = bf16[8,256,128]{2,1,0:T(8,128)(2,1)S(1)} collective-permute-done((bf16[8,256,128]{2,1,0:T(8,128)(2,1)S(1)}, bf16[8,256,128]{2,1,0:T(8,128)(2,1)S(1)}, u32[]{:S(2)}, u32[]{:S(2)}) %collective-permute-start.5) | collective-permute-done | bytes 524320 | tf_op jit(solution)/shard_map/ppermute | solution.py:234
  65.2 2.8 %collective-permute-start.2 = (bf16[896,128]{1,0:T(8,128)(2,1)S(1)}, bf16[896,128]{1,0:T(8,128)(2,1)S(1)}, u32[]{:S(2)}, u32[]{:S(2)}) collective-permute-start(bf16[896,128]{1,0:T(8,128)(2,1)S(1)} %get-tuple-element.14.refs_0_), channel_id=1, source_target_pairs={{0,48},{16,0},{32,16},{48,32},{1,49},{17,1},{33,17},{49,33},{2,50}... | collective-permute-start | bytes 688136 | tf_op jit(solution)/shard_map/ppermute | solution.py:234
  67.9 5.5 %collective-permute-done.2.refs_2_ = bf16[896,128]{1,0:T(8,128)(2,1)S(1)} collective-permute-done((bf16[896,128]{1,0:T(8,128)(2,1)S(1)}, bf16[896,128]{1,0:T(8,128)(2,1)S(1)}, u32[]{:S(2)}, u32[]{:S(2)}) %collective-permute-start.2) | collective-permute-done | bytes 229408 | tf_op jit(solution)/shard_map/ppermute | solution.py:234
  73.5 2.7 %collective-permute-start.3 = (bf16[896,128]{1,0:T(8,128)(2,1)S(1)}, bf16[896,128]{1,0:T(8,128)(2,1)S(1)}, u32[]{:S(2)}, u32[]{:S(2)}) collective-permute-start(bf16[896,128]{1,0:T(8,128)(2,1)S(1)} %get-tuple-element.14.refs_0_), channel_id=1, source_target_pairs={{0,32},{16,48},{32,0},{48,16},{1,33},{17,49},{33,1},{49,17},{2,34}... | collective-permute-start | bytes 688136 | tf_op jit(solution)/shard_map/ppermute | solution.py:234
  76.2 6.0 %collective-permute-done.3.refs_3_ = bf16[896,128]{1,0:T(8,128)(2,1)S(1)} collective-permute-done((bf16[896,128]{1,0:T(8,128)(2,1)S(1)}, bf16[896,128]{1,0:T(8,128)(2,1)S(1)}, u32[]{:S(2)}, u32[]{:S(2)}) %collective-permute-start.3) | collective-permute-done | bytes 229408 | tf_op jit(solution)/shard_map/ppermute | solution.py:234
  82.2 10.2 %attend.1 = (bf16[928,128]{1,0:T(8,128)(2,1)S(1)}, bf16[928,128]{1,0:T(8,128)(2,1)S(1)}, bf16[928,128]{1,0:T(8,128)(2,1)S(1)}, bf16[928,128]{1,0:T(8,128)(2,1)S(1)}) custom-call(bf16[896,128]{1,0:T(8,128)(2,1)S(1)} %get-tuple-element.14.refs_0_, bf16[896,128]{1,0:T(8,128)(2,1)S(1)} %collective-permute-done.1.refs_1_, ...), custom_call_target="tpu_custom_call" | custom-call | tf_op jit(solution)/shard_map/attend/pallas_call | solution.py:281
  92.4 3.8 %collective-permute-start.11 = (bf16[928,128]{1,0:T(8,128)(2,1)S(1)}, bf16[928,128]{1,0:T(8,128)(2,1)S(1)}, u32[]{:S(2)}, u32[]{:S(2)}) collective-permute-start(bf16[928,128]{1,0:T(8,128)(2,1)S(1)} %get-tuple-element.17), channel_id=1, source_target_pairs={{0,48},{16,0},{32,16},{48,32},{1,49},{17,1},{33,17},{49,33},{2,50}... | collective-permute-start | bytes 712712 | tf_op jit(solution)/shard_map/ppermute | solution.py:234
  96.1 1.6 %collective-permute-start.13 = (bf16[928,128]{1,0:T(8,128)(2,1)S(1)}, bf16[928,128]{1,0:T(8,128)(2,1)S(1)}, u32[]{:S(2)}, u32[]{:S(2)}) collective-permute-start(bf16[928,128]{1,0:T(8,128)(2,1)S(1)} %get-tuple-element.19), channel_id=1, source_target_pairs={{0,32},{16,48},{32,0},{48,16},{1,33},{17,49},{33,1},{49,17},{2,34}... | collective-permute-start | bytes 712712 | tf_op jit(solution)/shard_map/ppermute | solution.py:234
  97.7 7.6 %collective-permute-done.11.refs_1_ = bf16[928,128]{1,0:T(8,128)(2,1)S(1)} collective-permute-done((bf16[928,128]{1,0:T(8,128)(2,1)S(1)}, bf16[928,128]{1,0:T(8,128)(2,1)S(1)}, u32[]{:S(2)}, u32[]{:S(2)}) %collective-permute-start.11) | collective-permute-done | bytes 237600 | tf_op jit(solution)/shard_map/ppermute | solution.py:234
  105.3 3.4 %collective-permute-done.12.refs_2_ = bf16[928,128]{1,0:T(8,128)(2,1)S(1)} collective-permute-done((bf16[928,128]{1,0:T(8,128)(2,1)S(1)}, bf16[928,128]{1,0:T(8,128)(2,1)S(1)}, u32[]{:S(2)}, u32[]{:S(2)}) %collective-permute-start.12) | collective-permute-done | bytes 237600 | tf_op jit(solution)/shard_map/ppermute | solution.py:234
  108.7 1.3 %combine.1 = bf16[8,4,32,128]{3,2,1,0:T(8,128)(2,1)} custom-call(bf16[928,128]{1,0:T(8,128)(2,1)S(1)} %get-tuple-element.16.refs_0_, bf16[928,128]{1,0:T(8,128)(2,1)S(1)} %collective-permute-done.11.refs_1_, bf16[928,128]{1,0:T(8,128)(2,1)S(1)} %collective-permute-done.12.refs_2_, bf16[928,128]{1,0:T(8,128)(2,1)S(1)} %collective-permute-done.13.refs_3_), custom_call_target="tpu_custom_call" | custom-call | tf_op jit(solution)/shard_map/combine/pallas_call | solution.py:297
  110.0 3.5 %all-to-all-start.1 = ((bf16[8,4,32,128]{3,2,1,0:T(8,128)(2,1)}), bf16[8,4,32,128]{3,2,1,0:T(8,128)(2,1)S(1)}, u32[]{:S(2)}, u32[]{:S(2)}) async-start(bf16[8,4,32,128]{3,2,1,0:T(8,128)(2,1)} %combine.1), calls=%async_computation.1 | async-start | bytes 524288 | tf_op jit(solution)/shard_map/all_to_all | solution.py:305
  113.6 0.3 copy.14.main_head
  113.9 0.6 copy-done.10
  114.5 0.2 copy.15.guide_head
  115.3 8.6 %all-to-all-done.1.got = bf16[8,4,32,128]{3,2,1,0:T(8,128)(2,1)S(1)} async-done(((bf16[8,4,32,128]{3,2,1,0:T(8,128)(2,1)}), bf16[8,4,32,128]{3,2,1,0:T(8,128)(2,1)S(1)}, u32[]{:S(2)}, u32[]{:S(2)}) %all-to-all-start.1) | async-done | bytes 262176 | tf_op jit(solution)/shard_map/all_to_all | solution.py:305
  123.9 1.5 %final.1 = (f32[1,32,64]{2,1,0:T(8,128)}, f32[1,32,64]{2,1,0:T(8,128)}) custom-call(s32[1]{0:T(128)S(6)} %copy.16.step, s32[1]{0:T(128)} %bitcast.half, bf16[8,4,32,128]{3,2,1,0:T(8,128)(2,1)S(1)} %all-to-all-done.1.got, f32[1,32,64]{2,1,0:T(8,128)S(1)} %copy-done.8, bf16[50,2,2560]{2,1,0:T(2,128)(2,1)S(1)} %copy-done, bf16[50,2,1024]{2,1,0:T(2,128)(2,1)S(1)} %copy-done.1, ...), custom_call_target="tpu_custom_call" | custom-call | tf_op jit(solution)/shard_map/final/pallas_call | solution.py:319
  (29 shorter events, 0.1 us)
Async XLA Ops:
  0.6 0.9 copy-start.2
  1.6 0.9 copy-start.3
  2.5 0.9 copy-start.4
  3.4 0.8 copy-start.5
  4.2 0.8 copy-start.6
  5.1 0.8 copy-start.7
  6.8 31.6 %all-to-all-start = ((bf16[8,9,32,128]{3,2,1,0:T(8,128)(2,1)}), bf16[8,9,32,128]{3,2,1,0:T(8,128)(2,1)S(1)}, u32[]{:S(2)}, u32[]{:S(2)}) async-start(bf16[8,9,32,128]{3,2,1,0:T(8,128)(2,1)} %get-tuple-element.11), calls=%async_computation | async-start | bytes 1179648 | tf_op jit(solution)/shard_map/all_to_all | solution.py:265
  15.3 23.1 %collective-permute-start = (bf16[3,128,128]{2,1,0:T(8,128)(2,1)S(1)}, bf16[3,128,128]{2,1,0:T(8,128)(2,1)S(1)}, u32[]{:S(2)}, u32[]{:S(2)}) collective-permute-start(bf16[3,128,128]{2,1,0:T(8,128)(2,1)S(1)} %get-tuple-element.13), channel_id=1, source_target_pairs={{0,2},{2,0},{1,3},{3,1},{4,6},{6,4},{5,7},{7,5},{8,10},{10,8},{9,1... | collective-permute-start | bytes 294920 | tf_op jit(solution)/shard_map/ppermute | solution.py:234
  38.5 16.4 %collective-permute-start.6 = (bf16[8,256,128]{2,1,0:T(8,128)(2,1)S(1)}, bf16[8,256,128]{2,1,0:T(8,128)(2,1)S(1)}, u32[]{:S(2)}, u32[]{:S(2)}) collective-permute-start(bf16[8,256,128]{2,1,0:T(8,128)(2,1)S(1)} %get-tuple-element.15.refs_4_), channel_id=1, source_target_pairs={{0,8},{4,12},{8,0},{12,4},{1,9},{5,13},{9,1},{13,5},{2,10},{6,14},... | collective-permute-start | bytes 1572872 | tf_op jit(solution)/shard_map/ppermute | solution.py:234
  39.8 22.9 %collective-permute-start.4 = (bf16[8,256,128]{2,1,0:T(8,128)(2,1)S(1)}, bf16[8,256,128]{2,1,0:T(8,128)(2,1)S(1)}, u32[]{:S(2)}, u32[]{:S(2)}) collective-permute-start(bf16[8,256,128]{2,1,0:T(8,128)(2,1)S(1)} %get-tuple-element.15.refs_4_), channel_id=1, source_target_pairs={{0,4},{4,8},{8,12},{12,0},{1,5},{5,9},{9,13},{13,1},{2,6},{6,10},{... | collective-permute-start | bytes 1572872 | tf_op jit(solution)/shard_map/ppermute | solution.py:234
  42.0 23.2 %collective-permute-start.5 = (bf16[8,256,128]{2,1,0:T(8,128)(2,1)S(1)}, bf16[8,256,128]{2,1,0:T(8,128)(2,1)S(1)}, u32[]{:S(2)}, u32[]{:S(2)}) collective-permute-start(bf16[8,256,128]{2,1,0:T(8,128)(2,1)S(1)} %get-tuple-element.15.refs_4_), channel_id=1, source_target_pairs={{0,12},{4,0},{8,4},{12,8},{1,13},{5,1},{9,5},{13,9},{2,14},{6,2},{... | collective-permute-start | bytes 1572872 | tf_op jit(solution)/shard_map/ppermute | solution.py:234
  42.0 23.2 %collective-permute-start.1 = (bf16[896,128]{1,0:T(8,128)(2,1)S(1)}, bf16[896,128]{1,0:T(8,128)(2,1)S(1)}, u32[]{:S(2)}, u32[]{:S(2)}) collective-permute-start(bf16[896,128]{1,0:T(8,128)(2,1)S(1)} %get-tuple-element.14.refs_0_), channel_id=1, source_target_pairs={{0,16},{16,32},{32,48},{48,0},{1,17},{17,33},{33,49},{49,1},{2,18}... | collective-permute-start | bytes 688136 | tf_op jit(solution)/shard_map/ppermute | solution.py:234
  43.5 38.7 %collective-permute-start.7 = (bf16[8,256,128]{2,1,0:T(8,128)(2,1)S(1)}, bf16[8,256,128]{2,1,0:T(8,128)(2,1)S(1)}, u32[]{:S(2)}, u32[]{:S(2)}) collective-permute-start(bf16[8,256,128]{2,1,0:T(8,128)(2,1)S(1)} %get-tuple-element.15.refs_4_), channel_id=1, source_target_pairs={{0,1},{1,0},{2,3},{3,2},{4,5},{5,4},{6,7},{7,6},{8,9},{9,8},{10,11... | collective-permute-start | bytes 1572872 | tf_op jit(solution)/shard_map/ppermute | solution.py:234
  54.9 27.3 %collective-permute-start.10 = (bf16[8,256,128]{2,1,0:T(8,128)(2,1)S(1)}, bf16[8,256,128]{2,1,0:T(8,128)(2,1)S(1)}, u32[]{:S(2)}, u32[]{:S(2)}) collective-permute-start(bf16[8,256,128]{2,1,0:T(8,128)(2,1)S(1)} %collective-permute-done.6.refs_7_), channel_id=1, source_target_pairs={{0,1},{1,0},{2,3},{3,2},{4,5},{5,4},{6,7},{7,6},{8,9},{9,8},{10,11... | collective-permute-start | bytes 1572872 | tf_op jit(solution)/shard_map/ppermute | solution.py:234
  62.7 19.4 %collective-permute-start.8 = (bf16[8,256,128]{2,1,0:T(8,128)(2,1)S(1)}, bf16[8,256,128]{2,1,0:T(8,128)(2,1)S(1)}, u32[]{:S(2)}, u32[]{:S(2)}) collective-permute-start(bf16[8,256,128]{2,1,0:T(8,128)(2,1)S(1)} %collective-permute-done.4.refs_5_), channel_id=1, source_target_pairs={{0,1},{1,0},{2,3},{3,2},{4,5},{5,4},{6,7},{7,6},{8,9},{9,8},{10,11... | collective-permute-start | bytes 1572872 | tf_op jit(solution)/shard_map/ppermute | solution.py:234
  65.2 17.0 %collective-permute-start.9 = (bf16[8,256,128]{2,1,0:T(8,128)(2,1)S(1)}, bf16[8,256,128]{2,1,0:T(8,128)(2,1)S(1)}, u32[]{:S(2)}, u32[]{:S(2)}) collective-permute-start(bf16[8,256,128]{2,1,0:T(8,128)(2,1)S(1)} %collective-permute-done.5.refs_6_), channel_id=1, source_target_pairs={{0,1},{1,0},{2,3},{3,2},{4,5},{5,4},{6,7},{7,6},{8,9},{9,8},{10,11... | collective-permute-start | bytes 1572872 | tf_op jit(solution)/shard_map/ppermute | solution.py:234
  65.2 8.3 %collective-permute-start.2 = (bf16[896,128]{1,0:T(8,128)(2,1)S(1)}, bf16[896,128]{1,0:T(8,128)(2,1)S(1)}, u32[]{:S(2)}, u32[]{:S(2)}) collective-permute-start(bf16[896,128]{1,0:T(8,128)(2,1)S(1)} %get-tuple-element.14.refs_0_), channel_id=1, source_target_pairs={{0,48},{16,0},{32,16},{48,32},{1,49},{17,1},{33,17},{49,33},{2,50}... | collective-permute-start | bytes 688136 | tf_op jit(solution)/shard_map/ppermute | solution.py:234
  73.5 8.7 %collective-permute-start.3 = (bf16[896,128]{1,0:T(8,128)(2,1)S(1)}, bf16[896,128]{1,0:T(8,128)(2,1)S(1)}, u32[]{:S(2)}, u32[]{:S(2)}) collective-permute-start(bf16[896,128]{1,0:T(8,128)(2,1)S(1)} %get-tuple-element.14.refs_0_), channel_id=1, source_target_pairs={{0,32},{16,48},{32,0},{48,16},{1,33},{17,49},{33,1},{49,17},{2,34}... | collective-permute-start | bytes 688136 | tf_op jit(solution)/shard_map/ppermute | solution.py:234
  92.4 12.9 %collective-permute-start.11 = (bf16[928,128]{1,0:T(8,128)(2,1)S(1)}, bf16[928,128]{1,0:T(8,128)(2,1)S(1)}, u32[]{:S(2)}, u32[]{:S(2)}) collective-permute-start(bf16[928,128]{1,0:T(8,128)(2,1)S(1)} %get-tuple-element.17), channel_id=1, source_target_pairs={{0,48},{16,0},{32,16},{48,32},{1,49},{17,1},{33,17},{49,33},{2,50}... | collective-permute-start | bytes 712712 | tf_op jit(solution)/shard_map/ppermute | solution.py:234
  96.1 12.5 %collective-permute-start.12 = (bf16[928,128]{1,0:T(8,128)(2,1)S(1)}, bf16[928,128]{1,0:T(8,128)(2,1)S(1)}, u32[]{:S(2)}, u32[]{:S(2)}) collective-permute-start(bf16[928,128]{1,0:T(8,128)(2,1)S(1)} %get-tuple-element.18), channel_id=1, source_target_pairs={{0,16},{16,32},{32,48},{48,0},{1,17},{17,33},{33,49},{49,1},{2,18}... | collective-permute-start | bytes 712712 | tf_op jit(solution)/shard_map/ppermute | solution.py:234
  96.1 12.5 %collective-permute-start.13 = (bf16[928,128]{1,0:T(8,128)(2,1)S(1)}, bf16[928,128]{1,0:T(8,128)(2,1)S(1)}, u32[]{:S(2)}, u32[]{:S(2)}) collective-permute-start(bf16[928,128]{1,0:T(8,128)(2,1)S(1)} %get-tuple-element.19), channel_id=1, source_target_pairs={{0,32},{16,48},{32,0},{48,16},{1,33},{17,49},{33,1},{49,17},{2,34}... | collective-permute-start | bytes 712712 | tf_op jit(solution)/shard_map/ppermute | solution.py:234
  110.0 3.6 %copy-start.9 = (bf16[2560,64]{0,1:T(8,128)(2,1)S(1)}, bf16[2560,64]{0,1:T(8,128)(2,1)}, u32[]{:S(2)}) copy-start(bf16[2560,64]{0,1:T(8,128)(2,1)} %param.22) | copy-start | bytes 983044
  110.0 13.9 %all-to-all-start.1 = ((bf16[8,4,32,128]{3,2,1,0:T(8,128)(2,1)}), bf16[8,4,32,128]{3,2,1,0:T(8,128)(2,1)S(1)}, u32[]{:S(2)}, u32[]{:S(2)}) async-start(bf16[8,4,32,128]{3,2,1,0:T(8,128)(2,1)} %combine.1), calls=%async_computation.1 | async-start | bytes 524288 | tf_op jit(solution)/shard_map/all_to_all | solution.py:305
  113.6 0.9 copy-start.10
  113.6 10.4 %copy-start = (bf16[50,2,2560]{2,1,0:T(2,128)(2,1)S(1)}, bf16[50,2,2560]{2,1,0:T(2,128)(2,1)}, u32[]{:S(2)}) copy-start(bf16[50,2,2560]{2,1,0:T(2,128)(2,1)} %main_mod.1) | copy-start | bytes 1536004
  114.5 9.5 %copy-start.1 = (bf16[50,2,1024]{2,1,0:T(2,128)(2,1)S(1)}, bf16[50,2,1024]{2,1,0:T(2,128)(2,1)}, u32[]{:S(2)}) copy-start(bf16[50,2,1024]{2,1,0:T(2,128)(2,1)} %guide_mod.1) | copy-start | bytes 614404
  114.5 9.5 %copy-start.8 = (f32[1,32,64]{2,1,0:T(8,128)S(1)}, f32[1,32,64]{2,1,0:T(8,128)}, u32[]{:S(2)}) copy-start(f32[1,32,64]{2,1,0:T(8,128)} %latents.1) | copy-start | bytes 24580

commit v2 on v1

v2 whole, which is shorter than its diff:
```python
import math

import jax
import jax.numpy as jnp
from jax import lax
from jax.experimental import pallas as pl
from jax.experimental.pallas import tpu as pltpu
from jax.sharding import Mesh, PartitionSpec as P

HD = 128
STEPS = 50
ZL, X, Y, ZH, CORE = 4, 4, 4, 2, 2
Z = ZL * ZH
SIDE = 4
ROWS = 32
BLOCK = 128
COLUMN = ROWS * Z
TOKENS = COLUMN * CORE
TILE = 256
HEADS = 2
STAT = 32
KEYS = SIDE * TOKENS

guidance = 2.5
flow_shift = 3.0
epsilon = 1e-06
score_scale = math.log2(math.e) / math.sqrt(HD)

f32 = jnp.float32
bf16 = jnp.bfloat16
VMEM = pl.BlockSpec(memory_space=pltpu.VMEM)
SMEM = pl.BlockSpec(memory_space=pltpu.SMEM)
ANY = pl.BlockSpec(memory_space=pl.ANY)


def shape(*dims, dtype=bf16):
    return jax.ShapeDtypeStruct(dims, dtype)


def params(mib):
    return pltpu.CompilerParams(vmem_limit_bytes=mib * 1024 * 1024)


def pack_kernel(place, mq, mk, mv, gq, gk, gv, send, guide_send, guide_own, main, guide, sems):
    zh = place[0]
    copies = []
    for kind, ref in enumerate((mq, mk, mv)):
        copies.append(pltpu.make_async_copy(ref.at[0], main.at[kind], sems.at[kind]))
    for kind, ref in enumerate((gq, gk, gv)):
        copies.append(pltpu.make_async_copy(ref.at[0], guide.at[kind], sems.at[3 + kind]))
    for copy in copies:
        copy.start()
    for kind in range(3):
        copies[kind].wait()
        for zh_to in range(ZH):
            for zl_to in range(ZL):
                for slot in range(3):
                    head = zl_to * 5 + (4 if slot == 2 else 2 * zh_to + slot)
                    lanes = slice(head * HD, (head + 1) * HD)
                    send[zh_to * ZL + zl_to, slot * 3 + kind] = main[kind, :, lanes]
    own = pl.ds(pl.multiple_of(zh * HD, HD), HD)
    other = pl.ds(pl.multiple_of((1 - zh) * HD, HD), HD)
    for kind in range(3):
        copies[3 + kind].wait()
        guide_own[kind] = guide[kind, :, own]
        guide_send[kind] = guide[kind, :, other]


def unpack_kernel(
    place, got, sibling, guide_own, guide_core, guide_half, guide_across, queries, pairs
):
    zh, core = place[0], place[1]
    for ref, whose in ((got, core), (sibling, 1 - core)):
        base = whose * COLUMN
        for source in range(Z):
            rows = pl.ds(pl.multiple_of(base + source * ROWS, ROWS), ROWS)
            queries[rows, :] = ref[source, core * 3]
            for kind in range(2):
                pairs[kind, rows, :] = ref[source, core * 3 + 1 + kind]

    @pl.when(core == 0)
    def _():
        for ref, zh_from, core_from in (
            (guide_own, zh, 0),
            (guide_core, zh, 1),
            (guide_half, 1 - zh, 0),
            (guide_across, 1 - zh, 1),
        ):
            at = pl.multiple_of(core_from * COLUMN + zh_from * BLOCK, BLOCK)
            queries[pl.ds(pl.multiple_of(TOKENS + at, BLOCK), BLOCK), :] = ref[0]
            pairs[2, pl.ds(at, BLOCK), :] = ref[1]
            pairs[3, pl.ds(at, BLOCK), :] = ref[2]

    @pl.when(core == 1)
    def _():
        for ref, whose in ((got, 1), (sibling, 0)):
            for source in range(Z):
                rows = pl.ds(whose * COLUMN + source * ROWS, ROWS)
                for kind in range(2):
                    pairs[2 + kind, rows, :] = ref[source, 7 + kind]
            for zl in range(ZL):
                rows = pl.ds(TOKENS + whose * BLOCK + zl * ROWS, ROWS)
                queries[rows, :] = ref[zh * ZL + zl, 6]
        queries[pl.ds(TOKENS + COLUMN, COLUMN), :] = jnp.zeros((COLUMN, HD), bf16)


def diagonal():
    return lax.broadcasted_iota(jnp.int32, (HD, HD), 0) == lax.broadcasted_iota(
        jnp.int32, (HD, HD), 1
    )


def attend_kernel(queries, *refs):
    pairs, out = refs[:SIDE], refs[SIDE]
    values, scores, weights, stats = refs[SIDE + 1 :]
    for head in range(HEADS):
        for piece in range(SIDE):
            rows = pl.ds(piece * TOKENS, TOKENS)
            values[head, rows, :HD] = pairs[piece][head * 2 + 1]
            values[head, rows, HD:] = jnp.ones((TOKENS, HD), bf16)
    on_diagonal = diagonal()
    parts = [(piece, half) for piece in range(SIDE) for half in range(TOKENS // TILE)]
    tiles = HEADS * TOKENS // TILE

    def score_tile(tile):
        head = tile * TILE // TOKENS
        query = queries[tile * TILE : (tile + 1) * TILE, :]
        highest = None
        for index, (piece, half) in enumerate(parts):
            part = lax.dot_general(
                query,
                pairs[piece][head * 2, half * TILE : (half + 1) * TILE, :],
                (((1,), (1,)), ((), ())),
                preferred_element_type=f32,
            )
            scores[tile, :, index * TILE : (index + 1) * TILE] = part
            here = jnp.maximum(part[:, :HD], part[:, HD:])
            highest = here if highest is None else jnp.maximum(highest, here)
        return jnp.max(highest, axis=1, keepdims=True) * score_scale

    def weight_tile(tile, highest):
        for index in range(len(parts)):
            columns = slice(index * TILE, (index + 1) * TILE)
            part = scores[tile, :, columns]
            weights[tile, :, columns] = jnp.exp2(part * score_scale - highest).astype(bf16)
        total = jnp.dot(
            weights[tile], values[tile * TILE // TOKENS], preferred_element_type=f32
        )
        weight_sum = total[:, HD:]
        out[tile * TILE : (tile + 1) * TILE, :] = (total[:, :HD] / weight_sum).astype(bf16)
        level = highest + jnp.log2(weight_sum)
        for part in range(TILE // HD):
            block = level[part * HD : (part + 1) * HD, :]
            row = jnp.sum(jnp.where(on_diagonal, block, 0.0), axis=0, keepdims=True)
            stats[tile * (TILE // HD) + part : tile * (TILE // HD) + part + 1, :] = row

    tops = [score_tile(0)]
    for tile in range(tiles):
        if tile + 1 < tiles:
            tops.append(score_tile(tile + 1))
        weight_tile(tile, tops[tile])
    level = stats[...]
    high = level.astype(bf16).astype(f32)
    middle = (level - high).astype(bf16).astype(f32)
    low = level - high - middle
    block = jnp.concatenate([high, middle, low, jnp.zeros_like(low)], axis=0)
    out[HEADS * TOKENS :, :] = block.astype(bf16)


def combine_kernel(place, *refs):
    parts, send = refs[:SIDE], refs[SIDE]
    on_diagonal = diagonal()
    levels = []
    for part in parts:
        block = part[HEADS * TOKENS :, :].astype(f32)
        levels.append(block[0:8] + block[8:16] + block[16:24])
    top = levels[0]
    for level in levels[1:]:
        top = jnp.maximum(top, level)
    shares = [jnp.exp2(level - top) for level in levels]
    whole = shares[0] + shares[1] + shares[2] + shares[3]
    shares = [share / whole for share in shares]
    results = []
    for tile in range(HEADS * TOKENS // HD):
        total = None
        for part, share in zip(parts, shares):
            row = jnp.broadcast_to(share[tile : tile + 1, :], (HD, HD))
            column = jnp.sum(jnp.where(on_diagonal, row, 0.0), axis=1, keepdims=True)
            term = part[tile * HD : (tile + 1) * HD, :].astype(f32) * column
            total = term if total is None else total + term
        results.append(total.astype(bf16))

    def put(head, tiles):
        for tile, result in enumerate(tiles):
            for zl in range(ZL):
                send[tile * ZL + zl, head] = result[zl * ROWS : (zl + 1) * ROWS, :]

    blocks = TOKENS // HD
    put(0, results[:blocks])

    @pl.when(place[1] == 0)
    def _():
        put(1, results[blocks:])

    @pl.when(place[1] == 1)
    def _():
        put(1, [results[blocks + tile // ZH] for tile in range(blocks)])


def split_dot(left, weight):
    high = left.astype(bf16)
    low = (left - high.astype(f32)).astype(bf16)
    return jnp.dot(high, weight, preferred_element_type=f32) + jnp.dot(
        low, weight, preferred_element_type=f32
    )


def flow_of(heads, table, weight):
    width = len(heads) * HD
    center = sum(jnp.sum(h, axis=1, keepdims=True) for h in heads) / width
    centered = [h - center for h in heads]
    spread = sum(jnp.sum(h * h, axis=1, keepdims=True) for h in centered) / width
    shrink = lax.rsqrt(spread + epsilon)
    shift, scale = table[0, 0:1, :].astype(f32), table[0, 1:2, :].astype(f32)
    total = None
    for index, head in enumerate(centered):
        lanes = slice(index * HD, (index + 1) * HD)
        modulated = head * shrink * (1.0 + scale[:, lanes]) + shift[:, lanes]
        term = split_dot(modulated, weight[lanes, :])
        total = term if total is None else total + term
    return total


def sigma_at(index):
    remaining = 1.0 - index.astype(f32) / STEPS
    return flow_shift * remaining / (1.0 + (flow_shift - 1.0) * remaining)


def final_kernel(
    step,
    place,
    got,
    latents,
    main_mod,
    guide_mod,
    main_head,
    guide_head,
    velocity,
    advanced,
):
    zh = place[0]
    main, guide = [], []
    for zl in range(ZL):
        for zh_from in range(ZH):
            main += [got[core * Z + zh_from * ZL + zl, 0] for core in range(CORE)]
            guide += [got[zh_from * ZL + zl, 1]]
        main += [got[Z + zh * ZL + zl, 1]]
    main_flow = flow_of([h.astype(f32) for h in main], main_mod, main_head)
    guide_flow = flow_of([h.astype(f32) for h in guide], guide_mod, guide_head)
    result = guide_flow + guidance * (main_flow - guide_flow)
    now = jnp.full((1, 1), step[0], jnp.int32)
    velocity[0] = result
    advanced[0] = latents[0] + (sigma_at(now + 1) - sigma_at(now)) * result


def plane_shift(array, by, axis_of_core):
    pairs = []
    for x in range(X):
        for y in range(Y):
            for core in range(CORE):
                if axis_of_core[core] == "x":
                    to = ((x + by) % X, y)
                else:
                    to = (x, (y + by) % Y)
                pairs.append(((x * Y + y) * CORE + core, (to[0] * Y + to[1]) * CORE + core))
    return lax.ppermute(array, ("x", "y", "core"), pairs)


SHIFTS = (2, 1, -1)


def attend(queries, pairs):
    return pl.pallas_call(
        attend_kernel,
        out_shape=shape(HEADS * TOKENS + STAT, HD),
        in_specs=[VMEM] * (1 + SIDE),
        out_specs=VMEM,
        scratch_shapes=[
            pltpu.VMEM((HEADS, KEYS, 2 * HD), bf16),
            pltpu.VMEM((HEADS * TOKENS // TILE, TILE, KEYS), f32),
            pltpu.VMEM((HEADS * TOKENS // TILE, TILE, KEYS), bf16),
            pltpu.VMEM((8, HD), f32),
        ],
        compiler_params=params(32),
        cost_estimate=pl.CostEstimate(
            flops=4 * HEADS * TOKENS * KEYS * HD,
            bytes_accessed=4 * HEADS * KEYS * HD,
            transcendentals=HEADS * TOKENS * KEYS,
        ),
        name="attend",
    )(queries, *pairs)


def on_device(
    main_query,
    main_key,
    main_value,
    guide_query,
    guide_key,
    guide_value,
    latents,
    step_index,
    main_mod,
    guide_mod,
    main_head,
    guide_head,
):
    zh, core = lax.axis_index("zh"), lax.axis_index("core")
    place = jnp.stack([zh, core]).astype(jnp.int32)
    send, guide_send, guide_own = pl.pallas_call(
        pack_kernel,
        out_shape=(shape(Z, 9, ROWS, HD), shape(3, BLOCK, HD), shape(3, BLOCK, HD)),
        in_specs=[SMEM] + [ANY] * 6,
        out_specs=(VMEM,) * 3,
        scratch_shapes=[
            pltpu.VMEM((3, ROWS, 20 * HD), bf16),
            pltpu.VMEM((3, BLOCK, 2 * HD), bf16),
            pltpu.SemaphoreType.DMA((6,)),
        ],
        compiler_params=params(60),
        name="pack",
    )(place, main_query, main_key, main_value, guide_query, guide_key, guide_value)
    halves = ("zh", "core")
    guide_core = lax.ppermute(guide_own, halves, [(1, 0), (3, 2)])
    guide_half = lax.ppermute(guide_send, halves, [(0, 2), (2, 0)])
    guide_across = lax.ppermute(guide_send, halves, [(1, 2), (3, 0)])
    got = lax.all_to_all(send, ("zh", "zl"), split_axis=0, concat_axis=0, tiled=True)
    got, guide_core, guide_half, guide_across = lax.optimization_barrier(
        (got, guide_core, guide_half, guide_across)
    )
    sibling = lax.ppermute(got, "core", [(0, 1), (1, 0)])
    queries, pairs = pl.pallas_call(
        unpack_kernel,
        out_shape=(shape(HEADS * TOKENS, HD), shape(2 * HEADS, TOKENS, HD)),
        in_specs=[SMEM] + [VMEM] * 6,
        out_specs=(VMEM,) * 2,
        compiler_params=params(16),
        name="unpack",
    )(place, got, sibling, guide_own, guide_core, guide_half, guide_across)
    all_pairs = [pairs] + [plane_shift(pairs, by, "yx") for by in SHIFTS]
    parts = [attend(queries, all_pairs)]
    for by in SHIFTS:
        arrived, parts[0] = lax.optimization_barrier((plane_shift(queries, by, "xy"), parts[0]))
        part = attend(arrived, all_pairs)
        parts.append(plane_shift(part, -by, "xy"))
    send = pl.pallas_call(
        combine_kernel,
        out_shape=shape(CORE * Z, HEADS, ROWS, HD),
        in_specs=[SMEM] + [VMEM] * SIDE,
        out_specs=VMEM,
        compiler_params=params(16),
        name="combine",
    )(place, *parts)
    got = lax.all_to_all(send, ("core", "zh", "zl"), split_axis=0, concat_axis=0, tiled=True)

    whole = lambda *dims: pl.BlockSpec(dims, lambda i, step, place: (0,) * len(dims))
    row = lambda *dims: pl.BlockSpec(dims, lambda i, step, place: (step[0], 0, 0))
    velocity, advanced = pl.pallas_call(
        final_kernel,
        out_shape=(shape(1, ROWS, 64, dtype=f32),) * 2,
        grid_spec=pltpu.PrefetchScalarGridSpec(
            num_scalar_prefetch=2,
            grid=(1,),
            in_specs=[
                whole(CORE * Z, HEADS, ROWS, HD),
                whole(1, ROWS, 64),
                row(1, 2, 20 * HD),
                row(1, 2, 8 * HD),
                whole(20 * HD, 64),
                whole(8 * HD, 64),
            ],
            out_specs=[whole(1, ROWS, 64)] * 2,
        ),
        compiler_params=params(16),
        name="final",
    )(step_index, place, got, latents, main_mod, guide_mod, main_head, guide_head)
    return velocity, advanced


def solution(mesh):
    fine = Mesh(mesh.devices.reshape(ZL, X, Y, ZH, CORE), ("zl", "x", "y", "zh", "core"))
    seq = ("x", "y", "zh", "core")
    return jax.shard_map(
        on_device,
        mesh=fine,
        in_specs=(P(seq, "zl", None),) * 3
        + (P(seq, None, "zl"),) * 3
        + (P(seq, "zl", None),)
        + (P(),) * 5,
        out_specs=(P(seq, "zl", None),) * 2,
        check_vma=False,
    )
```

time: 126 us -> 104 us (0.83)
  waiting for transfers between devices: 70 us -> 39.2 us
  starting transfers between devices: 33.8 us -> 40.4 us
  Pallas kernels: 14 us -> 20 us
  local copies, waits for them, and re-layouts: 6.32 us -> 1.1 us
    ppermute x14 -> x13, waiting for transfers between devices: 61.3 us -> 30.5 us  [the longest x9 15.9 us: plane_shift(): return lax.ppermute(array, ('x', 'y', 'core'), pairs)]
    all_to_all x0 -> x1, waiting for transfers between devices: none -> 8.65 us  [on_device(): lax.all_to_all(send, ('core', 'zh', 'zl'), split_axis=0, concat_axis=0, t...]
    all_to_all x2 -> x1, waiting for transfers between devices: 8.64 us -> 0.01 us  [on_device(): lax.all_to_all(send, ('zh', 'zl'), split_axis=0, concat_axis=0, tiled=True)]
    ppermute x14 -> x13, starting transfers between devices: 21.8 us -> 28.2 us  [the longest x9 17.8 us: plane_shift(): return lax.ppermute(array, ('x', 'y', 'core'), pairs)]
    pallas_call x5 -> x8, Pallas kernels: 14 us -> 20 us  [the longest x4 12.6 us: attend(): pl.pallas_call(attend_kernel, out_shape=shape(HEADS * TOKENS + STAT, HD),...]
    unnamed x24 -> x18, local copies, waits for them, and re-layouts: 6.32 us -> 1.1 us
    all_to_all x0 -> x1, starting transfers between devices: none -> 3.66 us  [on_device(): lax.all_to_all(send, ('core', 'zh', 'zl'), split_axis=0, concat_axis=0, t...]
    all_to_all x2 -> x1, starting transfers between devices: 12 us -> 8.61 us  [on_device(): lax.all_to_all(send, ('zh', 'zl'), split_axis=0, concat_axis=0, tiled=True)]
  transfers between devices with their start and end apart: 16 -> 15, of which waited for: 9 -> 8; matrix products, arithmetic and copies ran while one was open for 0% -> 0% of each run, Pallas kernels for 0% -> 9%
where the time goes in v2:
time: 104 us; the launch traced here: 103 us
  starting transfers between devices  40.4 us (39%)
  waiting for transfers between devices  39.2 us (38%)
  Pallas kernels  20 us (19%)
  between operations  1.46 us (1%)
  local copies, waits for them, and re-layouts  1.1 us (1%)
    ppermute x9, starting transfers between devices, plane_shift(): return lax.ppermute(array, ('x', 'y', 'core'), pairs)  17.8 us
    ppermute x9, waiting for transfers between devices, plane_shift(): return lax.ppermute(array, ('x', 'y', 'core'), pairs)  15.9 us
    pallas_call x4, Pallas kernels, attend(): pl.pallas_call(attend_kernel, out_shape=shape(HEADS * TOKENS + STAT, HD),...  12.6 us
    ppermute x1, waiting for transfers between devices, on_device(): guide_half = lax.ppermute(guide_send, halves, [(0, 2), (2, 0)])  12.5 us
    all_to_all x1, waiting for transfers between devices, on_device(): lax.all_to_all(send, ('core', 'zh', 'zl'), split_axis=0, concat_axis=0, t...  8.65 us
    all_to_all x1, starting transfers between devices, on_device(): lax.all_to_all(send, ('zh', 'zl'), split_axis=0, concat_axis=0, tiled=True)  8.61 us
    ppermute x1, starting transfers between devices, on_device(): guide_half = lax.ppermute(guide_send, halves, [(0, 2), (2, 0)])  7.82 us
    all_to_all x1, starting transfers between devices, on_device(): lax.all_to_all(send, ('core', 'zh', 'zl'), split_axis=0, concat_axis=0, t...  3.66 us
  transfers between devices with their start and end apart: 15, of which 8 were waited for; matrix products, arithmetic and copies ran while one was open for 0% of the time, Pallas kernels for 9%

profile of v2, /device:TPU:24, one launch (start us, length us, event | category | flops | bytes accessed | tf_op | source)
XLA Modules:
  0.0 102.7 jit_solution(5322442721247004681)
XLA Ops:
  0.6 0.6 pad_add_fusion.place
  1.2 2.7 %pack.1 = (bf16[8,9,32,128]{3,2,1,0:T(8,128)(2,1)}, bf16[3,128,128]{2,1,0:T(8,128)(2,1)}, bf16[3,128,128]{2,1,0:T(8,128)(2,1)}) custom-call(s32[2]{0:T(128)} %pad_add_fusion.place, bf16[1,32,2560]{2,1,0:T(8,128)(2,1)} %mq.1, bf16[1,32,2560]{2,1,0:T(8,128)(2,1)} %mk.1, bf16[1,32,2560]{2,1,0:T(8,128)(2,1)} %mv.1, bf16[1,128,256]{2,1,0:T(8,128)(2,1)} %gq.1, ...), custom_call_target="tpu_custom_call" | custom-call | tf_op jit(solution)/shard_map/pack/pallas_call | solution.py:320
  4.0 8.6 %all-to-all-start = ((bf16[8,9,32,128]{3,2,1,0:T(8,128)(2,1)}), bf16[8,9,32,128]{3,2,1,0:T(8,128)(2,1)S(1)}, u32[]{:S(2)}, u32[]{:S(2)}) async-start(bf16[8,9,32,128]{3,2,1,0:T(8,128)(2,1)} %get-tuple-element.17), calls=%async_computation | async-start | bytes 1179648 | tf_op jit(solution)/shard_map/all_to_all | solution.py:337
  12.6 1.3 %collective-permute-start = (bf16[3,128,128]{2,1,0:T(8,128)(2,1)S(1)}, bf16[3,128,128]{2,1,0:T(8,128)(2,1)S(1)}, u32[]{:S(2)}, u32[]{:S(2)}) collective-permute-start(bf16[3,128,128]{2,1,0:T(8,128)(2,1)S(1)} %copy-done.2), channel_id=1, source_target_pairs={{1,0},{3,2},{5,4},{7,6},{9,8},{11,10},{13,12},{15,14},{17,16},{19,... | collective-permute-start | bytes 294920 | tf_op jit(solution)/shard_map/ppermute | solution.py:334
  13.9 7.8 %collective-permute-start.1 = (bf16[3,128,128]{2,1,0:T(8,128)(2,1)S(1)}, bf16[3,128,128]{2,1,0:T(8,128)(2,1)S(1)}, u32[]{:S(2)}, u32[]{:S(2)}) collective-permute-start(bf16[3,128,128]{2,1,0:T(8,128)(2,1)S(1)} %copy-done.7), channel_id=1, source_target_pairs={{0,2},{2,0},{4,6},{6,4},{8,10},{10,8},{12,14},{14,12},{16,18},{18,... | collective-permute-start | bytes 294920 | tf_op jit(solution)/shard_map/ppermute | solution.py:335
  21.8 1.3 %collective-permute-start.2 = (bf16[3,128,128]{2,1,0:T(8,128)(2,1)S(1)}, bf16[3,128,128]{2,1,0:T(8,128)(2,1)S(1)}, u32[]{:S(2)}, u32[]{:S(2)}) collective-permute-start(bf16[3,128,128]{2,1,0:T(8,128)(2,1)S(1)} %copy-done.7), channel_id=1, source_target_pairs={{1,2},{3,0},{5,6},{7,4},{9,10},{11,8},{13,14},{15,12},{17,18},{19,... | collective-permute-start | bytes 294920 | tf_op jit(solution)/shard_map/ppermute | solution.py:336
  23.1 12.5 %collective-permute-done.1.guide_half = bf16[3,128,128]{2,1,0:T(8,128)(2,1)S(1)} collective-permute-done((bf16[3,128,128]{2,1,0:T(8,128)(2,1)S(1)}, bf16[3,128,128]{2,1,0:T(8,128)(2,1)S(1)}, u32[]{:S(2)}, u32[]{:S(2)}) %collective-permute-start.1) | collective-permute-done | bytes 98336 | tf_op jit(solution)/shard_map/ppermute | solution.py:335
  35.5 0.2 collective-permute-done.2.guide_across
  35.7 2.0 %collective-permute-done.3.sibling = bf16[8,9,32,128]{3,2,1,0:T(8,128)(2,1)S(1)} collective-permute-done((bf16[8,9,32,128]{3,2,1,0:T(8,128)(2,1)S(1)}, bf16[8,9,32,128]{3,2,1,0:T(8,128)(2,1)S(1)}, u32[]{:S(2)}, u32[]{:S(2)}) %collective-permute-start.3) | collective-permute-done | bytes 589856 | tf_op jit(solution)/shard_map/ppermute | solution.py:341
  37.7 0.6 unpack.1
  38.4 1.3 %collective-permute-start.7 = (bf16[4,512,128]{2,1,0:T(8,128)(2,1)S(1)}, bf16[4,512,128]{2,1,0:T(8,128)(2,1)S(1)}, u32[]{:S(2)}, u32[]{:S(2)}) collective-permute-start(bf16[4,512,128]{2,1,0:T(8,128)(2,1)S(1)} %get-tuple-element.25.refs_0_), channel_id=1, source_target_pairs={{0,8},{1,33},{4,12},{5,37},{8,0},{9,41},{12,4},{13,45},{16,24},{17... | collective-permute-start | bytes 1572872 | tf_op jit(solution)/shard_map/ppermute | solution.py:276
  39.7 2.2 %collective-permute-start.8 = (bf16[4,512,128]{2,1,0:T(8,128)(2,1)S(1)}, bf16[4,512,128]{2,1,0:T(8,128)(2,1)S(1)}, u32[]{:S(2)}, u32[]{:S(2)}) collective-permute-start(bf16[4,512,128]{2,1,0:T(8,128)(2,1)S(1)} %get-tuple-element.25.refs_0_), channel_id=1, source_target_pairs={{0,4},{1,17},{4,8},{5,21},{8,12},{9,25},{12,0},{13,29},{16,20},{17... | collective-permute-start | bytes 1572872 | tf_op jit(solution)/shard_map/ppermute | solution.py:276
  41.9 3.0 %collective-permute-start.6 = (bf16[1024,128]{1,0:T(8,128)(2,1)S(1)}, bf16[1024,128]{1,0:T(8,128)(2,1)S(1)}, u32[]{:S(2)}, u32[]{:S(2)}) collective-permute-start(bf16[1024,128]{1,0:T(8,128)(2,1)S(1)} %get-tuple-element.24.queries), channel_id=1, source_target_pairs={{0,32},{1,9},{4,36},{5,13},{8,40},{9,1},{12,44},{13,5},{16,48},{17... | collective-permute-start | bytes 786440 | tf_op jit(solution)/shard_map/ppermute | solution.py:276
  44.9 0.6 collective-permute-start.5
  45.5 4.7 %collective-permute-done.7.refs_1_ = bf16[4,512,128]{2,1,0:T(8,128)(2,1)S(1)} collective-permute-done((bf16[4,512,128]{2,1,0:T(8,128)(2,1)S(1)}, bf16[4,512,128]{2,1,0:T(8,128)(2,1)S(1)}, u32[]{:S(2)}, u32[]{:S(2)}) %collective-permute-start.7) | collective-permute-done | bytes 524320 | tf_op jit(solution)/shard_map/ppermute | solution.py:276
  50.2 5.2 %collective-permute-start.4 = (bf16[1024,128]{1,0:T(8,128)(2,1)S(1)}, bf16[1024,128]{1,0:T(8,128)(2,1)S(1)}, u32[]{:S(2)}, u32[]{:S(2)}) collective-permute-start(bf16[1024,128]{1,0:T(8,128)(2,1)S(1)} %get-tuple-element.24.queries), channel_id=1, source_target_pairs={{0,48},{1,13},{4,52},{5,1},{8,56},{9,5},{12,60},{13,9},{16,0},{17,... | collective-permute-start | bytes 786440 | tf_op jit(solution)/shard_map/ppermute | solution.py:276
  55.4 2.6 %collective-permute-done.8.refs_2_ = bf16[4,512,128]{2,1,0:T(8,128)(2,1)S(1)} collective-permute-done((bf16[4,512,128]{2,1,0:T(8,128)(2,1)S(1)}, bf16[4,512,128]{2,1,0:T(8,128)(2,1)S(1)}, u32[]{:S(2)}, u32[]{:S(2)}) %collective-permute-start.8) | collective-permute-done | bytes 524320 | tf_op jit(solution)/shard_map/ppermute | solution.py:276
  58.0 2.4 %collective-permute-done.9.refs_3_ = bf16[4,512,128]{2,1,0:T(8,128)(2,1)S(1)} collective-permute-done((bf16[4,512,128]{2,1,0:T(8,128)(2,1)S(1)}, bf16[4,512,128]{2,1,0:T(8,128)(2,1)S(1)}, u32[]{:S(2)}, u32[]{:S(2)}) %collective-permute-start.9) | collective-permute-done | bytes 524320 | tf_op jit(solution)/shard_map/ppermute | solution.py:276
  60.4 3.2 %attend.4.refs_0_ = bf16[1056,128]{1,0:T(8,128)(2,1)S(1)} custom-call(bf16[1024,128]{1,0:T(8,128)(2,1)S(1)} %get-tuple-element.24.queries, bf16[4,512,128]{2,1,0:T(8,128)(2,1)S(1)} %get-tuple-element.25.refs_0_, bf16[4,512,128]{2,1,0:T(8,128)(2,1)S(1)} %collective-permute-done.7.refs_1_, bf16[4,512,128]{2,1,0:T(8,128)(2,1)S(1)} %collective-permute-done.8.refs_2_, ...), custom_call_target="tpu_custom_call" | custom-call | flops 1073741824 | bytes 2097152 | tf_op jit(solution)/shard_map/attend/pallas_call | solution.py:283
  63.6 3.2 %attend.7 = bf16[1056,128]{1,0:T(8,128)(2,1)S(1)} custom-call(bf16[1024,128]{1,0:T(8,128)(2,1)S(1)} %collective-permute-done.4.queries, bf16[4,512,128]{2,1,0:T(8,128)(2,1)S(1)} %get-tuple-element.25.refs_0_, bf16[4,512,128]{2,1,0:T(8,128)(2,1)S(1)} %collective-permute-done.7.refs_1_, bf16[4,512,128]{2,1,0:T(8,128)(2,1)S(1)} %collective-permute-done.8.refs_2_, ...), custom_call_target="tpu_custom_call" | custom-call | flops 1073741824 | bytes 2097152 | tf_op jit(solution)/shard_map/attend/pallas_call | solution.py:283
  66.7 1.7 %collective-permute-start.12 = (bf16[1056,128]{1,0:T(8,128)(2,1)S(1)}, bf16[1056,128]{1,0:T(8,128)(2,1)S(1)}, u32[]{:S(2)}, u32[]{:S(2)}) collective-permute-start(bf16[1056,128]{1,0:T(8,128)(2,1)S(1)} %attend.7), channel_id=1, source_target_pairs={{0,16},{1,5},{4,20},{5,9},{8,24},{9,13},{12,28},{13,1},{16,32},{17... | collective-permute-start | bytes 811016 | tf_op jit(solution)/shard_map/ppermute | solution.py:276
  68.5 3.2 %attend.6 = bf16[1056,128]{1,0:T(8,128)(2,1)S(1)} custom-call(bf16[1024,128]{1,0:T(8,128)(2,1)S(1)} %collective-permute-done.5.queries, bf16[4,512,128]{2,1,0:T(8,128)(2,1)S(1)} %get-tuple-element.25.refs_0_, bf16[4,512,128]{2,1,0:T(8,128)(2,1)S(1)} %collective-permute-done.7.refs_1_, bf16[4,512,128]{2,1,0:T(8,128)(2,1)S(1)} %collective-permute-done.8.refs_2_, ...), custom_call_target="tpu_custom_call" | custom-call | flops 1073741824 | bytes 2097152 | tf_op jit(solution)/shard_map/attend/pallas_call | solution.py:283
  71.6 1.8 %collective-permute-start.11 = (bf16[1056,128]{1,0:T(8,128)(2,1)S(1)}, bf16[1056,128]{1,0:T(8,128)(2,1)S(1)}, u32[]{:S(2)}, u32[]{:S(2)}) collective-permute-start(bf16[1056,128]{1,0:T(8,128)(2,1)S(1)} %attend.6), channel_id=1, source_target_pairs={{0,48},{1,13},{4,52},{5,1},{8,56},{9,5},{12,60},{13,9},{16,0},{17,... | collective-permute-start | bytes 811016 | tf_op jit(solution)/shard_map/ppermute | solution.py:276
  73.4 3.2 %attend.5 = bf16[1056,128]{1,0:T(8,128)(2,1)S(1)} custom-call(bf16[1024,128]{1,0:T(8,128)(2,1)S(1)} %collective-permute-done.6.queries, bf16[4,512,128]{2,1,0:T(8,128)(2,1)S(1)} %get-tuple-element.25.refs_0_, bf16[4,512,128]{2,1,0:T(8,128)(2,1)S(1)} %collective-permute-done.7.refs_1_, bf16[4,512,128]{2,1,0:T(8,128)(2,1)S(1)} %collective-permute-done.8.refs_2_, ...), custom_call_target="tpu_custom_call" | custom-call | flops 1073741824 | bytes 2097152 | tf_op jit(solution)/shard_map/attend/pallas_call | solution.py:283
  76.6 1.9 %collective-permute-start.10 = (bf16[1056,128]{1,0:T(8,128)(2,1)S(1)}, bf16[1056,128]{1,0:T(8,128)(2,1)S(1)}, u32[]{:S(2)}, u32[]{:S(2)}) collective-permute-start(bf16[1056,128]{1,0:T(8,128)(2,1)S(1)} %attend.5), channel_id=1, source_target_pairs={{0,32},{1,9},{4,36},{5,13},{8,40},{9,1},{12,44},{13,5},{16,48},{17... | collective-permute-start | bytes 811016 | tf_op jit(solution)/shard_map/ppermute | solution.py:276
  78.5 6.1 %collective-permute-done.10.refs_1_ = bf16[1056,128]{1,0:T(8,128)(2,1)S(1)} collective-permute-done((bf16[1056,128]{1,0:T(8,128)(2,1)S(1)}, bf16[1056,128]{1,0:T(8,128)(2,1)S(1)}, u32[]{:S(2)}, u32[]{:S(2)}) %collective-permute-start.10) | collective-permute-done | bytes 270368 | tf_op jit(solution)/shard_map/ppermute | solution.py:276
  84.6 1.9 %combine.1 = bf16[16,2,32,128]{3,2,1,0:T(8,128)(2,1)} custom-call(s32[2]{0:T(128)S(1)} %copy-done.4, bf16[1056,128]{1,0:T(8,128)(2,1)S(1)} %attend.4.refs_0_, bf16[1056,128]{1,0:T(8,128)(2,1)S(1)} %collective-permute-done.10.refs_1_, bf16[1056,128]{1,0:T(8,128)(2,1)S(1)} %collective-permute-done.11.refs_2_, bf16[1056,128]{1,0:T(8,128)(2,1)S(1)} %collective-permute-done.12.refs_3_), custom_call_target="tpu_custom_call" | custom-call | tf_op jit(solution)/shard_map/combine/pallas_call | solution.py:356
  86.6 3.7 %all-to-all-start.1 = ((bf16[16,2,32,128]{3,2,1,0:T(8,128)(2,1)}), bf16[16,2,32,128]{3,2,1,0:T(8,128)(2,1)S(1)}, u32[]{:S(2)}, u32[]{:S(2)}) async-start(bf16[16,2,32,128]{3,2,1,0:T(8,128)(2,1)} %combine.1), calls=%async_computation.1 | async-start | bytes 524288 | tf_op jit(solution)/shard_map/all_to_all | solution.py:364
  90.3 0.3 copy.14.main_head
  90.6 0.6 copy-done.6
  92.0 8.6 %all-to-all-done.1.got = bf16[16,2,32,128]{3,2,1,0:T(8,128)(2,1)S(1)} async-done(((bf16[16,2,32,128]{3,2,1,0:T(8,128)(2,1)}), bf16[16,2,32,128]{3,2,1,0:T(8,128)(2,1)S(1)}, u32[]{:S(2)}, u32[]{:S(2)}) %all-to-all-start.1) | async-done | bytes 262176 | tf_op jit(solution)/shard_map/all_to_all | solution.py:364
  100.7 2.1 %final.1 = (f32[1,32,64]{2,1,0:T(8,128)}, f32[1,32,64]{2,1,0:T(8,128)}) custom-call(s32[1]{0:T(128)S(6)} %copy.16.step, s32[2]{0:T(128)S(1)} %copy-done.4, bf16[16,2,32,128]{3,2,1,0:T(8,128)(2,1)S(1)} %all-to-all-done.1.got, f32[1,32,64]{2,1,0:T(8,128)S(1)} %copy-done.3, bf16[50,2,2560]{2,1,0:T(2,128)(2,1)S(1)} %copy-done, ...), custom_call_target="tpu_custom_call" | custom-call | tf_op jit(solution)/shard_map/final/pallas_call | solution.py:368
  (25 shorter events, 0.2 us)
Async XLA Ops:
  4.0 8.6 %copy-start.2 = (bf16[3,128,128]{2,1,0:T(8,128)(2,1)S(1)}, bf16[3,128,128]{2,1,0:T(8,128)(2,1)}, u32[]{:S(2)}) copy-start(bf16[3,128,128]{2,1,0:T(8,128)(2,1)} %get-tuple-element.18.guide_own) | copy-start | bytes 294916
  4.0 9.9 %copy-start.7 = (bf16[3,128,128]{2,1,0:T(8,128)(2,1)S(1)}, bf16[3,128,128]{2,1,0:T(8,128)(2,1)}, u32[]{:S(2)}) copy-start(bf16[3,128,128]{2,1,0:T(8,128)(2,1)} %get-tuple-element.19) | copy-start | bytes 294916
  4.0 31.7 %all-to-all-start = ((bf16[8,9,32,128]{3,2,1,0:T(8,128)(2,1)}), bf16[8,9,32,128]{3,2,1,0:T(8,128)(2,1)S(1)}, u32[]{:S(2)}, u32[]{:S(2)}) async-start(bf16[8,9,32,128]{3,2,1,0:T(8,128)(2,1)} %get-tuple-element.17), calls=%async_computation | async-start | bytes 1179648 | tf_op jit(solution)/shard_map/all_to_all | solution.py:337
  12.6 25.1 %copy-start.4 = (s32[2]{0:T(128)S(1)}, s32[2]{0:T(128)}, u32[]{:S(2)}) copy-start(s32[2]{0:T(128)} %pad_add_fusion.place) | copy-start | bytes 28
  12.6 10.4 %collective-permute-start = (bf16[3,128,128]{2,1,0:T(8,128)(2,1)S(1)}, bf16[3,128,128]{2,1,0:T(8,128)(2,1)S(1)}, u32[]{:S(2)}, u32[]{:S(2)}) collective-permute-start(bf16[3,128,128]{2,1,0:T(8,128)(2,1)S(1)} %copy-done.2), channel_id=1, source_target_pairs={{1,0},{3,2},{5,4},{7,6},{9,8},{11,10},{13,12},{15,14},{17,16},{19,... | collective-permute-start | bytes 294920 | tf_op jit(solution)/shard_map/ppermute | solution.py:334
  13.9 21.6 %collective-permute-start.1 = (bf16[3,128,128]{2,1,0:T(8,128)(2,1)S(1)}, bf16[3,128,128]{2,1,0:T(8,128)(2,1)S(1)}, u32[]{:S(2)}, u32[]{:S(2)}) collective-permute-start(bf16[3,128,128]{2,1,0:T(8,128)(2,1)S(1)} %copy-done.7), channel_id=1, source_target_pairs={{0,2},{2,0},{4,6},{6,4},{8,10},{10,8},{12,14},{14,12},{16,18},{18,... | collective-permute-start | bytes 294920 | tf_op jit(solution)/shard_map/ppermute | solution.py:335
  21.8 14.0 %collective-permute-start.2 = (bf16[3,128,128]{2,1,0:T(8,128)(2,1)S(1)}, bf16[3,128,128]{2,1,0:T(8,128)(2,1)S(1)}, u32[]{:S(2)}, u32[]{:S(2)}) collective-permute-start(bf16[3,128,128]{2,1,0:T(8,128)(2,1)S(1)} %copy-done.7), channel_id=1, source_target_pairs={{1,2},{3,0},{5,6},{7,4},{9,10},{11,8},{13,14},{15,12},{17,18},{19,... | collective-permute-start | bytes 294920 | tf_op jit(solution)/shard_map/ppermute | solution.py:336
  35.7 2.0 %collective-permute-start.3 = (bf16[8,9,32,128]{3,2,1,0:T(8,128)(2,1)S(1)}, bf16[8,9,32,128]{3,2,1,0:T(8,128)(2,1)S(1)}, u32[]{:S(2)}, u32[]{:S(2)}) collective-permute-start(bf16[8,9,32,128]{3,2,1,0:T(8,128)(2,1)S(1)} %all-to-all-done.got), channel_id=1, source_target_pairs={{0,1},{1,0},{2,3},{3,2},{4,5},{5,4},{6,7},{7,6},{8,9},{9,8},{10,11... | collective-permute-start | bytes 1769480 | tf_op jit(solution)/shard_map/ppermute | solution.py:341
  38.4 11.8 %collective-permute-start.7 = (bf16[4,512,128]{2,1,0:T(8,128)(2,1)S(1)}, bf16[4,512,128]{2,1,0:T(8,128)(2,1)S(1)}, u32[]{:S(2)}, u32[]{:S(2)}) collective-permute-start(bf16[4,512,128]{2,1,0:T(8,128)(2,1)S(1)} %get-tuple-element.25.refs_0_), channel_id=1, source_target_pairs={{0,8},{1,33},{4,12},{5,37},{8,0},{9,41},{12,4},{13,45},{16,24},{17... | collective-permute-start | bytes 1572872 | tf_op jit(solution)/shard_map/ppermute | solution.py:276
  39.7 18.3 %collective-permute-start.8 = (bf16[4,512,128]{2,1,0:T(8,128)(2,1)S(1)}, bf16[4,512,128]{2,1,0:T(8,128)(2,1)S(1)}, u32[]{:S(2)}, u32[]{:S(2)}) collective-permute-start(bf16[4,512,128]{2,1,0:T(8,128)(2,1)S(1)} %get-tuple-element.25.refs_0_), channel_id=1, source_target_pairs={{0,4},{1,17},{4,8},{5,21},{8,12},{9,25},{12,0},{13,29},{16,20},{17... | collective-permute-start | bytes 1572872 | tf_op jit(solution)/shard_map/ppermute | solution.py:276
  41.9 18.5 %collective-permute-start.9 = (bf16[4,512,128]{2,1,0:T(8,128)(2,1)S(1)}, bf16[4,512,128]{2,1,0:T(8,128)(2,1)S(1)}, u32[]{:S(2)}, u32[]{:S(2)}) collective-permute-start(bf16[4,512,128]{2,1,0:T(8,128)(2,1)S(1)} %get-tuple-element.25.refs_0_), channel_id=1, source_target_pairs={{0,12},{1,49},{4,0},{5,53},{8,4},{9,57},{12,8},{13,61},{16,28},{17... | collective-permute-start | bytes 1572872 | tf_op jit(solution)/shard_map/ppermute | solution.py:276
  41.9 21.7 %collective-permute-start.6 = (bf16[1024,128]{1,0:T(8,128)(2,1)S(1)}, bf16[1024,128]{1,0:T(8,128)(2,1)S(1)}, u32[]{:S(2)}, u32[]{:S(2)}) collective-permute-start(bf16[1024,128]{1,0:T(8,128)(2,1)S(1)} %get-tuple-element.24.queries), channel_id=1, source_target_pairs={{0,32},{1,9},{4,36},{5,13},{8,40},{9,1},{12,44},{13,5},{16,48},{17... | collective-permute-start | bytes 786440 | tf_op jit(solution)/shard_map/ppermute | solution.py:276
  44.9 18.6 %collective-permute-start.5 = (bf16[1024,128]{1,0:T(8,128)(2,1)S(1)}, bf16[1024,128]{1,0:T(8,128)(2,1)S(1)}, u32[]{:S(2)}, u32[]{:S(2)}) collective-permute-start(bf16[1024,128]{1,0:T(8,128)(2,1)S(1)} %get-tuple-element.24.queries), channel_id=1, source_target_pairs={{0,16},{1,5},{4,20},{5,9},{8,24},{9,13},{12,28},{13,1},{16,32},{17... | collective-permute-start | bytes 786440 | tf_op jit(solution)/shard_map/ppermute | solution.py:276
  50.2 13.4 %collective-permute-start.4 = (bf16[1024,128]{1,0:T(8,128)(2,1)S(1)}, bf16[1024,128]{1,0:T(8,128)(2,1)S(1)}, u32[]{:S(2)}, u32[]{:S(2)}) collective-permute-start(bf16[1024,128]{1,0:T(8,128)(2,1)S(1)} %get-tuple-element.24.queries), channel_id=1, source_target_pairs={{0,48},{1,13},{4,52},{5,1},{8,56},{9,5},{12,60},{13,9},{16,0},{17,... | collective-permute-start | bytes 786440 | tf_op jit(solution)/shard_map/ppermute | solution.py:276
  66.7 11.8 %collective-permute-start.12 = (bf16[1056,128]{1,0:T(8,128)(2,1)S(1)}, bf16[1056,128]{1,0:T(8,128)(2,1)S(1)}, u32[]{:S(2)}, u32[]{:S(2)}) collective-permute-start(bf16[1056,128]{1,0:T(8,128)(2,1)S(1)} %attend.7), channel_id=1, source_target_pairs={{0,16},{1,5},{4,20},{5,9},{8,24},{9,13},{12,28},{13,1},{16,32},{17... | collective-permute-start | bytes 811016 | tf_op jit(solution)/shard_map/ppermute | solution.py:276
  71.6 6.9 %collective-permute-start.11 = (bf16[1056,128]{1,0:T(8,128)(2,1)S(1)}, bf16[1056,128]{1,0:T(8,128)(2,1)S(1)}, u32[]{:S(2)}, u32[]{:S(2)}) collective-permute-start(bf16[1056,128]{1,0:T(8,128)(2,1)S(1)} %attend.6), channel_id=1, source_target_pairs={{0,48},{1,13},{4,52},{5,1},{8,56},{9,5},{12,60},{13,9},{16,0},{17,... | collective-permute-start | bytes 811016 | tf_op jit(solution)/shard_map/ppermute | solution.py:276
  76.6 8.0 %collective-permute-start.10 = (bf16[1056,128]{1,0:T(8,128)(2,1)S(1)}, bf16[1056,128]{1,0:T(8,128)(2,1)S(1)}, u32[]{:S(2)}, u32[]{:S(2)}) collective-permute-start(bf16[1056,128]{1,0:T(8,128)(2,1)S(1)} %attend.5), channel_id=1, source_target_pairs={{0,32},{1,9},{4,36},{5,13},{8,40},{9,1},{12,44},{13,5},{16,48},{17... | collective-permute-start | bytes 811016 | tf_op jit(solution)/shard_map/ppermute | solution.py:276
  86.6 3.7 %copy-start.5 = (bf16[2560,64]{0,1:T(8,128)(2,1)S(1)}, bf16[2560,64]{0,1:T(8,128)(2,1)}, u32[]{:S(2)}) copy-start(bf16[2560,64]{0,1:T(8,128)(2,1)} %param.22) | copy-start | bytes 983044
  86.6 14.1 %all-to-all-start.1 = ((bf16[16,2,32,128]{3,2,1,0:T(8,128)(2,1)}), bf16[16,2,32,128]{3,2,1,0:T(8,128)(2,1)S(1)}, u32[]{:S(2)}, u32[]{:S(2)}) async-start(bf16[16,2,32,128]{3,2,1,0:T(8,128)(2,1)} %combine.1), calls=%async_computation.1 | async-start | bytes 524288 | tf_op jit(solution)/shard_map/all_to_all | solution.py:364
  90.2 0.9 copy-start.6
  90.3 10.4 %copy-start = (bf16[50,2,2560]{2,1,0:T(2,128)(2,1)S(1)}, bf16[50,2,2560]{2,1,0:T(2,128)(2,1)}, u32[]{:S(2)}) copy-start(bf16[50,2,2560]{2,1,0:T(2,128)(2,1)} %main_mod.1) | copy-start | bytes 1536004
  91.2 9.5 %copy-start.1 = (bf16[50,2,1024]{2,1,0:T(2,128)(2,1)S(1)}, bf16[50,2,1024]{2,1,0:T(2,128)(2,1)}, u32[]{:S(2)}) copy-start(bf16[50,2,1024]{2,1,0:T(2,128)(2,1)} %guide_mod.1) | copy-start | bytes 614404
  91.2 9.5 %copy-start.3 = (f32[1,32,64]{2,1,0:T(8,128)S(1)}, f32[1,32,64]{2,1,0:T(8,128)}, u32[]{:S(2)}) copy-start(f32[1,32,64]{2,1,0:T(8,128)} %latents.1) | copy-start | bytes 24580

commit v3 on v2

--- a/solution.py
+++ b/solution.py
@@ -120,9 +120,9 @@
             values[head, rows, HD:] = jnp.ones((TOKENS, HD), bf16)
     on_diagonal = diagonal()
     parts = [(piece, half) for piece in range(SIDE) for half in range(TOKENS // TILE)]
-    tiles = HEADS * TOKENS // TILE
-
-    def score_tile(tile):
+    tiles = range(HEADS * TOKENS // TILE)
+    tops = []
+    for tile in tiles:
         head = tile * TILE // TOKENS
         query = queries[tile * TILE : (tile + 1) * TILE, :]
         highest = None
@@ -136,29 +136,23 @@
             scores[tile, :, index * TILE : (index + 1) * TILE] = part
             here = jnp.maximum(part[:, :HD], part[:, HD:])
             highest = here if highest is None else jnp.maximum(highest, here)
-        return jnp.max(highest, axis=1, keepdims=True) * score_scale
-
-    def weight_tile(tile, highest):
+        tops.append(jnp.max(highest, axis=1, keepdims=True) * score_scale)
+    for tile in tiles:
         for index in range(len(parts)):
             columns = slice(index * TILE, (index + 1) * TILE)
             part = scores[tile, :, columns]
-            weights[tile, :, columns] = jnp.exp2(part * score_scale - highest).astype(bf16)
+            weights[tile, :, columns] = jnp.exp2(part * score_scale - tops[tile]).astype(bf16)
+    for tile in tiles:
         total = jnp.dot(
             weights[tile], values[tile * TILE // TOKENS], preferred_element_type=f32
         )
         weight_sum = total[:, HD:]
         out[tile * TILE : (tile + 1) * TILE, :] = (total[:, :HD] / weight_sum).astype(bf16)
-        level = highest + jnp.log2(weight_sum)
+        level = tops[tile] + jnp.log2(weight_sum)
         for part in range(TILE // HD):
             block = level[part * HD : (part + 1) * HD, :]
             row = jnp.sum(jnp.where(on_diagonal, block, 0.0), axis=0, keepdims=True)
             stats[tile * (TILE // HD) + part : tile * (TILE // HD) + part + 1, :] = row
-
-    tops = [score_tile(0)]
-    for tile in range(tiles):
-        if tile + 1 < tiles:
-            tops.append(score_tile(tile + 1))
-        weight_tile(tile, tops[tile])
     level = stats[...]
     high = level.astype(bf16).astype(f32)
     middle = (level - high).astype(bf16).astype(f32)
@@ -169,7 +163,6 @@
 
 def combine_kernel(place, *refs):
     parts, send = refs[:SIDE], refs[SIDE]
-    on_diagonal = diagonal()
     levels = []
     for part in parts:
         block = part[HEADS * TOKENS :, :].astype(f32)
@@ -179,13 +172,13 @@
         top = jnp.maximum(top, level)
     shares = [jnp.exp2(level - top) for level in levels]
     whole = shares[0] + shares[1] + shares[2] + shares[3]
-    shares = [share / whole for share in shares]
+    filler = jnp.zeros((HD - 8, HD), f32)
+    shares = [jnp.transpose(jnp.concatenate([share / whole, filler], axis=0)) for share in shares]
     results = []
     for tile in range(HEADS * TOKENS // HD):
         total = None
         for part, share in zip(parts, shares):
-            row = jnp.broadcast_to(share[tile : tile + 1, :], (HD, HD))
-            column = jnp.sum(jnp.where(on_diagonal, row, 0.0), axis=1, keepdims=True)
+            column = share[:, tile : tile + 1]
             term = part[tile * HD : (tile + 1) * HD, :].astype(f32) * column
             total = term if total is None else total + term
         results.append(total.astype(bf16))
@@ -207,28 +200,20 @@
         put(1, [results[blocks + tile // ZH] for tile in range(blocks)])
 
 
-def split_dot(left, weight):
-    high = left.astype(bf16)
-    low = (left - high.astype(f32)).astype(bf16)
-    return jnp.dot(high, weight, preferred_element_type=f32) + jnp.dot(
-        low, weight, preferred_element_type=f32
-    )
-
-
 def flow_of(heads, table, weight):
     width = len(heads) * HD
-    center = sum(jnp.sum(h, axis=1, keepdims=True) for h in heads) / width
+    center = jnp.sum(sum(heads), axis=1, keepdims=True) / width
     centered = [h - center for h in heads]
-    spread = sum(jnp.sum(h * h, axis=1, keepdims=True) for h in centered) / width
+    spread = jnp.sum(sum(h * h for h in centered), axis=1, keepdims=True) / width
     shrink = lax.rsqrt(spread + epsilon)
     shift, scale = table[0, 0:1, :].astype(f32), table[0, 1:2, :].astype(f32)
-    total = None
-    for index, head in enumerate(centered):
-        lanes = slice(index * HD, (index + 1) * HD)
-        modulated = head * shrink * (1.0 + scale[:, lanes]) + shift[:, lanes]
-        term = split_dot(modulated, weight[lanes, :])
-        total = term if total is None else total + term
-    return total
+    modulated = jnp.concatenate(centered, axis=1) * shrink * (1.0 + scale) + shift
+    high = modulated.astype(bf16)
+    low = (modulated - high.astype(f32)).astype(bf16)
+    both = jnp.dot(
+        jnp.concatenate([high, low], axis=0), weight[...], preferred_element_type=f32
+    )
+    return both[:ROWS] + both[ROWS:]
 
 
 def sigma_at(index):
@@ -280,22 +265,23 @@
 
 
 def attend(queries, pairs):
+    rows, tiles = HEADS * TOKENS, HEADS * TOKENS // TILE
     return pl.pallas_call(
         attend_kernel,
-        out_shape=shape(HEADS * TOKENS + STAT, HD),
+        out_shape=shape(rows + STAT, HD),
         in_specs=[VMEM] * (1 + SIDE),
         out_specs=VMEM,
         scratch_shapes=[
             pltpu.VMEM((HEADS, KEYS, 2 * HD), bf16),
-            pltpu.VMEM((HEADS * TOKENS // TILE, TILE, KEYS), f32),
-            pltpu.VMEM((HEADS * TOKENS // TILE, TILE, KEYS), bf16),
+            pltpu.VMEM((tiles, TILE, KEYS), f32),
+            pltpu.VMEM((tiles, TILE, KEYS), bf16),
             pltpu.VMEM((8, HD), f32),
         ],
         compiler_params=params(32),
         cost_estimate=pl.CostEstimate(
-            flops=4 * HEADS * TOKENS * KEYS * HD,
+            flops=4 * rows * KEYS * HD,
             bytes_accessed=4 * HEADS * KEYS * HD,
-            transcendentals=HEADS * TOKENS * KEYS,
+            transcendentals=rows * KEYS,
         ),
         name="attend",
     )(queries, *pairs)
@@ -347,12 +333,10 @@
         compiler_params=params(16),
         name="unpack",
     )(place, got, sibling, guide_own, guide_core, guide_half, guide_across)
+    all_queries = [queries] + [plane_shift(queries, by, "xy") for by in SHIFTS]
     all_pairs = [pairs] + [plane_shift(pairs, by, "yx") for by in SHIFTS]
-    parts = [attend(queries, all_pairs)]
-    for by in SHIFTS:
-        arrived, parts[0] = lax.optimization_barrier((plane_shift(queries, by, "xy"), parts[0]))
-        part = attend(arrived, all_pairs)
-        parts.append(plane_shift(part, -by, "xy"))
+    parts = [attend(q, all_pairs) for q in all_queries]
+    parts[1:] = [plane_shift(p, -by, "xy") for p, by in zip(parts[1:], SHIFTS)]
     send = pl.pallas_call(
         combine_kernel,
         out_shape=shape(CORE * Z, HEADS, ROWS, HD),

time: 104 us -> 97.5 us (0.938)
  starting transfers between devices: 40.4 us -> 36.2 us
  waiting for transfers between devices: 39.2 us -> 38 us
    ppermute x9, starting transfers between devices: 17.8 us -> 13.5 us  [plane_shift(): return lax.ppermute(array, ('x', 'y', 'core'), pairs)]
    ppermute x9, waiting for transfers between devices: 15.9 us -> 14.7 us  [plane_shift(): return lax.ppermute(array, ('x', 'y', 'core'), pairs)]
  transfers between devices with their start and end apart: 15 -> 15, of which waited for: 8 -> 8; matrix products, arithmetic and copies ran while one was open for 0% -> 1% of each run, Pallas kernels for 9% -> 12%
where the time goes in v3:
time: 97.5 us; the launch traced here: 96.3 us
  waiting for transfers between devices  38 us (39%)
  starting transfers between devices  36.2 us (37%)
  Pallas kernels  19 us (19%)
  between operations  1.46 us (1%)
  local copies, waits for them, and re-layouts  1.1 us (1%)
    ppermute x9, waiting for transfers between devices, plane_shift(): return lax.ppermute(array, ('x', 'y', 'core'), pairs)  14.7 us
    ppermute x9, starting transfers between devices, plane_shift(): return lax.ppermute(array, ('x', 'y', 'core'), pairs)  13.5 us
    ppermute x1, waiting for transfers between devices, on_device(): guide_half = lax.ppermute(guide_send, halves, [(0, 2), (2, 0)])  12.5 us
    pallas_call x4, Pallas kernels, attend(): pl.pallas_call(attend_kernel, out_shape=shape(rows + STAT, HD), in_specs=...  12 us
    all_to_all x1, waiting for transfers between devices, on_device(): lax.all_to_all(send, ('core', 'zh', 'zl'), split_axis=0, concat_axis=0, t...  8.65 us
    all_to_all x1, starting transfers between devices, on_device(): lax.all_to_all(send, ('zh', 'zl'), split_axis=0, concat_axis=0, tiled=True)  8.61 us
    ppermute x1, starting transfers between devices, on_device(): guide_half = lax.ppermute(guide_send, halves, [(0, 2), (2, 0)])  7.82 us
    all_to_all x1, starting transfers between devices, on_device(): lax.all_to_all(send, ('core', 'zh', 'zl'), split_axis=0, concat_axis=0, t...  3.66 us
  transfers between devices with their start and end apart: 15, of which 8 were waited for; matrix products, arithmetic and copies ran while one was open for 1% of the time, Pallas kernels for 12%

profile of v3, /device:TPU:24, one launch (start us, length us, event | category | flops | bytes accessed | tf_op | source)
XLA Modules:
  0.0 96.3 jit_solution(16993173968469345629)
XLA Ops:
  0.6 0.6 pad_add_fusion.place
  1.2 2.7 %pack.1 = (bf16[8,9,32,128]{3,2,1,0:T(8,128)(2,1)}, bf16[3,128,128]{2,1,0:T(8,128)(2,1)}, bf16[3,128,128]{2,1,0:T(8,128)(2,1)}) custom-call(s32[2]{0:T(128)} %pad_add_fusion.place, bf16[1,32,2560]{2,1,0:T(8,128)(2,1)} %mq.1, bf16[1,32,2560]{2,1,0:T(8,128)(2,1)} %mk.1, bf16[1,32,2560]{2,1,0:T(8,128)(2,1)} %mv.1, bf16[1,128,256]{2,1,0:T(8,128)(2,1)} %gq.1, ...), custom_call_target="tpu_custom_call" | custom-call | tf_op jit(solution)/shard_map/pack/pallas_call | solution.py:306
  4.0 8.6 %all-to-all-start = ((bf16[8,9,32,128]{3,2,1,0:T(8,128)(2,1)}), bf16[8,9,32,128]{3,2,1,0:T(8,128)(2,1)S(1)}, u32[]{:S(2)}, u32[]{:S(2)}) async-start(bf16[8,9,32,128]{3,2,1,0:T(8,128)(2,1)} %get-tuple-element.11), calls=%async_computation | async-start | bytes 1179648 | tf_op jit(solution)/shard_map/all_to_all | solution.py:323
  12.6 1.3 %collective-permute-start = (bf16[3,128,128]{2,1,0:T(8,128)(2,1)S(1)}, bf16[3,128,128]{2,1,0:T(8,128)(2,1)S(1)}, u32[]{:S(2)}, u32[]{:S(2)}) collective-permute-start(bf16[3,128,128]{2,1,0:T(8,128)(2,1)S(1)} %copy-done.2), channel_id=1, source_target_pairs={{1,0},{3,2},{5,4},{7,6},{9,8},{11,10},{13,12},{15,14},{17,16},{19,... | collective-permute-start | bytes 294920 | tf_op jit(solution)/shard_map/ppermute | solution.py:320
  13.9 7.8 %collective-permute-start.1 = (bf16[3,128,128]{2,1,0:T(8,128)(2,1)S(1)}, bf16[3,128,128]{2,1,0:T(8,128)(2,1)S(1)}, u32[]{:S(2)}, u32[]{:S(2)}) collective-permute-start(bf16[3,128,128]{2,1,0:T(8,128)(2,1)S(1)} %copy-done.7), channel_id=1, source_target_pairs={{0,2},{2,0},{4,6},{6,4},{8,10},{10,8},{12,14},{14,12},{16,18},{18,... | collective-permute-start | bytes 294920 | tf_op jit(solution)/shard_map/ppermute | solution.py:321
  21.8 1.3 %collective-permute-start.2 = (bf16[3,128,128]{2,1,0:T(8,128)(2,1)S(1)}, bf16[3,128,128]{2,1,0:T(8,128)(2,1)S(1)}, u32[]{:S(2)}, u32[]{:S(2)}) collective-permute-start(bf16[3,128,128]{2,1,0:T(8,128)(2,1)S(1)} %copy-done.7), channel_id=1, source_target_pairs={{1,2},{3,0},{5,6},{7,4},{9,10},{11,8},{13,14},{15,12},{17,18},{19,... | collective-permute-start | bytes 294920 | tf_op jit(solution)/shard_map/ppermute | solution.py:322
  23.1 12.5 %collective-permute-done.1.guide_half = bf16[3,128,128]{2,1,0:T(8,128)(2,1)S(1)} collective-permute-done((bf16[3,128,128]{2,1,0:T(8,128)(2,1)S(1)}, bf16[3,128,128]{2,1,0:T(8,128)(2,1)S(1)}, u32[]{:S(2)}, u32[]{:S(2)}) %collective-permute-start.1) | collective-permute-done | bytes 98336 | tf_op jit(solution)/shard_map/ppermute | solution.py:321
  35.5 0.2 collective-permute-done.2.guide_across
  35.7 2.0 %collective-permute-done.3.sibling = bf16[8,9,32,128]{3,2,1,0:T(8,128)(2,1)S(1)} collective-permute-done((bf16[8,9,32,128]{3,2,1,0:T(8,128)(2,1)S(1)}, bf16[8,9,32,128]{3,2,1,0:T(8,128)(2,1)S(1)}, u32[]{:S(2)}, u32[]{:S(2)}) %collective-permute-start.3) | collective-permute-done | bytes 589856 | tf_op jit(solution)/shard_map/ppermute | solution.py:327
  37.7 0.6 unpack.1
  38.4 1.3 %collective-permute-start.4 = (bf16[4,512,128]{2,1,0:T(8,128)(2,1)S(1)}, bf16[4,512,128]{2,1,0:T(8,128)(2,1)S(1)}, u32[]{:S(2)}, u32[]{:S(2)}) collective-permute-start(bf16[4,512,128]{2,1,0:T(8,128)(2,1)S(1)} %get-tuple-element.19.refs_0_), channel_id=1, source_target_pairs={{0,8},{1,33},{4,12},{5,37},{8,0},{9,41},{12,4},{13,45},{16,24},{17... | collective-permute-start | bytes 1572872 | tf_op jit(solution)/shard_map/ppermute | solution.py:261
  39.7 2.2 %collective-permute-start.5 = (bf16[4,512,128]{2,1,0:T(8,128)(2,1)S(1)}, bf16[4,512,128]{2,1,0:T(8,128)(2,1)S(1)}, u32[]{:S(2)}, u32[]{:S(2)}) collective-permute-start(bf16[4,512,128]{2,1,0:T(8,128)(2,1)S(1)} %get-tuple-element.19.refs_0_), channel_id=1, source_target_pairs={{0,4},{1,17},{4,8},{5,21},{8,12},{9,25},{12,0},{13,29},{16,20},{17... | collective-permute-start | bytes 1572872 | tf_op jit(solution)/shard_map/ppermute | solution.py:261
  41.9 2.8 %collective-permute-start.11 = (bf16[1024,128]{1,0:T(8,128)(2,1)S(1)}, bf16[1024,128]{1,0:T(8,128)(2,1)S(1)}, u32[]{:S(2)}, u32[]{:S(2)}) collective-permute-start(bf16[1024,128]{1,0:T(8,128)(2,1)S(1)} %get-tuple-element.18.queries), channel_id=1, source_target_pairs={{0,48},{1,13},{4,52},{5,1},{8,56},{9,5},{12,60},{13,9},{16,0},{17,... | collective-permute-start | bytes 786440 | tf_op jit(solution)/shard_map/ppermute | solution.py:261
  44.6 9.0 %collective-permute-done.11.queries = bf16[1024,128]{1,0:T(8,128)(2,1)S(1)} collective-permute-done((bf16[1024,128]{1,0:T(8,128)(2,1)S(1)}, bf16[1024,128]{1,0:T(8,128)(2,1)S(1)}, u32[]{:S(2)}, u32[]{:S(2)}) %collective-permute-start.11) | collective-permute-done | bytes 262176 | tf_op jit(solution)/shard_map/ppermute | solution.py:261
  53.6 1.5 %collective-permute-start.7 = (bf16[1024,128]{1,0:T(8,128)(2,1)S(1)}, bf16[1024,128]{1,0:T(8,128)(2,1)S(1)}, u32[]{:S(2)}, u32[]{:S(2)}) collective-permute-start(bf16[1024,128]{1,0:T(8,128)(2,1)S(1)} %get-tuple-element.18.queries), channel_id=1, source_target_pairs={{0,32},{1,9},{4,36},{5,13},{8,40},{9,1},{12,44},{13,5},{16,48},{17... | collective-permute-start | bytes 786440 | tf_op jit(solution)/shard_map/ppermute | solution.py:261
  55.1 0.1 collective-permute-done.5.refs_2_
  55.2 2.6 %collective-permute-done.6.refs_3_ = bf16[4,512,128]{2,1,0:T(8,128)(2,1)S(1)} collective-permute-done((bf16[4,512,128]{2,1,0:T(8,128)(2,1)S(1)}, bf16[4,512,128]{2,1,0:T(8,128)(2,1)S(1)}, u32[]{:S(2)}, u32[]{:S(2)}) %collective-permute-start.6) | collective-permute-done | bytes 524320 | tf_op jit(solution)/shard_map/ppermute | solution.py:261
  57.7 3.0 %attend.7 = bf16[1056,128]{1,0:T(8,128)(2,1)S(1)} custom-call(bf16[1024,128]{1,0:T(8,128)(2,1)S(1)} %collective-permute-done.11.queries, bf16[4,512,128]{2,1,0:T(8,128)(2,1)S(1)} %get-tuple-element.19.refs_0_, bf16[4,512,128]{2,1,0:T(8,128)(2,1)S(1)} %collective-permute-done.4.refs_1_, bf16[4,512,128]{2,1,0:T(8,128)(2,1)S(1)} %collective-permute-done.5.refs_2_, ...), custom_call_target="tpu_custom_call" | custom-call | flops 1073741824 | bytes 2097152 | tf_op jit(solution)/shard_map/attend/pallas_call | solution.py:269
  60.7 2.2 %collective-permute-start.12 = (bf16[1056,128]{1,0:T(8,128)(2,1)S(1)}, bf16[1056,128]{1,0:T(8,128)(2,1)S(1)}, u32[]{:S(2)}, u32[]{:S(2)}) collective-permute-start(bf16[1056,128]{1,0:T(8,128)(2,1)S(1)} %attend.7), channel_id=1, source_target_pairs={{0,16},{1,5},{4,20},{5,9},{8,24},{9,13},{12,28},{13,1},{16,32},{17... | collective-permute-start | bytes 811016 | tf_op jit(solution)/shard_map/ppermute | solution.py:261
  62.9 3.0 %attend.6 = bf16[1056,128]{1,0:T(8,128)(2,1)S(1)} custom-call(bf16[1024,128]{1,0:T(8,128)(2,1)S(1)} %collective-permute-done.9.queries, bf16[4,512,128]{2,1,0:T(8,128)(2,1)S(1)} %get-tuple-element.19.refs_0_, bf16[4,512,128]{2,1,0:T(8,128)(2,1)S(1)} %collective-permute-done.4.refs_1_, bf16[4,512,128]{2,1,0:T(8,128)(2,1)S(1)} %collective-permute-done.5.refs_2_, ...), custom_call_target="tpu_custom_call" | custom-call | flops 1073741824 | bytes 2097152 | tf_op jit(solution)/shard_map/attend/pallas_call | solution.py:269
  65.9 1.5 %collective-permute-start.10 = (bf16[1056,128]{1,0:T(8,128)(2,1)S(1)}, bf16[1056,128]{1,0:T(8,128)(2,1)S(1)}, u32[]{:S(2)}, u32[]{:S(2)}) collective-permute-start(bf16[1056,128]{1,0:T(8,128)(2,1)S(1)} %attend.6), channel_id=1, source_target_pairs={{0,48},{1,13},{4,52},{5,1},{8,56},{9,5},{12,60},{13,9},{16,0},{17,... | collective-permute-start | bytes 811016 | tf_op jit(solution)/shard_map/ppermute | solution.py:261
  67.4 3.0 %attend.5 = bf16[1056,128]{1,0:T(8,128)(2,1)S(1)} custom-call(bf16[1024,128]{1,0:T(8,128)(2,1)S(1)} %collective-permute-done.7.queries, bf16[4,512,128]{2,1,0:T(8,128)(2,1)S(1)} %get-tuple-element.19.refs_0_, bf16[4,512,128]{2,1,0:T(8,128)(2,1)S(1)} %collective-permute-done.4.refs_1_, bf16[4,512,128]{2,1,0:T(8,128)(2,1)S(1)} %collective-permute-done.5.refs_2_, ...), custom_call_target="tpu_custom_call" | custom-call | flops 1073741824 | bytes 2097152 | tf_op jit(solution)/shard_map/attend/pallas_call | solution.py:269
  70.4 2.0 %collective-permute-start.8 = (bf16[1056,128]{1,0:T(8,128)(2,1)S(1)}, bf16[1056,128]{1,0:T(8,128)(2,1)S(1)}, u32[]{:S(2)}, u32[]{:S(2)}) collective-permute-start(bf16[1056,128]{1,0:T(8,128)(2,1)S(1)} %attend.5), channel_id=1, source_target_pairs={{0,32},{1,9},{4,36},{5,13},{8,40},{9,1},{12,44},{13,5},{16,48},{17... | collective-permute-start | bytes 811016 | tf_op jit(solution)/shard_map/ppermute | solution.py:261
  72.5 3.0 %attend.4.refs_0_ = bf16[1056,128]{1,0:T(8,128)(2,1)S(1)} custom-call(bf16[1024,128]{1,0:T(8,128)(2,1)S(1)} %get-tuple-element.18.queries, bf16[4,512,128]{2,1,0:T(8,128)(2,1)S(1)} %get-tuple-element.19.refs_0_, bf16[4,512,128]{2,1,0:T(8,128)(2,1)S(1)} %collective-permute-done.4.refs_1_, bf16[4,512,128]{2,1,0:T(8,128)(2,1)S(1)} %collective-permute-done.5.refs_2_, ...), custom_call_target="tpu_custom_call" | custom-call | flops 1073741824 | bytes 2097152 | tf_op jit(solution)/shard_map/attend/pallas_call | solution.py:269
  75.5 3.0 %collective-permute-done.8.refs_1_ = bf16[1056,128]{1,0:T(8,128)(2,1)S(1)} collective-permute-done((bf16[1056,128]{1,0:T(8,128)(2,1)S(1)}, bf16[1056,128]{1,0:T(8,128)(2,1)S(1)}, u32[]{:S(2)}, u32[]{:S(2)}) %collective-permute-start.8) | collective-permute-done | bytes 270368 | tf_op jit(solution)/shard_map/ppermute | solution.py:261
  78.5 2.0 %combine.1 = bf16[16,2,32,128]{3,2,1,0:T(8,128)(2,1)} custom-call(s32[2]{0:T(128)S(1)} %copy-done.4, bf16[1056,128]{1,0:T(8,128)(2,1)S(1)} %attend.4.refs_0_, bf16[1056,128]{1,0:T(8,128)(2,1)S(1)} %collective-permute-done.8.refs_1_, bf16[1056,128]{1,0:T(8,128)(2,1)S(1)} %collective-permute-done.10.refs_2_, bf16[1056,128]{1,0:T(8,128)(2,1)S(1)} %collective-permute-done.12.refs_3_), custom_call_target="tpu_custom_call" | custom-call | tf_op jit(solution)/shard_map/combine/pallas_call | solution.py:340
  80.5 3.7 %all-to-all-start.1 = ((bf16[16,2,32,128]{3,2,1,0:T(8,128)(2,1)}), bf16[16,2,32,128]{3,2,1,0:T(8,128)(2,1)S(1)}, u32[]{:S(2)}, u32[]{:S(2)}) async-start(bf16[16,2,32,128]{3,2,1,0:T(8,128)(2,1)} %combine.1), calls=%async_computation.1 | async-start | bytes 524288 | tf_op jit(solution)/shard_map/all_to_all | solution.py:348
  84.2 0.3 copy.14.main_head
  84.6 0.6 copy-done.6
  85.1 0.2 copy.15.guide_head
  86.0 8.6 %all-to-all-done.1.got = bf16[16,2,32,128]{3,2,1,0:T(8,128)(2,1)S(1)} async-done(((bf16[16,2,32,128]{3,2,1,0:T(8,128)(2,1)}), bf16[16,2,32,128]{3,2,1,0:T(8,128)(2,1)S(1)}, u32[]{:S(2)}, u32[]{:S(2)}) %all-to-all-start.1) | async-done | bytes 262176 | tf_op jit(solution)/shard_map/all_to_all | solution.py:348
  94.6 1.7 %final.1 = (f32[1,32,64]{2,1,0:T(8,128)}, f32[1,32,64]{2,1,0:T(8,128)}) custom-call(s32[1]{0:T(128)S(6)} %copy.16.step, s32[2]{0:T(128)S(1)} %copy-done.4, bf16[16,2,32,128]{3,2,1,0:T(8,128)(2,1)S(1)} %all-to-all-done.1.got, f32[1,32,64]{2,1,0:T(8,128)S(1)} %copy-done.3, bf16[50,2,2560]{2,1,0:T(2,128)(2,1)S(1)} %copy-done, ...), custom_call_target="tpu_custom_call" | custom-call | tf_op jit(solution)/shard_map/final/pallas_call | solution.py:352
  (25 shorter events, 0.1 us)
Async XLA Ops:
  4.0 8.6 %copy-start.2 = (bf16[3,128,128]{2,1,0:T(8,128)(2,1)S(1)}, bf16[3,128,128]{2,1,0:T(8,128)(2,1)}, u32[]{:S(2)}) copy-start(bf16[3,128,128]{2,1,0:T(8,128)(2,1)} %get-tuple-element.12.guide_own) | copy-start | bytes 294916
  4.0 9.9 %copy-start.7 = (bf16[3,128,128]{2,1,0:T(8,128)(2,1)S(1)}, bf16[3,128,128]{2,1,0:T(8,128)(2,1)}, u32[]{:S(2)}) copy-start(bf16[3,128,128]{2,1,0:T(8,128)(2,1)} %get-tuple-element.13) | copy-start | bytes 294916
  4.0 31.7 %all-to-all-start = ((bf16[8,9,32,128]{3,2,1,0:T(8,128)(2,1)}), bf16[8,9,32,128]{3,2,1,0:T(8,128)(2,1)S(1)}, u32[]{:S(2)}, u32[]{:S(2)}) async-start(bf16[8,9,32,128]{3,2,1,0:T(8,128)(2,1)} %get-tuple-element.11), calls=%async_computation | async-start | bytes 1179648 | tf_op jit(solution)/shard_map/all_to_all | solution.py:323
  12.6 25.1 %copy-start.4 = (s32[2]{0:T(128)S(1)}, s32[2]{0:T(128)}, u32[]{:S(2)}) copy-start(s32[2]{0:T(128)} %pad_add_fusion.place) | copy-start | bytes 28
  12.6 10.4 %collective-permute-start = (bf16[3,128,128]{2,1,0:T(8,128)(2,1)S(1)}, bf16[3,128,128]{2,1,0:T(8,128)(2,1)S(1)}, u32[]{:S(2)}, u32[]{:S(2)}) collective-permute-start(bf16[3,128,128]{2,1,0:T(8,128)(2,1)S(1)} %copy-done.2), channel_id=1, source_target_pairs={{1,0},{3,2},{5,4},{7,6},{9,8},{11,10},{13,12},{15,14},{17,16},{19,... | collective-permute-start | bytes 294920 | tf_op jit(solution)/shard_map/ppermute | solution.py:320
  13.9 21.6 %collective-permute-start.1 = (bf16[3,128,128]{2,1,0:T(8,128)(2,1)S(1)}, bf16[3,128,128]{2,1,0:T(8,128)(2,1)S(1)}, u32[]{:S(2)}, u32[]{:S(2)}) collective-permute-start(bf16[3,128,128]{2,1,0:T(8,128)(2,1)S(1)} %copy-done.7), channel_id=1, source_target_pairs={{0,2},{2,0},{4,6},{6,4},{8,10},{10,8},{12,14},{14,12},{16,18},{18,... | collective-permute-start | bytes 294920 | tf_op jit(solution)/shard_map/ppermute | solution.py:321
  21.8 14.0 %collective-permute-start.2 = (bf16[3,128,128]{2,1,0:T(8,128)(2,1)S(1)}, bf16[3,128,128]{2,1,0:T(8,128)(2,1)S(1)}, u32[]{:S(2)}, u32[]{:S(2)}) collective-permute-start(bf16[3,128,128]{2,1,0:T(8,128)(2,1)S(1)} %copy-done.7), channel_id=1, source_target_pairs={{1,2},{3,0},{5,6},{7,4},{9,10},{11,8},{13,14},{15,12},{17,18},{19,... | collective-permute-start | bytes 294920 | tf_op jit(solution)/shard_map/ppermute | solution.py:322
  35.7 2.0 %collective-permute-start.3 = (bf16[8,9,32,128]{3,2,1,0:T(8,128)(2,1)S(1)}, bf16[8,9,32,128]{3,2,1,0:T(8,128)(2,1)S(1)}, u32[]{:S(2)}, u32[]{:S(2)}) collective-permute-start(bf16[8,9,32,128]{3,2,1,0:T(8,128)(2,1)S(1)} %all-to-all-done.got), channel_id=1, source_target_pairs={{0,1},{1,0},{2,3},{3,2},{4,5},{5,4},{6,7},{7,6},{8,9},{9,8},{10,11... | collective-permute-start | bytes 1769480 | tf_op jit(solution)/shard_map/ppermute | solution.py:327
  38.4 16.7 %collective-permute-start.4 = (bf16[4,512,128]{2,1,0:T(8,128)(2,1)S(1)}, bf16[4,512,128]{2,1,0:T(8,128)(2,1)S(1)}, u32[]{:S(2)}, u32[]{:S(2)}) collective-permute-start(bf16[4,512,128]{2,1,0:T(8,128)(2,1)S(1)} %get-tuple-element.19.refs_0_), channel_id=1, source_target_pairs={{0,8},{1,33},{4,12},{5,37},{8,0},{9,41},{12,4},{13,45},{16,24},{17... | collective-permute-start | bytes 1572872 | tf_op jit(solution)/shard_map/ppermute | solution.py:261
  39.7 15.5 %collective-permute-start.5 = (bf16[4,512,128]{2,1,0:T(8,128)(2,1)S(1)}, bf16[4,512,128]{2,1,0:T(8,128)(2,1)S(1)}, u32[]{:S(2)}, u32[]{:S(2)}) collective-permute-start(bf16[4,512,128]{2,1,0:T(8,128)(2,1)S(1)} %get-tuple-element.19.refs_0_), channel_id=1, source_target_pairs={{0,4},{1,17},{4,8},{5,21},{8,12},{9,25},{12,0},{13,29},{16,20},{17... | collective-permute-start | bytes 1572872 | tf_op jit(solution)/shard_map/ppermute | solution.py:261
  41.9 15.8 %collective-permute-start.6 = (bf16[4,512,128]{2,1,0:T(8,128)(2,1)S(1)}, bf16[4,512,128]{2,1,0:T(8,128)(2,1)S(1)}, u32[]{:S(2)}, u32[]{:S(2)}) collective-permute-start(bf16[4,512,128]{2,1,0:T(8,128)(2,1)S(1)} %get-tuple-element.19.refs_0_), channel_id=1, source_target_pairs={{0,12},{1,49},{4,0},{5,53},{8,4},{9,57},{12,8},{13,61},{16,28},{17... | collective-permute-start | bytes 1572872 | tf_op jit(solution)/shard_map/ppermute | solution.py:261
  41.9 11.8 %collective-permute-start.11 = (bf16[1024,128]{1,0:T(8,128)(2,1)S(1)}, bf16[1024,128]{1,0:T(8,128)(2,1)S(1)}, u32[]{:S(2)}, u32[]{:S(2)}) collective-permute-start(bf16[1024,128]{1,0:T(8,128)(2,1)S(1)} %get-tuple-element.18.queries), channel_id=1, source_target_pairs={{0,48},{1,13},{4,52},{5,1},{8,56},{9,5},{12,60},{13,9},{16,0},{17,... | collective-permute-start | bytes 786440 | tf_op jit(solution)/shard_map/ppermute | solution.py:261
  44.6 18.3 %collective-permute-start.9 = (bf16[1024,128]{1,0:T(8,128)(2,1)S(1)}, bf16[1024,128]{1,0:T(8,128)(2,1)S(1)}, u32[]{:S(2)}, u32[]{:S(2)}) collective-permute-start(bf16[1024,128]{1,0:T(8,128)(2,1)S(1)} %get-tuple-element.18.queries), channel_id=1, source_target_pairs={{0,16},{1,5},{4,20},{5,9},{8,24},{9,13},{12,28},{13,1},{16,32},{17... | collective-permute-start | bytes 786440 | tf_op jit(solution)/shard_map/ppermute | solution.py:261
  53.6 13.8 %collective-permute-start.7 = (bf16[1024,128]{1,0:T(8,128)(2,1)S(1)}, bf16[1024,128]{1,0:T(8,128)(2,1)S(1)}, u32[]{:S(2)}, u32[]{:S(2)}) collective-permute-start(bf16[1024,128]{1,0:T(8,128)(2,1)S(1)} %get-tuple-element.18.queries), channel_id=1, source_target_pairs={{0,32},{1,9},{4,36},{5,13},{8,40},{9,1},{12,44},{13,5},{16,48},{17... | collective-permute-start | bytes 786440 | tf_op jit(solution)/shard_map/ppermute | solution.py:261
  60.7 14.7 %collective-permute-start.12 = (bf16[1056,128]{1,0:T(8,128)(2,1)S(1)}, bf16[1056,128]{1,0:T(8,128)(2,1)S(1)}, u32[]{:S(2)}, u32[]{:S(2)}) collective-permute-start(bf16[1056,128]{1,0:T(8,128)(2,1)S(1)} %attend.7), channel_id=1, source_target_pairs={{0,16},{1,5},{4,20},{5,9},{8,24},{9,13},{12,28},{13,1},{16,32},{17... | collective-permute-start | bytes 811016 | tf_op jit(solution)/shard_map/ppermute | solution.py:261
  65.9 9.5 %collective-permute-start.10 = (bf16[1056,128]{1,0:T(8,128)(2,1)S(1)}, bf16[1056,128]{1,0:T(8,128)(2,1)S(1)}, u32[]{:S(2)}, u32[]{:S(2)}) collective-permute-start(bf16[1056,128]{1,0:T(8,128)(2,1)S(1)} %attend.6), channel_id=1, source_target_pairs={{0,48},{1,13},{4,52},{5,1},{8,56},{9,5},{12,60},{13,9},{16,0},{17,... | collective-permute-start | bytes 811016 | tf_op jit(solution)/shard_map/ppermute | solution.py:261
  70.4 8.0 %collective-permute-start.8 = (bf16[1056,128]{1,0:T(8,128)(2,1)S(1)}, bf16[1056,128]{1,0:T(8,128)(2,1)S(1)}, u32[]{:S(2)}, u32[]{:S(2)}) collective-permute-start(bf16[1056,128]{1,0:T(8,128)(2,1)S(1)} %attend.5), channel_id=1, source_target_pairs={{0,32},{1,9},{4,36},{5,13},{8,40},{9,1},{12,44},{13,5},{16,48},{17... | collective-permute-start | bytes 811016 | tf_op jit(solution)/shard_map/ppermute | solution.py:261
  80.5 3.7 %copy-start.5 = (bf16[2560,64]{0,1:T(8,128)(2,1)S(1)}, bf16[2560,64]{0,1:T(8,128)(2,1)}, u32[]{:S(2)}) copy-start(bf16[2560,64]{0,1:T(8,128)(2,1)} %param.22) | copy-start | bytes 983044
  80.5 14.1 %all-to-all-start.1 = ((bf16[16,2,32,128]{3,2,1,0:T(8,128)(2,1)}), bf16[16,2,32,128]{3,2,1,0:T(8,128)(2,1)S(1)}, u32[]{:S(2)}, u32[]{:S(2)}) async-start(bf16[16,2,32,128]{3,2,1,0:T(8,128)(2,1)} %combine.1), calls=%async_computation.1 | async-start | bytes 524288 | tf_op jit(solution)/shard_map/all_to_all | solution.py:348
  84.2 0.9 copy-start.6
  84.2 10.4 %copy-start = (bf16[50,2,2560]{2,1,0:T(2,128)(2,1)S(1)}, bf16[50,2,2560]{2,1,0:T(2,128)(2,1)}, u32[]{:S(2)}) copy-start(bf16[50,2,2560]{2,1,0:T(2,128)(2,1)} %main_mod.1) | copy-start | bytes 1536004
  85.1 9.5 %copy-start.1 = (bf16[50,2,1024]{2,1,0:T(2,128)(2,1)S(1)}, bf16[50,2,1024]{2,1,0:T(2,128)(2,1)}, u32[]{:S(2)}) copy-start(bf16[50,2,1024]{2,1,0:T(2,128)(2,1)} %guide_mod.1) | copy-start | bytes 614404
  85.1 9.5 %copy-start.3 = (f32[1,32,64]{2,1,0:T(8,128)S(1)}, f32[1,32,64]{2,1,0:T(8,128)}, u32[]{:S(2)}) copy-start(f32[1,32,64]{2,1,0:T(8,128)} %latents.1) | copy-start | bytes 24580

commit v4 on v3

--- a/solution.py
+++ b/solution.py
@@ -8,6 +8,7 @@
 from jax.sharding import Mesh, PartitionSpec as P
 
 HD = 128
+C = 64
 STEPS = 50
 ZL, X, Y, ZH, CORE = 4, 4, 4, 2, 2
 Z = ZL * ZH
@@ -41,29 +42,32 @@
     return pltpu.CompilerParams(vmem_limit_bytes=mib * 1024 * 1024)
 
 
-def pack_kernel(place, mq, mk, mv, gq, gk, gv, send, guide_send, guide_own, main, guide, sems):
-    zh = place[0]
+def pack_guide_kernel(place, gq, gk, gv, send, own, sems):
+    copies = []
+    for head, to in ((1 - place[0], send), (place[0], own)):
+        lanes = pl.ds(pl.multiple_of(head * HD, HD), HD)
+        for kind, ref in enumerate((gq, gk, gv)):
+            copy = pltpu.make_async_copy(ref.at[0, :, lanes], to.at[kind], sems.at[len(copies)])
+            copy.start()
+            copies.append(copy)
+    for copy in copies:
+        copy.wait()
+
+
+def pack_kernel(mq, mk, mv, send, main, sems):
     copies = []
     for kind, ref in enumerate((mq, mk, mv)):
-        copies.append(pltpu.make_async_copy(ref.at[0], main.at[kind], sems.at[kind]))
-    for kind, ref in enumerate((gq, gk, gv)):
-        copies.append(pltpu.make_async_copy(ref.at[0], guide.at[kind], sems.at[3 + kind]))
-    for copy in copies:
+        copy = pltpu.make_async_copy(ref.at[0], main.at[kind], sems.at[kind])
         copy.start()
-    for kind in range(3):
-        copies[kind].wait()
+        copies.append(copy)
+    for kind, copy in enumerate(copies):
+        copy.wait()
         for zh_to in range(ZH):
             for zl_to in range(ZL):
                 for slot in range(3):
                     head = zl_to * 5 + (4 if slot == 2 else 2 * zh_to + slot)
                     lanes = slice(head * HD, (head + 1) * HD)
                     send[zh_to * ZL + zl_to, slot * 3 + kind] = main[kind, :, lanes]
-    own = pl.ds(pl.multiple_of(zh * HD, HD), HD)
-    other = pl.ds(pl.multiple_of((1 - zh) * HD, HD), HD)
-    for kind in range(3):
-        copies[3 + kind].wait()
-        guide_own[kind] = guide[kind, :, own]
-        guide_send[kind] = guide[kind, :, other]
 
 
 def unpack_kernel(
@@ -161,8 +165,67 @@
     out[HEADS * TOKENS :, :] = block.astype(bf16)
 
 
-def combine_kernel(place, *refs):
+def terms(value):
+    high = value.astype(bf16)
+    low = (value - high.astype(f32)).astype(bf16)
+    return jnp.concatenate([high, low], axis=0)
+
+
+def term_dot(value, weight):
+    both = jnp.dot(terms(value), weight, preferred_element_type=f32)
+    return both[: value.shape[0]] + both[value.shape[0] :]
+
+
+def prepare_kernel(
+    step, place, main_mod, guide_mod, main_head, guide_head, weights, scales, means, shifts
+):
+    zh, core, zl = place[0], place[1], place[2]
+    first = pl.ds(pl.multiple_of((zl * 5 + 2 * zh + core) * HD, HD), HD)
+    shared = pl.ds(pl.multiple_of((zl * 5 + 4) * HD, HD), HD)
+    guide = pl.ds(pl.multiple_of((zl * 2 + zh) * HD, HD), HD)
+    weights[0] = main_head[first, :]
+    scales[...] = jnp.zeros_like(scales)
+    scales[0:1, :] = 1.0 + main_mod[0, :, first][1:2].astype(f32)
+
+    @pl.when(core == 0)
+    def _():
+        weights[1] = guide_head[guide, :]
+        scales[1:2, :] = 1.0 + guide_mod[0, :, guide][1:2].astype(f32)
+
+    @pl.when(core == 1)
+    def _():
+        weights[1] = main_head[shared, :]
+        scales[1:2, :] = 1.0 + main_mod[0, :, shared][1:2].astype(f32)
+
+    def rows_of(table, order):
+        shift, scale = table[0, 0:1, :].astype(f32), 1.0 + table[0, 1:2, :].astype(f32)
+        owner = lax.broadcasted_iota(jnp.int32, scale.shape, 1) >> 7
+        rows = [jnp.where(owner == head, scale, 0.0) for head in order] + [shift]
+        rows += [jnp.zeros_like(shift)] * (-len(rows) % 8)
+        return jnp.concatenate(rows, axis=0)
+
+    main_order = [
+        zl * 5 + 2 * zh + core for core in range(CORE) for zh in range(ZH) for zl in range(ZL)
+    ] + [zl * 5 + 4 for zl in range(ZL)]
+    guide_order = [zl * 2 + zh for zh in range(ZH) for zl in range(ZL)]
+    main_rows = term_dot(rows_of(main_mod, main_order), main_head[...])
+    guide_rows = term_dot(rows_of(guide_mod, guide_order), guide_head[...])
+    main_rows = jnp.concatenate([main_rows, jnp.zeros_like(main_rows)], axis=1)
+    guide_rows = jnp.concatenate([jnp.zeros_like(guide_rows), guide_rows], axis=1)
+    means[...] = jnp.zeros_like(means)
+    for source in range(CORE * Z):
+        means[source * 8 : source * 8 + 1, :] = main_rows[source : source + 1]
+    for source in range(Z):
+        means[source * 8 + 4 : source * 8 + 5, :] = guide_rows[source : source + 1]
+        at = (Z + source) * 8 + 4
+        means[at : at + 1, :] = main_rows[2 * Z + source % ZL : 2 * Z + source % ZL + 1]
+    shifts[...] = jnp.zeros_like(shifts)
+    shifts[0:1, :] = main_rows[20:21] + guide_rows[8:9]
+
+
+def combine_kernel(place, weights, scales, *refs):
     parts, send = refs[:SIDE], refs[SIDE]
+    on_diagonal = diagonal()
     levels = []
     for part in parts:
         block = part[HEADS * TOKENS :, :].astype(f32)
@@ -174,46 +237,50 @@
     whole = shares[0] + shares[1] + shares[2] + shares[3]
     filler = jnp.zeros((HD - 8, HD), f32)
     shares = [jnp.transpose(jnp.concatenate([share / whole, filler], axis=0)) for share in shares]
-    results = []
-    for tile in range(HEADS * TOKENS // HD):
-        total = None
-        for part, share in zip(parts, shares):
-            column = share[:, tile : tile + 1]
-            term = part[tile * HD : (tile + 1) * HD, :].astype(f32) * column
-            total = term if total is None else total + term
-        results.append(total.astype(bf16))
-
-    def put(head, tiles):
-        for tile, result in enumerate(tiles):
+    blocks = TOKENS // HD
+    flows, stats = [], []
+    for head in range(HEADS):
+        merged = []
+        for tile in range(head * blocks, (head + 1) * blocks):
+            total = None
+            for part, share in zip(parts, shares):
+                column = share[:, tile : tile + 1]
+                term = part[tile * HD : (tile + 1) * HD, :].astype(f32) * column
+                total = term if total is None else total + term
+            merged.append(total)
+        attended = jnp.concatenate(merged, axis=0).astype(bf16).astype(f32)
+        mean = jnp.mean(attended, axis=1, keepdims=True)
+        centered = attended - mean
+        square = jnp.sum(centered * centered, axis=1, keepdims=True)
+        flow = term_dot(centered * scales[head : head + 1, :], weights[head]).astype(bf16)
+        for tile in range(blocks):
+            rows = slice(tile * HD, (tile + 1) * HD)
+            flows.append(flow[rows])
+            both = [
+                jnp.sum(jnp.where(on_diagonal, value[rows], 0.0), axis=0, keepdims=True)
+                for value in (mean, square)
+            ]
+            stats.append(terms(jnp.concatenate(both, axis=0)))
+
+    def put(pick):
+        for tile in range(TOKENS // HD):
+            other = pick(tile)
+            rows = jnp.concatenate([flows[tile], flows[other]], axis=1)
+            both = jnp.concatenate(
+                [stats[tile].astype(f32), stats[other].astype(f32), jnp.zeros((8, HD), f32)],
+                axis=0,
+            ).astype(bf16)
             for zl in range(ZL):
-                send[tile * ZL + zl, head] = result[zl * ROWS : (zl + 1) * ROWS, :]
-
-    blocks = TOKENS // HD
-    put(0, results[:blocks])
+                send[tile * ZL + zl, 0:ROWS, :] = rows[zl * ROWS : (zl + 1) * ROWS, :]
+                send[tile * ZL + zl, ROWS : ROWS + 16, :] = both
 
     @pl.when(place[1] == 0)
     def _():
-        put(1, results[blocks:])
+        put(lambda tile: blocks + tile)
 
     @pl.when(place[1] == 1)
     def _():
-        put(1, [results[blocks + tile // ZH] for tile in range(blocks)])
-
-
-def flow_of(heads, table, weight):
-    width = len(heads) * HD
-    center = jnp.sum(sum(heads), axis=1, keepdims=True) / width
-    centered = [h - center for h in heads]
-    spread = jnp.sum(sum(h * h for h in centered), axis=1, keepdims=True) / width
-    shrink = lax.rsqrt(spread + epsilon)
-    shift, scale = table[0, 0:1, :].astype(f32), table[0, 1:2, :].astype(f32)
-    modulated = jnp.concatenate(centered, axis=1) * shrink * (1.0 + scale) + shift
-    high = modulated.astype(bf16)
-    low = (modulated - high.astype(f32)).astype(bf16)
-    both = jnp.dot(
-        jnp.concatenate([high, low], axis=0), weight[...], preferred_element_type=f32
-    )
-    return both[:ROWS] + both[ROWS:]
+        put(lambda tile: blocks + tile // ZH)
 
 
 def sigma_at(index):
@@ -221,27 +288,50 @@
     return flow_shift * remaining / (1.0 + (flow_shift - 1.0) * remaining)
 
 
-def final_kernel(
-    step,
-    place,
-    got,
-    latents,
-    main_mod,
-    guide_mod,
-    main_head,
-    guide_head,
-    velocity,
-    advanced,
-):
-    zh = place[0]
-    main, guide = [], []
-    for zl in range(ZL):
-        for zh_from in range(ZH):
-            main += [got[core * Z + zh_from * ZL + zl, 0] for core in range(CORE)]
-            guide += [got[zh_from * ZL + zl, 1]]
-        main += [got[Z + zh * ZL + zl, 1]]
-    main_flow = flow_of([h.astype(f32) for h in main], main_mod, main_head)
-    guide_flow = flow_of([h.astype(f32) for h in guide], guide_mod, guide_head)
+def final_kernel(step, place, got, means, shifts, latents, velocity, advanced, columns):
+    zh, zl = place[0], place[2]
+
+    def flows(source):
+        return got[source, 0:ROWS, :].astype(f32)
+
+    lower = sum(flows(source) for source in range(Z))
+    upper = sum(flows(Z + source) for source in range(Z))
+    shared = sum(flows(Z + zh * ZL + source) for source in range(ZL))
+    upper = upper[:, :C] + shared[:, C:]
+    total = lower + jnp.concatenate([upper, jnp.zeros((ROWS, C), f32)], axis=1)
+
+    table = []
+    for source in range(CORE * Z):
+        block = got[source, ROWS : ROWS + 16, :].astype(f32)[:8]
+        table.append(block + jnp.concatenate([block[2:], block[:2]], axis=0))
+    table = jnp.concatenate(table, axis=0)
+    row = lax.broadcasted_iota(jnp.int32, (HD, HD), 0)
+    kind, source = row & 7, row >> 3
+    second = (source >= Z + zh * ZL) & (source < Z + zh * ZL + ZL)
+
+    def gathered(count, of_mean, of_square):
+        mean = jnp.sum(jnp.where(of_mean, table, 0.0), axis=0, keepdims=True) / count
+        apart = jnp.where(of_mean, table - mean, 0.0)
+        spread = jnp.where(of_square, table, 0.0) + HD * (apart * apart)
+        spread = jnp.sum(spread, axis=0, keepdims=True) / (count * HD)
+        return apart, lax.rsqrt(spread + epsilon)
+
+    main, main_shrink = gathered(
+        20, (kind == 0) | ((kind == 4) & second), (kind == 1) | ((kind == 5) & second)
+    )
+    guide, guide_shrink = gathered(8, (kind == 4) & (source < Z), (kind == 5) & (source < Z))
+    block = main + guide
+    block = jnp.where(row == 2, main_shrink, jnp.where(row == 3, guide_shrink, block))
+    columns[...] = jnp.transpose(block)
+    mine = columns[pl.ds(pl.multiple_of(zl * ROWS, ROWS), ROWS), :]
+    lane = lax.broadcasted_iota(jnp.int32, (ROWS, HD), 1)
+    shrink = jnp.where(lane < C, mine[:, 2:3], mine[:, 3:4])
+    high = means[...].astype(bf16)
+    moved = term_dot(mine, high) + jnp.dot(
+        mine.astype(bf16), (means[...] - high.astype(f32)).astype(bf16), preferred_element_type=f32
+    )
+    flow = shrink * (total + moved) + shifts[0:1, :]
+    main_flow, guide_flow = flow[:, :C], flow[:, C:]
     result = guide_flow + guidance * (main_flow - guide_flow)
     now = jnp.full((1, 1), step[0], jnp.int32)
     velocity[0] = result
@@ -261,7 +351,7 @@
     return lax.ppermute(array, ("x", "y", "core"), pairs)
 
 
-SHIFTS = (2, 1, -1)
+SHIFTS = (-1, 1, 2)
 
 
 def attend(queries, pairs):
@@ -301,28 +391,61 @@
     main_head,
     guide_head,
 ):
-    zh, core = lax.axis_index("zh"), lax.axis_index("core")
-    place = jnp.stack([zh, core]).astype(jnp.int32)
-    send, guide_send, guide_own = pl.pallas_call(
+    place = jnp.stack([lax.axis_index(name) for name in ("zh", "core", "zl")]).astype(jnp.int32)
+    guide_send, guide_own = pl.pallas_call(
+        pack_guide_kernel,
+        out_shape=(shape(3, BLOCK, HD),) * 2,
+        in_specs=[SMEM] + [ANY] * 3,
+        out_specs=(VMEM,) * 2,
+        scratch_shapes=[pltpu.SemaphoreType.DMA((6,))],
+        compiler_params=params(16),
+        name="pack_guide",
+    )(place, guide_query, guide_key, guide_value)
+    send = pl.pallas_call(
         pack_kernel,
-        out_shape=(shape(Z, 9, ROWS, HD), shape(3, BLOCK, HD), shape(3, BLOCK, HD)),
-        in_specs=[SMEM] + [ANY] * 6,
-        out_specs=(VMEM,) * 3,
+        out_shape=shape(Z, 9, ROWS, HD),
+        in_specs=[ANY] * 3,
+        out_specs=VMEM,
         scratch_shapes=[
             pltpu.VMEM((3, ROWS, 20 * HD), bf16),
-            pltpu.VMEM((3, BLOCK, 2 * HD), bf16),
-            pltpu.SemaphoreType.DMA((6,)),
+            pltpu.SemaphoreType.DMA((3,)),
         ],
         compiler_params=params(60),
         name="pack",
-    )(place, main_query, main_key, main_value, guide_query, guide_key, guide_value)
+    )(main_query, main_key, main_value)
+    whole = lambda *dims: pl.BlockSpec(dims, lambda i, step, place: (0,) * len(dims))
+    row = lambda *dims: pl.BlockSpec(dims, lambda i, step, place: (step[0], 0, 0))
+    weights, scales, means, shifts = pl.pallas_call(
+        prepare_kernel,
+        out_shape=(
+            shape(HEADS, HD, C),
+            shape(8, HD, dtype=f32),
+            shape(HD, HD, dtype=f32),
+            shape(8, HD, dtype=f32),
+        ),
+        grid_spec=pltpu.PrefetchScalarGridSpec(
+            num_scalar_prefetch=2,
+            grid=(1,),
+            in_specs=[
+                row(1, 2, 20 * HD),
+                row(1, 2, 8 * HD),
+                whole(20 * HD, C),
+                whole(8 * HD, C),
+            ],
+            out_specs=[whole(HEADS, HD, C), whole(8, HD), whole(HD, HD), whole(8, HD)],
+        ),
+        compiler_params=params(16),
+        name="prepare",
+    )(step_index, place, main_mod, guide_mod, main_head, guide_head)
     halves = ("zh", "core")
     guide_core = lax.ppermute(guide_own, halves, [(1, 0), (3, 2)])
     guide_half = lax.ppermute(guide_send, halves, [(0, 2), (2, 0)])
     guide_across = lax.ppermute(guide_send, halves, [(1, 2), (3, 0)])
     got = lax.all_to_all(send, ("zh", "zl"), split_axis=0, concat_axis=0, tiled=True)
-    got, guide_core, guide_half, guide_across = lax.optimization_barrier(
-        (got, guide_core, guide_half, guide_across)
+    got, guide_core, guide_half, guide_across, weights, scales, means, shifts = (
+        lax.optimization_barrier(
+            (got, guide_core, guide_half, guide_across, weights, scales, means, shifts)
+        )
     )
     sibling = lax.ppermute(got, "core", [(0, 1), (1, 0)])
     queries, pairs = pl.pallas_call(
@@ -339,35 +462,22 @@
     parts[1:] = [plane_shift(p, -by, "xy") for p, by in zip(parts[1:], SHIFTS)]
     send = pl.pallas_call(
         combine_kernel,
-        out_shape=shape(CORE * Z, HEADS, ROWS, HD),
-        in_specs=[SMEM] + [VMEM] * SIDE,
+        out_shape=shape(CORE * Z, ROWS + 16, HD),
+        in_specs=[SMEM] + [VMEM] * (2 + SIDE),
         out_specs=VMEM,
         compiler_params=params(16),
         name="combine",
-    )(place, *parts)
+    )(place, weights, scales, *parts)
     got = lax.all_to_all(send, ("core", "zh", "zl"), split_axis=0, concat_axis=0, tiled=True)
-
-    whole = lambda *dims: pl.BlockSpec(dims, lambda i, step, place: (0,) * len(dims))
-    row = lambda *dims: pl.BlockSpec(dims, lambda i, step, place: (step[0], 0, 0))
     velocity, advanced = pl.pallas_call(
         final_kernel,
-        out_shape=(shape(1, ROWS, 64, dtype=f32),) * 2,
-        grid_spec=pltpu.PrefetchScalarGridSpec(
-            num_scalar_prefetch=2,
-            grid=(1,),
-            in_specs=[
-                whole(CORE * Z, HEADS, ROWS, HD),
-                whole(1, ROWS, 64),
-                row(1, 2, 20 * HD),
-                row(1, 2, 8 * HD),
-                whole(20 * HD, 64),
-                whole(8 * HD, 64),
-            ],
-            out_specs=[whole(1, ROWS, 64)] * 2,
-        ),
+        out_shape=(shape(1, ROWS, C, dtype=f32),) * 2,
+        in_specs=[SMEM] * 2 + [VMEM] * 4,
+        out_specs=(VMEM,) * 2,
+        scratch_shapes=[pltpu.VMEM((HD, HD), f32)],
         compiler_params=params(16),
         name="final",
-    )(step_index, place, got, latents, main_mod, guide_mod, main_head, guide_head)
+    )(step_index, place, got, means, shifts, latents)
     return velocity, advanced
 
 

time: 97.5 us -> 93.7 us (0.961)
  waiting for transfers between devices: 38 us -> 25.6 us
  blocking collectives: 0 us -> 11.8 us
  starting transfers between devices: 36.2 us -> 32.5 us
  Pallas kernels: 19 us -> 20 us
    ppermute x1, waiting for transfers between devices: 12.5 us -> 0.1 us  [on_device(): guide_half = lax.ppermute(guide_send, halves, [(0, 2), (2, 0)])]
    all_to_all x0 -> x1, blocking collectives: none -> 11.8 us  [on_device(): lax.all_to_all(send, ('core', 'zh', 'zl'), split_axis=0, concat_axis=0, t...]
    all_to_all x1 -> x0, waiting for transfers between devices: 8.65 us -> none  [on_device(): lax.all_to_all(send, ('core', 'zh', 'zl'), split_axis=0, concat_axis=0, t...]
    ppermute x1, waiting for transfers between devices: 0.19 us -> 8.82 us  [on_device(): guide_across = lax.ppermute(guide_send, halves, [(1, 2), (3, 0)])]
    all_to_all x1 -> x0, starting transfers between devices: 3.66 us -> none  [on_device(): lax.all_to_all(send, ('core', 'zh', 'zl'), split_axis=0, concat_axis=0, t...]
    pallas_call x3 -> x5, Pallas kernels: 6.43 us -> 7.38 us  [the longest x1 1.98 us: on_device(): pl.pallas_call(combine_kernel, out_shape=shape(CORE * Z, ROWS + 16, HD),...]
  transfers between devices with their start and end apart: 15 -> 14, of which waited for: 8 -> 7; matrix products, arithmetic and copies ran while one was open for 1% -> 1% of each run, Pallas kernels for 12% -> 15%
where the time goes in v4:
time: 93.7 us; the launch traced here: 92.6 us
  starting transfers between devices  32.5 us (35%)
  waiting for transfers between devices  25.6 us (27%)
  Pallas kernels  20 us (21%)
  blocking collectives  11.8 us (13%)
  between operations  1.46 us (2%)
  local copies, waits for them, and re-layouts  1.27 us (1%)
    ppermute x9, waiting for transfers between devices, plane_shift(): return lax.ppermute(array, ('x', 'y', 'core'), pairs)  14.7 us
    ppermute x9, starting transfers between devices, plane_shift(): return lax.ppermute(array, ('x', 'y', 'core'), pairs)  13.5 us
    pallas_call x4, Pallas kernels, attend(): pl.pallas_call(attend_kernel, out_shape=shape(rows + STAT, HD), in_specs=...  12 us
    all_to_all x1, blocking collectives, on_device(): lax.all_to_all(send, ('core', 'zh', 'zl'), split_axis=0, concat_axis=0, t...  11.8 us
    ppermute x1, waiting for transfers between devices, on_device(): guide_across = lax.ppermute(guide_send, halves, [(1, 2), (3, 0)])  8.82 us
    all_to_all x1, starting transfers between devices, on_device(): lax.all_to_all(send, ('zh', 'zl'), split_axis=0, concat_axis=0, tiled=True)  8.61 us
    ppermute x1, starting transfers between devices, on_device(): guide_half = lax.ppermute(guide_send, halves, [(0, 2), (2, 0)])  7.83 us
    ppermute x1, waiting for transfers between devices, on_device(): sibling = lax.ppermute(got, 'core', [(0, 1), (1, 0)])  2 us
  transfers between devices with their start and end apart: 14, of which 7 were waited for; matrix products, arithmetic and copies ran while one was open for 1% of the time, Pallas kernels for 15%

profile of v4, /device:TPU:24, one launch (start us, length us, event | category | flops | bytes accessed | tf_op | source)
XLA Modules:
  0.0 92.6 jit_solution(17738161354378129096)
XLA Ops:
  0.6 2.0 %pack.1 = bf16[8,9,32,128]{3,2,1,0:T(8,128)(2,1)} custom-call(bf16[1,32,2560]{2,1,0:T(8,128)(2,1)} %mq.1, bf16[1,32,2560]{2,1,0:T(8,128)(2,1)} %mk.1, bf16[1,32,2560]{2,1,0:T(8,128)(2,1)} %mv.1), custom_call_target="tpu_custom_call" | custom-call | tf_op jit(solution)/shard_map/pack/pallas_call | solution.py:404
  2.7 8.6 %all-to-all-start = ((bf16[8,9,32,128]{3,2,1,0:T(8,128)(2,1)}), bf16[8,9,32,128]{3,2,1,0:T(8,128)(2,1)S(1)}, u32[]{:S(2)}, u32[]{:S(2)}) async-start(bf16[8,9,32,128]{3,2,1,0:T(8,128)(2,1)} %pack.1), calls=%async_computation | async-start | bytes 1179648 | tf_op jit(solution)/shard_map/all_to_all | solution.py:444
  11.3 0.1 pad_add_fusion.place
  11.4 0.7 pack_guide.1
  12.0 1.3 %collective-permute-start = (bf16[3,128,128]{2,1,0:T(8,128)(2,1)S(1)}, bf16[3,128,128]{2,1,0:T(8,128)(2,1)S(1)}, u32[]{:S(2)}, u32[]{:S(2)}) collective-permute-start(bf16[3,128,128]{2,1,0:T(8,128)(2,1)S(1)} %get-tuple-element.18.guide_own), channel_id=1, source_target_pairs={{1,0},{3,2},{5,4},{7,6},{9,8},{11,10},{13,12},{15,14},{17,16},{19,... | collective-permute-start | bytes 294920 | tf_op jit(solution)/shard_map/ppermute | solution.py:441
  13.3 1.3 %collective-permute-start.2 = (bf16[3,128,128]{2,1,0:T(8,128)(2,1)S(1)}, bf16[3,128,128]{2,1,0:T(8,128)(2,1)S(1)}, u32[]{:S(2)}, u32[]{:S(2)}) collective-permute-start(bf16[3,128,128]{2,1,0:T(8,128)(2,1)S(1)} %get-tuple-element.19), channel_id=1, source_target_pairs={{1,2},{3,0},{5,6},{7,4},{9,10},{11,8},{13,14},{15,12},{17,18},{19,... | collective-permute-start | bytes 294920 | tf_op jit(solution)/shard_map/ppermute | solution.py:443
  14.6 7.8 %collective-permute-start.1 = (bf16[3,128,128]{2,1,0:T(8,128)(2,1)S(1)}, bf16[3,128,128]{2,1,0:T(8,128)(2,1)S(1)}, u32[]{:S(2)}, u32[]{:S(2)}) collective-permute-start(bf16[3,128,128]{2,1,0:T(8,128)(2,1)S(1)} %get-tuple-element.19), channel_id=1, source_target_pairs={{0,2},{2,0},{4,6},{6,4},{8,10},{10,8},{12,14},{14,12},{16,18},{18,... | collective-permute-start | bytes 294920 | tf_op jit(solution)/shard_map/ppermute | solution.py:442
  23.1 0.2 copy.15.guide_head
  23.3 0.3 copy.14.main_head
  23.7 0.7 copy-done
  24.4 1.1 %prepare.1 = (bf16[2,128,64]{2,1,0:T(8,128)(2,1)S(1)}, f32[8,128]{1,0:T(8,128)S(1)}, f32[128,128]{1,0:T(8,128)S(1)}, f32[8,128]{1,0:T(8,128)S(1)}) custom-call(s32[1]{0:T(128)S(6)} %copy.16.step, s32[3]{0:T(128)S(1)} %pad_add_fusion.place, bf16[50,2,2560]{2,1,0:T(2,128)(2,1)S(1)} %copy-done, bf16[50,2,1024]{2,1,0:T(2,128)(2,1)S(1)} %copy-done.1, ...), custom_call_target="tpu_custom_call" | custom-call | tf_op jit(solution)/shard_map/prepare/pallas_call | solution.py:418
  25.5 8.8 %collective-permute-done.2.guide_across = bf16[3,128,128]{2,1,0:T(8,128)(2,1)S(1)} collective-permute-done((bf16[3,128,128]{2,1,0:T(8,128)(2,1)S(1)}, bf16[3,128,128]{2,1,0:T(8,128)(2,1)S(1)}, u32[]{:S(2)}, u32[]{:S(2)}) %collective-permute-start.2) | collective-permute-done | bytes 98336 | tf_op jit(solution)/shard_map/ppermute | solution.py:443
  34.3 0.1 collective-permute-done.1.guide_half
  34.4 2.0 %collective-permute-done.3.sibling = bf16[8,9,32,128]{3,2,1,0:T(8,128)(2,1)S(1)} collective-permute-done((bf16[8,9,32,128]{3,2,1,0:T(8,128)(2,1)S(1)}, bf16[8,9,32,128]{3,2,1,0:T(8,128)(2,1)S(1)}, u32[]{:S(2)}, u32[]{:S(2)}) %collective-permute-start.3) | collective-permute-done | bytes 589856 | tf_op jit(solution)/shard_map/ppermute | solution.py:450
  36.4 0.6 unpack.1
  37.0 1.3 %collective-permute-start.6 = (bf16[4,512,128]{2,1,0:T(8,128)(2,1)S(1)}, bf16[4,512,128]{2,1,0:T(8,128)(2,1)S(1)}, u32[]{:S(2)}, u32[]{:S(2)}) collective-permute-start(bf16[4,512,128]{2,1,0:T(8,128)(2,1)S(1)} %get-tuple-element.31.refs_0_), channel_id=1, source_target_pairs={{0,8},{1,33},{4,12},{5,37},{8,0},{9,41},{12,4},{13,45},{16,24},{17... | collective-permute-start | bytes 1572872 | tf_op jit(solution)/shard_map/ppermute | solution.py:351
  38.3 2.2 %collective-permute-start.5 = (bf16[4,512,128]{2,1,0:T(8,128)(2,1)S(1)}, bf16[4,512,128]{2,1,0:T(8,128)(2,1)S(1)}, u32[]{:S(2)}, u32[]{:S(2)}) collective-permute-start(bf16[4,512,128]{2,1,0:T(8,128)(2,1)S(1)} %get-tuple-element.31.refs_0_), channel_id=1, source_target_pairs={{0,4},{1,17},{4,8},{5,21},{8,12},{9,25},{12,0},{13,29},{16,20},{17... | collective-permute-start | bytes 1572872 | tf_op jit(solution)/shard_map/ppermute | solution.py:351
  40.5 2.8 %collective-permute-start.7 = (bf16[1024,128]{1,0:T(8,128)(2,1)S(1)}, bf16[1024,128]{1,0:T(8,128)(2,1)S(1)}, u32[]{:S(2)}, u32[]{:S(2)}) collective-permute-start(bf16[1024,128]{1,0:T(8,128)(2,1)S(1)} %get-tuple-element.30.queries), channel_id=1, source_target_pairs={{0,48},{1,13},{4,52},{5,1},{8,56},{9,5},{12,60},{13,9},{16,0},{17,... | collective-permute-start | bytes 786440 | tf_op jit(solution)/shard_map/ppermute | solution.py:351
  43.3 9.0 %collective-permute-done.7.queries = bf16[1024,128]{1,0:T(8,128)(2,1)S(1)} collective-permute-done((bf16[1024,128]{1,0:T(8,128)(2,1)S(1)}, bf16[1024,128]{1,0:T(8,128)(2,1)S(1)}, u32[]{:S(2)}, u32[]{:S(2)}) %collective-permute-start.7) | collective-permute-done | bytes 262176 | tf_op jit(solution)/shard_map/ppermute | solution.py:351
  52.3 1.5 %collective-permute-start.11 = (bf16[1024,128]{1,0:T(8,128)(2,1)S(1)}, bf16[1024,128]{1,0:T(8,128)(2,1)S(1)}, u32[]{:S(2)}, u32[]{:S(2)}) collective-permute-start(bf16[1024,128]{1,0:T(8,128)(2,1)S(1)} %get-tuple-element.30.queries), channel_id=1, source_target_pairs={{0,32},{1,9},{4,36},{5,13},{8,40},{9,1},{12,44},{13,5},{16,48},{17... | collective-permute-start | bytes 786440 | tf_op jit(solution)/shard_map/ppermute | solution.py:351
  53.8 2.6 %collective-permute-done.4.refs_1_ = bf16[4,512,128]{2,1,0:T(8,128)(2,1)S(1)} collective-permute-done((bf16[4,512,128]{2,1,0:T(8,128)(2,1)S(1)}, bf16[4,512,128]{2,1,0:T(8,128)(2,1)S(1)}, u32[]{:S(2)}, u32[]{:S(2)}) %collective-permute-start.4) | collective-permute-done | bytes 524320 | tf_op jit(solution)/shard_map/ppermute | solution.py:351
  56.4 3.0 %attend.5 = bf16[1056,128]{1,0:T(8,128)(2,1)S(1)} custom-call(bf16[1024,128]{1,0:T(8,128)(2,1)S(1)} %collective-permute-done.7.queries, bf16[4,512,128]{2,1,0:T(8,128)(2,1)S(1)} %get-tuple-element.31.refs_0_, bf16[4,512,128]{2,1,0:T(8,128)(2,1)S(1)} %collective-permute-done.4.refs_1_, bf16[4,512,128]{2,1,0:T(8,128)(2,1)S(1)} %collective-permute-done.5.refs_2_, ...), custom_call_target="tpu_custom_call" | custom-call | flops 1073741824 | bytes 2097152 | tf_op jit(solution)/shard_map/attend/pallas_call | solution.py:359
  59.4 2.4 %collective-permute-start.8 = (bf16[1056,128]{1,0:T(8,128)(2,1)S(1)}, bf16[1056,128]{1,0:T(8,128)(2,1)S(1)}, u32[]{:S(2)}, u32[]{:S(2)}) collective-permute-start(bf16[1056,128]{1,0:T(8,128)(2,1)S(1)} %attend.5), channel_id=1, source_target_pairs={{0,16},{1,5},{4,20},{5,9},{8,24},{9,13},{12,28},{13,1},{16,32},{17... | collective-permute-start | bytes 811016 | tf_op jit(solution)/shard_map/ppermute | solution.py:351
  61.7 3.0 %attend.6 = bf16[1056,128]{1,0:T(8,128)(2,1)S(1)} custom-call(bf16[1024,128]{1,0:T(8,128)(2,1)S(1)} %collective-permute-done.9.queries, bf16[4,512,128]{2,1,0:T(8,128)(2,1)S(1)} %get-tuple-element.31.refs_0_, bf16[4,512,128]{2,1,0:T(8,128)(2,1)S(1)} %collective-permute-done.4.refs_1_, bf16[4,512,128]{2,1,0:T(8,128)(2,1)S(1)} %collective-permute-done.5.refs_2_, ...), custom_call_target="tpu_custom_call" | custom-call | flops 1073741824 | bytes 2097152 | tf_op jit(solution)/shard_map/attend/pallas_call | solution.py:359
  64.7 1.3 %collective-permute-start.10 = (bf16[1056,128]{1,0:T(8,128)(2,1)S(1)}, bf16[1056,128]{1,0:T(8,128)(2,1)S(1)}, u32[]{:S(2)}, u32[]{:S(2)}) collective-permute-start(bf16[1056,128]{1,0:T(8,128)(2,1)S(1)} %attend.6), channel_id=1, source_target_pairs={{0,48},{1,13},{4,52},{5,1},{8,56},{9,5},{12,60},{13,9},{16,0},{17,... | collective-permute-start | bytes 811016 | tf_op jit(solution)/shard_map/ppermute | solution.py:351
  66.1 3.0 %attend.7 = bf16[1056,128]{1,0:T(8,128)(2,1)S(1)} custom-call(bf16[1024,128]{1,0:T(8,128)(2,1)S(1)} %collective-permute-done.11.queries, bf16[4,512,128]{2,1,0:T(8,128)(2,1)S(1)} %get-tuple-element.31.refs_0_, bf16[4,512,128]{2,1,0:T(8,128)(2,1)S(1)} %collective-permute-done.4.refs_1_, bf16[4,512,128]{2,1,0:T(8,128)(2,1)S(1)} %collective-permute-done.5.refs_2_, ...), custom_call_target="tpu_custom_call" | custom-call | flops 1073741824 | bytes 2097152 | tf_op jit(solution)/shard_map/attend/pallas_call | solution.py:359
  69.1 2.0 %collective-permute-start.12 = (bf16[1056,128]{1,0:T(8,128)(2,1)S(1)}, bf16[1056,128]{1,0:T(8,128)(2,1)S(1)}, u32[]{:S(2)}, u32[]{:S(2)}) collective-permute-start(bf16[1056,128]{1,0:T(8,128)(2,1)S(1)} %attend.7), channel_id=1, source_target_pairs={{0,32},{1,9},{4,36},{5,13},{8,40},{9,1},{12,44},{13,5},{16,48},{17... | collective-permute-start | bytes 811016 | tf_op jit(solution)/shard_map/ppermute | solution.py:351
  71.1 3.0 %attend.4.refs_0_ = bf16[1056,128]{1,0:T(8,128)(2,1)S(1)} custom-call(bf16[1024,128]{1,0:T(8,128)(2,1)S(1)} %get-tuple-element.30.queries, bf16[4,512,128]{2,1,0:T(8,128)(2,1)S(1)} %get-tuple-element.31.refs_0_, bf16[4,512,128]{2,1,0:T(8,128)(2,1)S(1)} %collective-permute-done.4.refs_1_, bf16[4,512,128]{2,1,0:T(8,128)(2,1)S(1)} %collective-permute-done.5.refs_2_, ...), custom_call_target="tpu_custom_call" | custom-call | flops 1073741824 | bytes 2097152 | tf_op jit(solution)/shard_map/attend/pallas_call | solution.py:359
  74.1 3.0 %collective-permute-done.12.refs_3_ = bf16[1056,128]{1,0:T(8,128)(2,1)S(1)} collective-permute-done((bf16[1056,128]{1,0:T(8,128)(2,1)S(1)}, bf16[1056,128]{1,0:T(8,128)(2,1)S(1)}, u32[]{:S(2)}, u32[]{:S(2)}) %collective-permute-start.12) | collective-permute-done | bytes 270368 | tf_op jit(solution)/shard_map/ppermute | solution.py:351
  77.1 2.0 %combine.1 = bf16[16,48,128]{2,1,0:T(8,128)(2,1)S(1)} custom-call(s32[3]{0:T(128)S(1)} %pad_add_fusion.place, bf16[2,128,64]{2,1,0:T(8,128)(2,1)S(1)} %get-tuple-element.24.weights, f32[8,128]{1,0:T(8,128)S(1)} %get-tuple-element.25.scales, bf16[1056,128]{1,0:T(8,128)(2,1)S(1)} %attend.4.refs_0_, bf16[1056,128]{1,0:T(8,128)(2,1)S(1)} %collective-permute-done.8.refs_1_, ...), custom_call_target="tpu_custom_call" | custom-call | tf_op jit(solution)/shard_map/combine/pallas_call | solution.py:463
  79.1 11.8 %all_to_all.10.got = bf16[16,48,128]{2,1,0:T(8,128)(2,1)S(1)} all-to-all(bf16[16,48,128]{2,1,0:T(8,128)(2,1)S(1)} %combine.1), channel_id=1, replica_groups=mesh['zl'=4,'x'=4,'y'=4,'zh'=2,'core'=2] {'core','zh','zl'}, dimensions={0} | all-to-all | bytes 393216 | tf_op jit(solution)/shard_map/all_to_all | solution.py:471
  90.9 1.7 %final.1 = (f32[1,32,64]{2,1,0:T(8,128)}, f32[1,32,64]{2,1,0:T(8,128)}) custom-call(s32[1]{0:T(128)S(6)} %copy.16.step, s32[3]{0:T(128)S(1)} %pad_add_fusion.place, bf16[16,48,128]{2,1,0:T(8,128)(2,1)S(1)} %all_to_all.10.got, f32[128,128]{1,0:T(8,128)S(1)} %get-tuple-element.32.means, f32[8,128]{1,0:T(8,128)S(1)} %get-tuple-element.33.shifts, ...), custom_call_target="tpu_custom_call" | custom-call | tf_op jit(solution)/shard_map/final/pallas_call | solution.py:472
  (26 shorter events, 0.2 us)
Async XLA Ops:
  2.6 8.7 %copy-start.2 = (bf16[1,128,256]{2,1,0:T(8,128)(2,1)S(1)}, bf16[1,128,256]{2,1,0:T(8,128)(2,1)}, u32[]{:S(2)}) copy-start(bf16[1,128,256]{2,1,0:T(8,128)(2,1)} %gq.1) | copy-start | bytes 196612
  2.6 8.7 %copy-start.3 = (bf16[1,128,256]{2,1,0:T(8,128)(2,1)S(1)}, bf16[1,128,256]{2,1,0:T(8,128)(2,1)}, u32[]{:S(2)}) copy-start(bf16[1,128,256]{2,1,0:T(8,128)(2,1)} %gk.1) | copy-start | bytes 196612
  2.6 8.7 %copy-start.4 = (bf16[1,128,256]{2,1,0:T(8,128)(2,1)S(1)}, bf16[1,128,256]{2,1,0:T(8,128)(2,1)}, u32[]{:S(2)}) copy-start(bf16[1,128,256]{2,1,0:T(8,128)(2,1)} %gv.1) | copy-start | bytes 196612
  2.6 20.5 %copy-start.7 = (bf16[1024,64]{0,1:T(8,128)(2,1)S(1)}, bf16[1024,64]{0,1:T(8,128)(2,1)}, u32[]{:S(2)}) copy-start(bf16[1024,64]{0,1:T(8,128)(2,1)} %param.23) | copy-start | bytes 393220
  2.7 31.7 %all-to-all-start = ((bf16[8,9,32,128]{3,2,1,0:T(8,128)(2,1)}), bf16[8,9,32,128]{3,2,1,0:T(8,128)(2,1)S(1)}, u32[]{:S(2)}, u32[]{:S(2)}) async-start(bf16[8,9,32,128]{3,2,1,0:T(8,128)(2,1)} %pack.1), calls=%async_computation | async-start | bytes 1179648 | tf_op jit(solution)/shard_map/all_to_all | solution.py:444
  11.3 12.0 %copy-start.6 = (bf16[2560,64]{0,1:T(8,128)(2,1)S(1)}, bf16[2560,64]{0,1:T(8,128)(2,1)}, u32[]{:S(2)}) copy-start(bf16[2560,64]{0,1:T(8,128)(2,1)} %param.22) | copy-start | bytes 983044
  12.0 13.4 %collective-permute-start = (bf16[3,128,128]{2,1,0:T(8,128)(2,1)S(1)}, bf16[3,128,128]{2,1,0:T(8,128)(2,1)S(1)}, u32[]{:S(2)}, u32[]{:S(2)}) collective-permute-start(bf16[3,128,128]{2,1,0:T(8,128)(2,1)S(1)} %get-tuple-element.18.guide_own), channel_id=1, source_target_pairs={{1,0},{3,2},{5,4},{7,6},{9,8},{11,10},{13,12},{15,14},{17,16},{19,... | collective-permute-start | bytes 294920 | tf_op jit(solution)/shard_map/ppermute | solution.py:441
  13.3 21.0 %collective-permute-start.2 = (bf16[3,128,128]{2,1,0:T(8,128)(2,1)S(1)}, bf16[3,128,128]{2,1,0:T(8,128)(2,1)S(1)}, u32[]{:S(2)}, u32[]{:S(2)}) collective-permute-start(bf16[3,128,128]{2,1,0:T(8,128)(2,1)S(1)} %get-tuple-element.19), channel_id=1, source_target_pairs={{1,2},{3,0},{5,6},{7,4},{9,10},{11,8},{13,14},{15,12},{17,18},{19,... | collective-permute-start | bytes 294920 | tf_op jit(solution)/shard_map/ppermute | solution.py:443
  14.6 19.8 %collective-permute-start.1 = (bf16[3,128,128]{2,1,0:T(8,128)(2,1)S(1)}, bf16[3,128,128]{2,1,0:T(8,128)(2,1)S(1)}, u32[]{:S(2)}, u32[]{:S(2)}) collective-permute-start(bf16[3,128,128]{2,1,0:T(8,128)(2,1)S(1)} %get-tuple-element.19), channel_id=1, source_target_pairs={{0,2},{2,0},{4,6},{6,4},{8,10},{10,8},{12,14},{14,12},{16,18},{18,... | collective-permute-start | bytes 294920 | tf_op jit(solution)/shard_map/ppermute | solution.py:442
  23.3 1.0 %copy-start = (bf16[50,2,2560]{2,1,0:T(2,128)(2,1)S(1)}, bf16[50,2,2560]{2,1,0:T(2,128)(2,1)}, u32[]{:S(2)}) copy-start(bf16[50,2,2560]{2,1,0:T(2,128)(2,1)} %main_mod.1) | copy-start | bytes 1536004
  23.3 1.1 %copy-start.1 = (bf16[50,2,1024]{2,1,0:T(2,128)(2,1)S(1)}, bf16[50,2,1024]{2,1,0:T(2,128)(2,1)}, u32[]{:S(2)}) copy-start(bf16[50,2,1024]{2,1,0:T(2,128)(2,1)} %guide_mod.1) | copy-start | bytes 614404
  34.4 2.0 %collective-permute-start.3 = (bf16[8,9,32,128]{3,2,1,0:T(8,128)(2,1)S(1)}, bf16[8,9,32,128]{3,2,1,0:T(8,128)(2,1)S(1)}, u32[]{:S(2)}, u32[]{:S(2)}) collective-permute-start(bf16[8,9,32,128]{3,2,1,0:T(8,128)(2,1)S(1)} %all-to-all-done.got), channel_id=1, source_target_pairs={{0,1},{1,0},{2,3},{3,2},{4,5},{5,4},{6,7},{7,6},{8,9},{9,8},{10,11... | collective-permute-start | bytes 1769480 | tf_op jit(solution)/shard_map/ppermute | solution.py:450
  37.0 16.7 %collective-permute-start.6 = (bf16[4,512,128]{2,1,0:T(8,128)(2,1)S(1)}, bf16[4,512,128]{2,1,0:T(8,128)(2,1)S(1)}, u32[]{:S(2)}, u32[]{:S(2)}) collective-permute-start(bf16[4,512,128]{2,1,0:T(8,128)(2,1)S(1)} %get-tuple-element.31.refs_0_), channel_id=1, source_target_pairs={{0,8},{1,33},{4,12},{5,37},{8,0},{9,41},{12,4},{13,45},{16,24},{17... | collective-permute-start | bytes 1572872 | tf_op jit(solution)/shard_map/ppermute | solution.py:351
  38.3 15.5 %collective-permute-start.5 = (bf16[4,512,128]{2,1,0:T(8,128)(2,1)S(1)}, bf16[4,512,128]{2,1,0:T(8,128)(2,1)S(1)}, u32[]{:S(2)}, u32[]{:S(2)}) collective-permute-start(bf16[4,512,128]{2,1,0:T(8,128)(2,1)S(1)} %get-tuple-element.31.refs_0_), channel_id=1, source_target_pairs={{0,4},{1,17},{4,8},{5,21},{8,12},{9,25},{12,0},{13,29},{16,20},{17... | collective-permute-start | bytes 1572872 | tf_op jit(solution)/shard_map/ppermute | solution.py:351
  40.5 15.8 %collective-permute-start.4 = (bf16[4,512,128]{2,1,0:T(8,128)(2,1)S(1)}, bf16[4,512,128]{2,1,0:T(8,128)(2,1)S(1)}, u32[]{:S(2)}, u32[]{:S(2)}) collective-permute-start(bf16[4,512,128]{2,1,0:T(8,128)(2,1)S(1)} %get-tuple-element.31.refs_0_), channel_id=1, source_target_pairs={{0,12},{1,49},{4,0},{5,53},{8,4},{9,57},{12,8},{13,61},{16,28},{17... | collective-permute-start | bytes 1572872 | tf_op jit(solution)/shard_map/ppermute | solution.py:351
  40.5 11.8 %collective-permute-start.7 = (bf16[1024,128]{1,0:T(8,128)(2,1)S(1)}, bf16[1024,128]{1,0:T(8,128)(2,1)S(1)}, u32[]{:S(2)}, u32[]{:S(2)}) collective-permute-start(bf16[1024,128]{1,0:T(8,128)(2,1)S(1)} %get-tuple-element.30.queries), channel_id=1, source_target_pairs={{0,48},{1,13},{4,52},{5,1},{8,56},{9,5},{12,60},{13,9},{16,0},{17,... | collective-permute-start | bytes 786440 | tf_op jit(solution)/shard_map/ppermute | solution.py:351
  43.3 18.5 %collective-permute-start.9 = (bf16[1024,128]{1,0:T(8,128)(2,1)S(1)}, bf16[1024,128]{1,0:T(8,128)(2,1)S(1)}, u32[]{:S(2)}, u32[]{:S(2)}) collective-permute-start(bf16[1024,128]{1,0:T(8,128)(2,1)S(1)} %get-tuple-element.30.queries), channel_id=1, source_target_pairs={{0,16},{1,5},{4,20},{5,9},{8,24},{9,13},{12,28},{13,1},{16,32},{17... | collective-permute-start | bytes 786440 | tf_op jit(solution)/shard_map/ppermute | solution.py:351
  52.3 13.8 %collective-permute-start.11 = (bf16[1024,128]{1,0:T(8,128)(2,1)S(1)}, bf16[1024,128]{1,0:T(8,128)(2,1)S(1)}, u32[]{:S(2)}, u32[]{:S(2)}) collective-permute-start(bf16[1024,128]{1,0:T(8,128)(2,1)S(1)} %get-tuple-element.30.queries), channel_id=1, source_target_pairs={{0,32},{1,9},{4,36},{5,13},{8,40},{9,1},{12,44},{13,5},{16,48},{17... | collective-permute-start | bytes 786440 | tf_op jit(solution)/shard_map/ppermute | solution.py:351
  59.4 14.7 %collective-permute-start.8 = (bf16[1056,128]{1,0:T(8,128)(2,1)S(1)}, bf16[1056,128]{1,0:T(8,128)(2,1)S(1)}, u32[]{:S(2)}, u32[]{:S(2)}) collective-permute-start(bf16[1056,128]{1,0:T(8,128)(2,1)S(1)} %attend.5), channel_id=1, source_target_pairs={{0,16},{1,5},{4,20},{5,9},{8,24},{9,13},{12,28},{13,1},{16,32},{17... | collective-permute-start | bytes 811016 | tf_op jit(solution)/shard_map/ppermute | solution.py:351
  64.7 9.4 %collective-permute-start.10 = (bf16[1056,128]{1,0:T(8,128)(2,1)S(1)}, bf16[1056,128]{1,0:T(8,128)(2,1)S(1)}, u32[]{:S(2)}, u32[]{:S(2)}) collective-permute-start(bf16[1056,128]{1,0:T(8,128)(2,1)S(1)} %attend.6), channel_id=1, source_target_pairs={{0,48},{1,13},{4,52},{5,1},{8,56},{9,5},{12,60},{13,9},{16,0},{17,... | collective-permute-start | bytes 811016 | tf_op jit(solution)/shard_map/ppermute | solution.py:351
  69.1 8.0 %collective-permute-start.12 = (bf16[1056,128]{1,0:T(8,128)(2,1)S(1)}, bf16[1056,128]{1,0:T(8,128)(2,1)S(1)}, u32[]{:S(2)}, u32[]{:S(2)}) collective-permute-start(bf16[1056,128]{1,0:T(8,128)(2,1)S(1)} %attend.7), channel_id=1, source_target_pairs={{0,32},{1,9},{4,36},{5,13},{8,40},{9,1},{12,44},{13,5},{16,48},{17... | collective-permute-start | bytes 811016 | tf_op jit(solution)/shard_map/ppermute | solution.py:351
  79.1 11.8 %copy-start.5 = (f32[1,32,64]{2,1,0:T(8,128)S(1)}, f32[1,32,64]{2,1,0:T(8,128)}, u32[]{:S(2)}) copy-start(f32[1,32,64]{2,1,0:T(8,128)} %latents.1) | copy-start | bytes 24580

commit v5 on v4

--- a/solution.py
+++ b/solution.py
@@ -223,34 +223,47 @@
     shifts[0:1, :] = main_rows[20:21] + guide_rows[8:9]
 
 
-def combine_kernel(place, weights, scales, *refs):
-    parts, send = refs[:SIDE], refs[SIDE]
-    on_diagonal = diagonal()
-    levels = []
-    for part in parts:
-        block = part[HEADS * TOKENS :, :].astype(f32)
-        levels.append(block[0:8] + block[8:16] + block[16:24])
+def levels_of(part):
+    block = part[HEADS * TOKENS :, :].astype(f32)
+    return block[0:8] + block[8:16] + block[16:24]
+
+
+def merge(parts, levels):
     top = levels[0]
     for level in levels[1:]:
         top = jnp.maximum(top, level)
     shares = [jnp.exp2(level - top) for level in levels]
-    whole = shares[0] + shares[1] + shares[2] + shares[3]
+    whole = sum(shares)
     filler = jnp.zeros((HD - 8, HD), f32)
     shares = [jnp.transpose(jnp.concatenate([share / whole, filler], axis=0)) for share in shares]
+    tiles = []
+    for tile in range(HEADS * TOKENS // HD):
+        rows = slice(tile * HD, (tile + 1) * HD)
+        tiles.append(
+            sum(
+                part[rows, :].astype(f32) * share[:, tile : tile + 1]
+                for part, share in zip(parts, shares)
+            )
+        )
+    return tiles, top + jnp.log2(whole)
+
+
+def merge_kernel(*refs):
+    parts, result, level = refs[:-2], refs[-2], refs[-1]
+    tiles, level[...] = merge(parts, [levels_of(part) for part in parts])
+    for tile, value in enumerate(tiles):
+        result[tile * HD : (tile + 1) * HD, :] = value
+
+
+def combine_kernel(place, weights, scales, former, former_level, part, send):
+    on_diagonal = diagonal()
+    tiles, unused = merge([former, part], [former_level[...], levels_of(part)])
     blocks = TOKENS // HD
     flows, stats = [], []
     for head in range(HEADS):
-        merged = []
-        for tile in range(head * blocks, (head + 1) * blocks):
-            total = None
-            for part, share in zip(parts, shares):
-                column = share[:, tile : tile + 1]
-                term = part[tile * HD : (tile + 1) * HD, :].astype(f32) * column
-                total = term if total is None else total + term
-            merged.append(total)
-        attended = jnp.concatenate(merged, axis=0).astype(bf16).astype(f32)
-        mean = jnp.mean(attended, axis=1, keepdims=True)
-        centered = attended - mean
+        attended = jnp.concatenate(tiles[head * blocks : (head + 1) * blocks], axis=0).astype(bf16)
+        mean = jnp.mean(attended.astype(f32), axis=1, keepdims=True)
+        centered = attended.astype(f32) - mean
         square = jnp.sum(centered * centered, axis=1, keepdims=True)
         flow = term_dot(centered * scales[head : head + 1, :], weights[head]).astype(bf16)
         for tile in range(blocks):
@@ -460,14 +473,22 @@
     all_pairs = [pairs] + [plane_shift(pairs, by, "yx") for by in SHIFTS]
     parts = [attend(q, all_pairs) for q in all_queries]
     parts[1:] = [plane_shift(p, -by, "xy") for p, by in zip(parts[1:], SHIFTS)]
+    former, level = pl.pallas_call(
+        merge_kernel,
+        out_shape=(shape(HEADS * TOKENS, HD, dtype=f32), shape(8, HD, dtype=f32)),
+        in_specs=[VMEM] * (SIDE - 1),
+        out_specs=(VMEM,) * 2,
+        compiler_params=params(16),
+        name="merge",
+    )(*parts[:-1])
     send = pl.pallas_call(
         combine_kernel,
         out_shape=shape(CORE * Z, ROWS + 16, HD),
-        in_specs=[SMEM] + [VMEM] * (2 + SIDE),
+        in_specs=[SMEM] + [VMEM] * 5,
         out_specs=VMEM,
         compiler_params=params(16),
         name="combine",
-    )(place, weights, scales, *parts)
+    )(place, weights, scales, former, level, parts[-1])
     got = lax.all_to_all(send, ("core", "zh", "zl"), split_axis=0, concat_axis=0, tiled=True)
     velocity, advanced = pl.pallas_call(
         final_kernel,

time: 93.7 us -> 93.3 us (level)
  transfers between devices with their start and end apart: 14 -> 14, of which waited for: 7 -> 7; matrix products, arithmetic and copies ran while one was open for 1% -> 1% of each run, Pallas kernels for 15% -> 16%
where the time goes in v5:
time: 93.3 us; the launch traced here: 92.2 us
  starting transfers between devices  32.5 us (35%)
  waiting for transfers between devices  24.9 us (27%)
  Pallas kernels  20.2 us (22%)
  blocking collectives  11.8 us (13%)
  between operations  1.46 us (2%)
  local copies, waits for them, and re-layouts  1.27 us (1%)
    ppermute x9, waiting for transfers between devices, plane_shift(): return lax.ppermute(array, ('x', 'y', 'core'), pairs)  14 us
    ppermute x9, starting transfers between devices, plane_shift(): return lax.ppermute(array, ('x', 'y', 'core'), pairs)  13.5 us
    pallas_call x4, Pallas kernels, attend(): pl.pallas_call(attend_kernel, out_shape=shape(rows + STAT, HD), in_specs=...  12 us
    all_to_all x1, blocking collectives, on_device(): lax.all_to_all(send, ('core', 'zh', 'zl'), split_axis=0, concat_axis=0, t...  11.8 us
    ppermute x1, waiting for transfers between devices, on_device(): guide_across = lax.ppermute(guide_send, halves, [(1, 2), (3, 0)])  8.82 us
    all_to_all x1, starting transfers between devices, on_device(): lax.all_to_all(send, ('zh', 'zl'), split_axis=0, concat_axis=0, tiled=True)  8.61 us
    ppermute x1, starting transfers between devices, on_device(): guide_half = lax.ppermute(guide_send, halves, [(0, 2), (2, 0)])  7.83 us
    ppermute x1, waiting for transfers between devices, on_device(): sibling = lax.ppermute(got, 'core', [(0, 1), (1, 0)])  2 us
  transfers between devices with their start and end apart: 14, of which 7 were waited for; matrix products, arithmetic and copies ran while one was open for 1% of the time, Pallas kernels for 16%

profile of v5, /device:TPU:24, one launch (start us, length us, event | category | flops | bytes accessed | tf_op | source)
XLA Modules:
  0.0 92.2 jit_solution(14118872019369270017)
XLA Ops:
  0.6 2.0 %pack.1 = bf16[8,9,32,128]{3,2,1,0:T(8,128)(2,1)} custom-call(bf16[1,32,2560]{2,1,0:T(8,128)(2,1)} %mq.1, bf16[1,32,2560]{2,1,0:T(8,128)(2,1)} %mk.1, bf16[1,32,2560]{2,1,0:T(8,128)(2,1)} %mv.1), custom_call_target="tpu_custom_call" | custom-call | tf_op jit(solution)/shard_map/pack/pallas_call | solution.py:417
  2.7 8.6 %all-to-all-start = ((bf16[8,9,32,128]{3,2,1,0:T(8,128)(2,1)}), bf16[8,9,32,128]{3,2,1,0:T(8,128)(2,1)S(1)}, u32[]{:S(2)}, u32[]{:S(2)}) async-start(bf16[8,9,32,128]{3,2,1,0:T(8,128)(2,1)} %pack.1), calls=%async_computation | async-start | bytes 1179648 | tf_op jit(solution)/shard_map/all_to_all | solution.py:457
  11.4 0.7 pack_guide.1
  12.0 1.3 %collective-permute-start = (bf16[3,128,128]{2,1,0:T(8,128)(2,1)S(1)}, bf16[3,128,128]{2,1,0:T(8,128)(2,1)S(1)}, u32[]{:S(2)}, u32[]{:S(2)}) collective-permute-start(bf16[3,128,128]{2,1,0:T(8,128)(2,1)S(1)} %get-tuple-element.20.guide_own), channel_id=1, source_target_pairs={{1,0},{3,2},{5,4},{7,6},{9,8},{11,10},{13,12},{15,14},{17,16},{19,... | collective-permute-start | bytes 294920 | tf_op jit(solution)/shard_map/ppermute | solution.py:454
  13.3 1.3 %collective-permute-start.2 = (bf16[3,128,128]{2,1,0:T(8,128)(2,1)S(1)}, bf16[3,128,128]{2,1,0:T(8,128)(2,1)S(1)}, u32[]{:S(2)}, u32[]{:S(2)}) collective-permute-start(bf16[3,128,128]{2,1,0:T(8,128)(2,1)S(1)} %get-tuple-element.21), channel_id=1, source_target_pairs={{1,2},{3,0},{5,6},{7,4},{9,10},{11,8},{13,14},{15,12},{17,18},{19,... | collective-permute-start | bytes 294920 | tf_op jit(solution)/shard_map/ppermute | solution.py:456
  14.6 7.8 %collective-permute-start.1 = (bf16[3,128,128]{2,1,0:T(8,128)(2,1)S(1)}, bf16[3,128,128]{2,1,0:T(8,128)(2,1)S(1)}, u32[]{:S(2)}, u32[]{:S(2)}) collective-permute-start(bf16[3,128,128]{2,1,0:T(8,128)(2,1)S(1)} %get-tuple-element.21), channel_id=1, source_target_pairs={{0,2},{2,0},{4,6},{6,4},{8,10},{10,8},{12,14},{14,12},{16,18},{18,... | collective-permute-start | bytes 294920 | tf_op jit(solution)/shard_map/ppermute | solution.py:455
  23.1 0.2 copy.15.guide_head
  23.3 0.3 copy.14.main_head
  23.7 0.7 copy-done
  24.4 1.1 %prepare.1 = (bf16[2,128,64]{2,1,0:T(8,128)(2,1)S(1)}, f32[8,128]{1,0:T(8,128)S(1)}, f32[128,128]{1,0:T(8,128)S(1)}, f32[8,128]{1,0:T(8,128)S(1)}) custom-call(s32[1]{0:T(128)S(6)} %copy.16.step, s32[3]{0:T(128)S(1)} %pad_add_fusion.place, bf16[50,2,2560]{2,1,0:T(2,128)(2,1)S(1)} %copy-done, bf16[50,2,1024]{2,1,0:T(2,128)(2,1)S(1)} %copy-done.1, ...), custom_call_target="tpu_custom_call" | custom-call | tf_op jit(solution)/shard_map/prepare/pallas_call | solution.py:431
  25.5 8.8 %collective-permute-done.2.guide_across = bf16[3,128,128]{2,1,0:T(8,128)(2,1)S(1)} collective-permute-done((bf16[3,128,128]{2,1,0:T(8,128)(2,1)S(1)}, bf16[3,128,128]{2,1,0:T(8,128)(2,1)S(1)}, u32[]{:S(2)}, u32[]{:S(2)}) %collective-permute-start.2) | collective-permute-done | bytes 98336 | tf_op jit(solution)/shard_map/ppermute | solution.py:456
  34.3 0.1 collective-permute-done.1.guide_half
  34.4 2.0 %collective-permute-done.3.sibling = bf16[8,9,32,128]{3,2,1,0:T(8,128)(2,1)S(1)} collective-permute-done((bf16[8,9,32,128]{3,2,1,0:T(8,128)(2,1)S(1)}, bf16[8,9,32,128]{3,2,1,0:T(8,128)(2,1)S(1)}, u32[]{:S(2)}, u32[]{:S(2)}) %collective-permute-start.3) | collective-permute-done | bytes 589856 | tf_op jit(solution)/shard_map/ppermute | solution.py:463
  36.4 0.6 unpack.1
  37.0 1.3 %collective-permute-start.6 = (bf16[4,512,128]{2,1,0:T(8,128)(2,1)S(1)}, bf16[4,512,128]{2,1,0:T(8,128)(2,1)S(1)}, u32[]{:S(2)}, u32[]{:S(2)}) collective-permute-start(bf16[4,512,128]{2,1,0:T(8,128)(2,1)S(1)} %get-tuple-element.33.refs_0_), channel_id=1, source_target_pairs={{0,8},{1,33},{4,12},{5,37},{8,0},{9,41},{12,4},{13,45},{16,24},{17... | collective-permute-start | bytes 1572872 | tf_op jit(solution)/shard_map/ppermute | solution.py:364
  38.3 2.2 %collective-permute-start.5 = (bf16[4,512,128]{2,1,0:T(8,128)(2,1)S(1)}, bf16[4,512,128]{2,1,0:T(8,128)(2,1)S(1)}, u32[]{:S(2)}, u32[]{:S(2)}) collective-permute-start(bf16[4,512,128]{2,1,0:T(8,128)(2,1)S(1)} %get-tuple-element.33.refs_0_), channel_id=1, source_target_pairs={{0,4},{1,17},{4,8},{5,21},{8,12},{9,25},{12,0},{13,29},{16,20},{17... | collective-permute-start | bytes 1572872 | tf_op jit(solution)/shard_map/ppermute | solution.py:364
  40.5 2.8 %collective-permute-start.7 = (bf16[1024,128]{1,0:T(8,128)(2,1)S(1)}, bf16[1024,128]{1,0:T(8,128)(2,1)S(1)}, u32[]{:S(2)}, u32[]{:S(2)}) collective-permute-start(bf16[1024,128]{1,0:T(8,128)(2,1)S(1)} %get-tuple-element.32.queries), channel_id=1, source_target_pairs={{0,48},{1,13},{4,52},{5,1},{8,56},{9,5},{12,60},{13,9},{16,0},{17,... | collective-permute-start | bytes 786440 | tf_op jit(solution)/shard_map/ppermute | solution.py:364
  43.3 9.0 %collective-permute-done.7.queries = bf16[1024,128]{1,0:T(8,128)(2,1)S(1)} collective-permute-done((bf16[1024,128]{1,0:T(8,128)(2,1)S(1)}, bf16[1024,128]{1,0:T(8,128)(2,1)S(1)}, u32[]{:S(2)}, u32[]{:S(2)}) %collective-permute-start.7) | collective-permute-done | bytes 262176 | tf_op jit(solution)/shard_map/ppermute | solution.py:364
  52.3 1.5 %collective-permute-start.11 = (bf16[1024,128]{1,0:T(8,128)(2,1)S(1)}, bf16[1024,128]{1,0:T(8,128)(2,1)S(1)}, u32[]{:S(2)}, u32[]{:S(2)}) collective-permute-start(bf16[1024,128]{1,0:T(8,128)(2,1)S(1)} %get-tuple-element.32.queries), channel_id=1, source_target_pairs={{0,32},{1,9},{4,36},{5,13},{8,40},{9,1},{12,44},{13,5},{16,48},{17... | collective-permute-start | bytes 786440 | tf_op jit(solution)/shard_map/ppermute | solution.py:364
  53.8 2.6 %collective-permute-done.4.refs_1_ = bf16[4,512,128]{2,1,0:T(8,128)(2,1)S(1)} collective-permute-done((bf16[4,512,128]{2,1,0:T(8,128)(2,1)S(1)}, bf16[4,512,128]{2,1,0:T(8,128)(2,1)S(1)}, u32[]{:S(2)}, u32[]{:S(2)}) %collective-permute-start.4) | collective-permute-done | bytes 524320 | tf_op jit(solution)/shard_map/ppermute | solution.py:364
  56.4 3.0 %attend.5 = bf16[1056,128]{1,0:T(8,128)(2,1)S(1)} custom-call(bf16[1024,128]{1,0:T(8,128)(2,1)S(1)} %collective-permute-done.7.queries, bf16[4,512,128]{2,1,0:T(8,128)(2,1)S(1)} %get-tuple-element.33.refs_0_, bf16[4,512,128]{2,1,0:T(8,128)(2,1)S(1)} %collective-permute-done.4.refs_1_, bf16[4,512,128]{2,1,0:T(8,128)(2,1)S(1)} %collective-permute-done.5.refs_2_, ...), custom_call_target="tpu_custom_call" | custom-call | flops 1073741824 | bytes 2097152 | tf_op jit(solution)/shard_map/attend/pallas_call | solution.py:372
  59.4 2.4 %collective-permute-start.8 = (bf16[1056,128]{1,0:T(8,128)(2,1)S(1)}, bf16[1056,128]{1,0:T(8,128)(2,1)S(1)}, u32[]{:S(2)}, u32[]{:S(2)}) collective-permute-start(bf16[1056,128]{1,0:T(8,128)(2,1)S(1)} %attend.5), channel_id=1, source_target_pairs={{0,16},{1,5},{4,20},{5,9},{8,24},{9,13},{12,28},{13,1},{16,32},{17... | collective-permute-start | bytes 811016 | tf_op jit(solution)/shard_map/ppermute | solution.py:364
  61.8 3.0 %attend.6 = bf16[1056,128]{1,0:T(8,128)(2,1)S(1)} custom-call(bf16[1024,128]{1,0:T(8,128)(2,1)S(1)} %collective-permute-done.9.queries, bf16[4,512,128]{2,1,0:T(8,128)(2,1)S(1)} %get-tuple-element.33.refs_0_, bf16[4,512,128]{2,1,0:T(8,128)(2,1)S(1)} %collective-permute-done.4.refs_1_, bf16[4,512,128]{2,1,0:T(8,128)(2,1)S(1)} %collective-permute-done.5.refs_2_, ...), custom_call_target="tpu_custom_call" | custom-call | flops 1073741824 | bytes 2097152 | tf_op jit(solution)/shard_map/attend/pallas_call | solution.py:372
  64.8 1.3 %collective-permute-start.10 = (bf16[1056,128]{1,0:T(8,128)(2,1)S(1)}, bf16[1056,128]{1,0:T(8,128)(2,1)S(1)}, u32[]{:S(2)}, u32[]{:S(2)}) collective-permute-start(bf16[1056,128]{1,0:T(8,128)(2,1)S(1)} %attend.6), channel_id=1, source_target_pairs={{0,48},{1,13},{4,52},{5,1},{8,56},{9,5},{12,60},{13,9},{16,0},{17,... | collective-permute-start | bytes 811016 | tf_op jit(solution)/shard_map/ppermute | solution.py:364
  66.1 3.0 %attend.7 = bf16[1056,128]{1,0:T(8,128)(2,1)S(1)} custom-call(bf16[1024,128]{1,0:T(8,128)(2,1)S(1)} %collective-permute-done.11.queries, bf16[4,512,128]{2,1,0:T(8,128)(2,1)S(1)} %get-tuple-element.33.refs_0_, bf16[4,512,128]{2,1,0:T(8,128)(2,1)S(1)} %collective-permute-done.4.refs_1_, bf16[4,512,128]{2,1,0:T(8,128)(2,1)S(1)} %collective-permute-done.5.refs_2_, ...), custom_call_target="tpu_custom_call" | custom-call | flops 1073741824 | bytes 2097152 | tf_op jit(solution)/shard_map/attend/pallas_call | solution.py:372
  69.1 2.0 %collective-permute-start.12 = (bf16[1056,128]{1,0:T(8,128)(2,1)S(1)}, bf16[1056,128]{1,0:T(8,128)(2,1)S(1)}, u32[]{:S(2)}, u32[]{:S(2)}) collective-permute-start(bf16[1056,128]{1,0:T(8,128)(2,1)S(1)} %attend.7), channel_id=1, source_target_pairs={{0,32},{1,9},{4,36},{5,13},{8,40},{9,1},{12,44},{13,5},{16,48},{17... | collective-permute-start | bytes 811016 | tf_op jit(solution)/shard_map/ppermute | solution.py:364
  71.1 3.0 %attend.4.refs_0_ = bf16[1056,128]{1,0:T(8,128)(2,1)S(1)} custom-call(bf16[1024,128]{1,0:T(8,128)(2,1)S(1)} %get-tuple-element.32.queries, bf16[4,512,128]{2,1,0:T(8,128)(2,1)S(1)} %get-tuple-element.33.refs_0_, bf16[4,512,128]{2,1,0:T(8,128)(2,1)S(1)} %collective-permute-done.4.refs_1_, bf16[4,512,128]{2,1,0:T(8,128)(2,1)S(1)} %collective-permute-done.5.refs_2_, ...), custom_call_target="tpu_custom_call" | custom-call | flops 1073741824 | bytes 2097152 | tf_op jit(solution)/shard_map/attend/pallas_call | solution.py:372
  74.1 0.7 merge.1
  74.8 2.3 %collective-permute-done.12.part = bf16[1056,128]{1,0:T(8,128)(2,1)S(1)} collective-permute-done((bf16[1056,128]{1,0:T(8,128)(2,1)S(1)}, bf16[1056,128]{1,0:T(8,128)(2,1)S(1)}, u32[]{:S(2)}, u32[]{:S(2)}) %collective-permute-start.12) | collective-permute-done | bytes 270368 | tf_op jit(solution)/shard_map/ppermute | solution.py:364
  77.1 1.6 %combine.1 = bf16[16,48,128]{2,1,0:T(8,128)(2,1)S(1)} custom-call(s32[3]{0:T(128)S(1)} %pad_add_fusion.place, bf16[2,128,64]{2,1,0:T(8,128)(2,1)S(1)} %get-tuple-element.26.weights, f32[8,128]{1,0:T(8,128)S(1)} %get-tuple-element.27.scales, f32[1024,128]{1,0:T(8,128)S(1)} %get-tuple-element.34.former, f32[8,128]{1,0:T(8,128)S(1)} %get-tuple-element.35.former_level, ...), custom_call_target="tpu_custom_call" | custom-call | tf_op jit(solution)/shard_map/combine/pallas_call | solution.py:484
  78.7 11.8 %all_to_all.10.got = bf16[16,48,128]{2,1,0:T(8,128)(2,1)S(1)} all-to-all(bf16[16,48,128]{2,1,0:T(8,128)(2,1)S(1)} %combine.1), channel_id=1, replica_groups=mesh['zl'=4,'x'=4,'y'=4,'zh'=2,'core'=2] {'core','zh','zl'}, dimensions={0} | all-to-all | bytes 393216 | tf_op jit(solution)/shard_map/all_to_all | solution.py:492
  90.5 1.7 %final.1 = (f32[1,32,64]{2,1,0:T(8,128)}, f32[1,32,64]{2,1,0:T(8,128)}) custom-call(s32[1]{0:T(128)S(6)} %copy.16.step, s32[3]{0:T(128)S(1)} %pad_add_fusion.place, bf16[16,48,128]{2,1,0:T(8,128)(2,1)S(1)} %all_to_all.10.got, f32[128,128]{1,0:T(8,128)S(1)} %get-tuple-element.36.means, f32[8,128]{1,0:T(8,128)S(1)} %get-tuple-element.37.shifts, ...), custom_call_target="tpu_custom_call" | custom-call | tf_op jit(solution)/shard_map/final/pallas_call | solution.py:493
  (27 shorter events, 0.3 us)
Async XLA Ops:
  2.6 8.7 %copy-start.2 = (bf16[1,128,256]{2,1,0:T(8,128)(2,1)S(1)}, bf16[1,128,256]{2,1,0:T(8,128)(2,1)}, u32[]{:S(2)}) copy-start(bf16[1,128,256]{2,1,0:T(8,128)(2,1)} %gq.1) | copy-start | bytes 196612
  2.6 8.7 %copy-start.3 = (bf16[1,128,256]{2,1,0:T(8,128)(2,1)S(1)}, bf16[1,128,256]{2,1,0:T(8,128)(2,1)}, u32[]{:S(2)}) copy-start(bf16[1,128,256]{2,1,0:T(8,128)(2,1)} %gk.1) | copy-start | bytes 196612
  2.6 8.7 %copy-start.4 = (bf16[1,128,256]{2,1,0:T(8,128)(2,1)S(1)}, bf16[1,128,256]{2,1,0:T(8,128)(2,1)}, u32[]{:S(2)}) copy-start(bf16[1,128,256]{2,1,0:T(8,128)(2,1)} %gv.1) | copy-start | bytes 196612
  2.7 20.5 %copy-start.7 = (bf16[1024,64]{0,1:T(8,128)(2,1)S(1)}, bf16[1024,64]{0,1:T(8,128)(2,1)}, u32[]{:S(2)}) copy-start(bf16[1024,64]{0,1:T(8,128)(2,1)} %param.23) | copy-start | bytes 393220
  2.7 31.7 %all-to-all-start = ((bf16[8,9,32,128]{3,2,1,0:T(8,128)(2,1)}), bf16[8,9,32,128]{3,2,1,0:T(8,128)(2,1)S(1)}, u32[]{:S(2)}, u32[]{:S(2)}) async-start(bf16[8,9,32,128]{3,2,1,0:T(8,128)(2,1)} %pack.1), calls=%async_computation | async-start | bytes 1179648 | tf_op jit(solution)/shard_map/all_to_all | solution.py:457
  11.3 12.0 %copy-start.6 = (bf16[2560,64]{0,1:T(8,128)(2,1)S(1)}, bf16[2560,64]{0,1:T(8,128)(2,1)}, u32[]{:S(2)}) copy-start(bf16[2560,64]{0,1:T(8,128)(2,1)} %param.22) | copy-start | bytes 983044
  12.0 13.4 %collective-permute-start = (bf16[3,128,128]{2,1,0:T(8,128)(2,1)S(1)}, bf16[3,128,128]{2,1,0:T(8,128)(2,1)S(1)}, u32[]{:S(2)}, u32[]{:S(2)}) collective-permute-start(bf16[3,128,128]{2,1,0:T(8,128)(2,1)S(1)} %get-tuple-element.20.guide_own), channel_id=1, source_target_pairs={{1,0},{3,2},{5,4},{7,6},{9,8},{11,10},{13,12},{15,14},{17,16},{19,... | collective-permute-start | bytes 294920 | tf_op jit(solution)/shard_map/ppermute | solution.py:454
  13.3 21.0 %collective-permute-start.2 = (bf16[3,128,128]{2,1,0:T(8,128)(2,1)S(1)}, bf16[3,128,128]{2,1,0:T(8,128)(2,1)S(1)}, u32[]{:S(2)}, u32[]{:S(2)}) collective-permute-start(bf16[3,128,128]{2,1,0:T(8,128)(2,1)S(1)} %get-tuple-element.21), channel_id=1, source_target_pairs={{1,2},{3,0},{5,6},{7,4},{9,10},{11,8},{13,14},{15,12},{17,18},{19,... | collective-permute-start | bytes 294920 | tf_op jit(solution)/shard_map/ppermute | solution.py:456
  14.6 19.8 %collective-permute-start.1 = (bf16[3,128,128]{2,1,0:T(8,128)(2,1)S(1)}, bf16[3,128,128]{2,1,0:T(8,128)(2,1)S(1)}, u32[]{:S(2)}, u32[]{:S(2)}) collective-permute-start(bf16[3,128,128]{2,1,0:T(8,128)(2,1)S(1)} %get-tuple-element.21), channel_id=1, source_target_pairs={{0,2},{2,0},{4,6},{6,4},{8,10},{10,8},{12,14},{14,12},{16,18},{18,... | collective-permute-start | bytes 294920 | tf_op jit(solution)/shard_map/ppermute | solution.py:455
  23.3 1.0 %copy-start = (bf16[50,2,2560]{2,1,0:T(2,128)(2,1)S(1)}, bf16[50,2,2560]{2,1,0:T(2,128)(2,1)}, u32[]{:S(2)}) copy-start(bf16[50,2,2560]{2,1,0:T(2,128)(2,1)} %main_mod.1) | copy-start | bytes 1536004
  23.3 1.1 %copy-start.1 = (bf16[50,2,1024]{2,1,0:T(2,128)(2,1)S(1)}, bf16[50,2,1024]{2,1,0:T(2,128)(2,1)}, u32[]{:S(2)}) copy-start(bf16[50,2,1024]{2,1,0:T(2,128)(2,1)} %guide_mod.1) | copy-start | bytes 614404
  34.4 2.0 %collective-permute-start.3 = (bf16[8,9,32,128]{3,2,1,0:T(8,128)(2,1)S(1)}, bf16[8,9,32,128]{3,2,1,0:T(8,128)(2,1)S(1)}, u32[]{:S(2)}, u32[]{:S(2)}) collective-permute-start(bf16[8,9,32,128]{3,2,1,0:T(8,128)(2,1)S(1)} %all-to-all-done.got), channel_id=1, source_target_pairs={{0,1},{1,0},{2,3},{3,2},{4,5},{5,4},{6,7},{7,6},{8,9},{9,8},{10,11... | collective-permute-start | bytes 1769480 | tf_op jit(solution)/shard_map/ppermute | solution.py:463
  37.0 16.7 %collective-permute-start.6 = (bf16[4,512,128]{2,1,0:T(8,128)(2,1)S(1)}, bf16[4,512,128]{2,1,0:T(8,128)(2,1)S(1)}, u32[]{:S(2)}, u32[]{:S(2)}) collective-permute-start(bf16[4,512,128]{2,1,0:T(8,128)(2,1)S(1)} %get-tuple-element.33.refs_0_), channel_id=1, source_target_pairs={{0,8},{1,33},{4,12},{5,37},{8,0},{9,41},{12,4},{13,45},{16,24},{17... | collective-permute-start | bytes 1572872 | tf_op jit(solution)/shard_map/ppermute | solution.py:364
  38.3 15.5 %collective-permute-start.5 = (bf16[4,512,128]{2,1,0:T(8,128)(2,1)S(1)}, bf16[4,512,128]{2,1,0:T(8,128)(2,1)S(1)}, u32[]{:S(2)}, u32[]{:S(2)}) collective-permute-start(bf16[4,512,128]{2,1,0:T(8,128)(2,1)S(1)} %get-tuple-element.33.refs_0_), channel_id=1, source_target_pairs={{0,4},{1,17},{4,8},{5,21},{8,12},{9,25},{12,0},{13,29},{16,20},{17... | collective-permute-start | bytes 1572872 | tf_op jit(solution)/shard_map/ppermute | solution.py:364
  40.5 15.8 %collective-permute-start.4 = (bf16[4,512,128]{2,1,0:T(8,128)(2,1)S(1)}, bf16[4,512,128]{2,1,0:T(8,128)(2,1)S(1)}, u32[]{:S(2)}, u32[]{:S(2)}) collective-permute-start(bf16[4,512,128]{2,1,0:T(8,128)(2,1)S(1)} %get-tuple-element.33.refs_0_), channel_id=1, source_target_pairs={{0,12},{1,49},{4,0},{5,53},{8,4},{9,57},{12,8},{13,61},{16,28},{17... | collective-permute-start | bytes 1572872 | tf_op jit(solution)/shard_map/ppermute | solution.py:364
  40.5 11.8 %collective-permute-start.7 = (bf16[1024,128]{1,0:T(8,128)(2,1)S(1)}, bf16[1024,128]{1,0:T(8,128)(2,1)S(1)}, u32[]{:S(2)}, u32[]{:S(2)}) collective-permute-start(bf16[1024,128]{1,0:T(8,128)(2,1)S(1)} %get-tuple-element.32.queries), channel_id=1, source_target_pairs={{0,48},{1,13},{4,52},{5,1},{8,56},{9,5},{12,60},{13,9},{16,0},{17,... | collective-permute-start | bytes 786440 | tf_op jit(solution)/shard_map/ppermute | solution.py:364
  43.3 18.5 %collective-permute-start.9 = (bf16[1024,128]{1,0:T(8,128)(2,1)S(1)}, bf16[1024,128]{1,0:T(8,128)(2,1)S(1)}, u32[]{:S(2)}, u32[]{:S(2)}) collective-permute-start(bf16[1024,128]{1,0:T(8,128)(2,1)S(1)} %get-tuple-element.32.queries), channel_id=1, source_target_pairs={{0,16},{1,5},{4,20},{5,9},{8,24},{9,13},{12,28},{13,1},{16,32},{17... | collective-permute-start | bytes 786440 | tf_op jit(solution)/shard_map/ppermute | solution.py:364
  52.3 13.8 %collective-permute-start.11 = (bf16[1024,128]{1,0:T(8,128)(2,1)S(1)}, bf16[1024,128]{1,0:T(8,128)(2,1)S(1)}, u32[]{:S(2)}, u32[]{:S(2)}) collective-permute-start(bf16[1024,128]{1,0:T(8,128)(2,1)S(1)} %get-tuple-element.32.queries), channel_id=1, source_target_pairs={{0,32},{1,9},{4,36},{5,13},{8,40},{9,1},{12,44},{13,5},{16,48},{17... | collective-permute-start | bytes 786440 | tf_op jit(solution)/shard_map/ppermute | solution.py:364
  59.4 14.7 %collective-permute-start.8 = (bf16[1056,128]{1,0:T(8,128)(2,1)S(1)}, bf16[1056,128]{1,0:T(8,128)(2,1)S(1)}, u32[]{:S(2)}, u32[]{:S(2)}) collective-permute-start(bf16[1056,128]{1,0:T(8,128)(2,1)S(1)} %attend.5), channel_id=1, source_target_pairs={{0,16},{1,5},{4,20},{5,9},{8,24},{9,13},{12,28},{13,1},{16,32},{17... | collective-permute-start | bytes 811016 | tf_op jit(solution)/shard_map/ppermute | solution.py:364
  64.8 9.4 %collective-permute-start.10 = (bf16[1056,128]{1,0:T(8,128)(2,1)S(1)}, bf16[1056,128]{1,0:T(8,128)(2,1)S(1)}, u32[]{:S(2)}, u32[]{:S(2)}) collective-permute-start(bf16[1056,128]{1,0:T(8,128)(2,1)S(1)} %attend.6), channel_id=1, source_target_pairs={{0,48},{1,13},{4,52},{5,1},{8,56},{9,5},{12,60},{13,9},{16,0},{17,... | collective-permute-start | bytes 811016 | tf_op jit(solution)/shard_map/ppermute | solution.py:364
  69.1 8.0 %collective-permute-start.12 = (bf16[1056,128]{1,0:T(8,128)(2,1)S(1)}, bf16[1056,128]{1,0:T(8,128)(2,1)S(1)}, u32[]{:S(2)}, u32[]{:S(2)}) collective-permute-start(bf16[1056,128]{1,0:T(8,128)(2,1)S(1)} %attend.7), channel_id=1, source_target_pairs={{0,32},{1,9},{4,36},{5,13},{8,40},{9,1},{12,44},{13,5},{16,48},{17... | collective-permute-start | bytes 811016 | tf_op jit(solution)/shard_map/ppermute | solution.py:364
  78.7 11.8 %copy-start.5 = (f32[1,32,64]{2,1,0:T(8,128)S(1)}, f32[1,32,64]{2,1,0:T(8,128)}, u32[]{:S(2)}) copy-start(f32[1,32,64]{2,1,0:T(8,128)} %latents.1) | copy-start | bytes 24580

commit v6 on v5

--- a/solution.py
+++ b/solution.py
@@ -14,6 +14,9 @@
 Z = ZL * ZH
 SIDE = 4
 ROWS = 32
+PART = ROWS // ZH
+SET = 3 * ROWS
+MESSAGE = 2 * SET + 2 * ROWS + PART
 BLOCK = 128
 COLUMN = ROWS * Z
 TOKENS = COLUMN * CORE
@@ -64,10 +67,18 @@
         copy.wait()
         for zh_to in range(ZH):
             for zl_to in range(ZL):
-                for slot in range(3):
-                    head = zl_to * 5 + (4 if slot == 2 else 2 * zh_to + slot)
-                    lanes = slice(head * HD, (head + 1) * HD)
-                    send[zh_to * ZL + zl_to, slot * 3 + kind] = main[kind, :, lanes]
+                to = zh_to * ZL + zl_to
+                for slot in range(2):
+                    head = zl_to * 5 + 2 * zh_to + slot
+                    start = slot * SET + kind * ROWS
+                    send[to, start : start + ROWS, :] = main[kind, :, head * HD : (head + 1) * HD]
+                lanes = slice((zl_to * 5 + 4) * HD, (zl_to * 5 + 5) * HD)
+                if kind == 0:
+                    rows = slice(zh_to * PART, (zh_to + 1) * PART)
+                    send[to, 2 * SET + 2 * ROWS :, :] = main[0, rows, lanes]
+                else:
+                    start = 2 * SET + (kind - 1) * ROWS
+                    send[to, start : start + ROWS, :] = main[kind, :, lanes]
 
 
 def unpack_kernel(
@@ -78,9 +89,11 @@
         base = whose * COLUMN
         for source in range(Z):
             rows = pl.ds(pl.multiple_of(base + source * ROWS, ROWS), ROWS)
-            queries[rows, :] = ref[source, core * 3]
+            start = pl.multiple_of(core * SET, ROWS)
+            queries[rows, :] = ref[source, pl.ds(start, ROWS), :]
             for kind in range(2):
-                pairs[kind, rows, :] = ref[source, core * 3 + 1 + kind]
+                at = pl.multiple_of(start + (1 + kind) * ROWS, ROWS)
+                pairs[kind, rows, :] = ref[source, pl.ds(at, ROWS), :]
 
     @pl.when(core == 0)
     def _():
@@ -101,10 +114,10 @@
             for source in range(Z):
                 rows = pl.ds(whose * COLUMN + source * ROWS, ROWS)
                 for kind in range(2):
-                    pairs[2 + kind, rows, :] = ref[source, 7 + kind]
-            for zl in range(ZL):
-                rows = pl.ds(TOKENS + whose * BLOCK + zl * ROWS, ROWS)
-                queries[rows, :] = ref[zh * ZL + zl, 6]
+                    start = 2 * SET + kind * ROWS
+                    pairs[2 + kind, rows, :] = ref[source, start : start + ROWS, :]
+                rows = pl.ds(TOKENS + whose * BLOCK + source * PART, PART)
+                queries[rows, :] = ref[source, 2 * SET + 2 * ROWS :, :]
         queries[pl.ds(TOKENS + COLUMN, COLUMN), :] = jnp.zeros((COLUMN, HD), bf16)
 
 
@@ -259,6 +272,15 @@
     on_diagonal = diagonal()
     tiles, unused = merge([former, part], [former_level[...], levels_of(part)])
     blocks = TOKENS // HD
+    for tile in range(blocks):
+        narrow = tiles[blocks + tile // ZH]
+        start = tile % ZH * (HD // ZH)
+        pieces = []
+        for row in range(start, start + HD // ZH, PART):
+            pieces += [narrow[row : row + PART]] * ZH
+        wide = jnp.concatenate(pieces, axis=0)
+        tiles.append(jnp.where(place[1] == 1, wide, tiles[blocks + tile]))
+    tiles = tiles[:blocks] + tiles[2 * blocks :]
     flows, stats = [], []
     for head in range(HEADS):
         attended = jnp.concatenate(tiles[head * blocks : (head + 1) * blocks], axis=0).astype(bf16)
@@ -275,25 +297,16 @@
             ]
             stats.append(terms(jnp.concatenate(both, axis=0)))
 
-    def put(pick):
-        for tile in range(TOKENS // HD):
-            other = pick(tile)
-            rows = jnp.concatenate([flows[tile], flows[other]], axis=1)
-            both = jnp.concatenate(
-                [stats[tile].astype(f32), stats[other].astype(f32), jnp.zeros((8, HD), f32)],
-                axis=0,
-            ).astype(bf16)
-            for zl in range(ZL):
-                send[tile * ZL + zl, 0:ROWS, :] = rows[zl * ROWS : (zl + 1) * ROWS, :]
-                send[tile * ZL + zl, ROWS : ROWS + 16, :] = both
-
-    @pl.when(place[1] == 0)
-    def _():
-        put(lambda tile: blocks + tile)
-
-    @pl.when(place[1] == 1)
-    def _():
-        put(lambda tile: blocks + tile // ZH)
+    for tile in range(blocks):
+        other = blocks + tile
+        rows = jnp.concatenate([flows[tile], flows[other]], axis=1)
+        both = jnp.concatenate(
+            [stats[tile].astype(f32), stats[other].astype(f32), jnp.zeros((8, HD), f32)],
+            axis=0,
+        ).astype(bf16)
+        for zl in range(ZL):
+            send[tile * ZL + zl, 0:ROWS, :] = rows[zl * ROWS : (zl + 1) * ROWS, :]
+            send[tile * ZL + zl, ROWS : ROWS + 16, :] = both
 
 
 def sigma_at(index):
@@ -302,14 +315,15 @@
 
 
 def final_kernel(step, place, got, means, shifts, latents, velocity, advanced, columns):
-    zh, zl = place[0], place[2]
+    zl = place[2]
 
     def flows(source):
         return got[source, 0:ROWS, :].astype(f32)
 
     lower = sum(flows(source) for source in range(Z))
     upper = sum(flows(Z + source) for source in range(Z))
-    shared = sum(flows(Z + zh * ZL + source) for source in range(ZL))
+    shared = [sum(flows(Z + zh * ZL + zl) for zl in range(ZL)) for zh in range(ZH)]
+    shared = jnp.concatenate([shared[0][:PART], shared[1][PART:]], axis=0)
     upper = upper[:, :C] + shared[:, C:]
     total = lower + jnp.concatenate([upper, jnp.zeros((ROWS, C), f32)], axis=1)
 
@@ -320,7 +334,8 @@
     table = jnp.concatenate(table, axis=0)
     row = lax.broadcasted_iota(jnp.int32, (HD, HD), 0)
     kind, source = row & 7, row >> 3
-    second = (source >= Z + zh * ZL) & (source < Z + zh * ZL + ZL)
+    token = lax.broadcasted_iota(jnp.int32, (HD, HD), 1)
+    second = (source >= Z) & (((source - Z) >> 2) == ((token >> 4) & 1))
 
     def gathered(count, of_mean, of_square):
         mean = jnp.sum(jnp.where(of_mean, table, 0.0), axis=0, keepdims=True) / count
@@ -416,7 +431,7 @@
     )(place, guide_query, guide_key, guide_value)
     send = pl.pallas_call(
         pack_kernel,
-        out_shape=shape(Z, 9, ROWS, HD),
+        out_shape=shape(Z, MESSAGE, HD),
         in_specs=[ANY] * 3,
         out_specs=VMEM,
         scratch_shapes=[

time: 93.3 us -> 92.5 us (level)
  no operation moved by 1% of the time
where the time goes in v6:
time: 92.5 us; the launch traced here: 91.4 us
  starting transfers between devices  32.5 us (35%)
  waiting for transfers between devices  24.2 us (26%)
  Pallas kernels  20.2 us (22%)
  blocking collectives  11.8 us (13%)
  between operations  1.46 us (2%)
  local copies, waits for them, and re-layouts  1.27 us (1%)
    ppermute x9, waiting for transfers between devices, plane_shift(): return lax.ppermute(array, ('x', 'y', 'core'), pairs)  14 us
    ppermute x9, starting transfers between devices, plane_shift(): return lax.ppermute(array, ('x', 'y', 'core'), pairs)  13.5 us
    pallas_call x4, Pallas kernels, attend(): pl.pallas_call(attend_kernel, out_shape=shape(rows + STAT, HD), in_specs=...  12 us
    all_to_all x1, blocking collectives, on_device(): lax.all_to_all(send, ('core', 'zh', 'zl'), split_axis=0, concat_axis=0, t...  11.8 us
    all_to_all x1, starting transfers between devices, on_device(): lax.all_to_all(send, ('zh', 'zl'), split_axis=0, concat_axis=0, tiled=True)  8.61 us
    ppermute x1, waiting for transfers between devices, on_device(): guide_across = lax.ppermute(guide_send, halves, [(1, 2), (3, 0)])  8.11 us
    ppermute x1, starting transfers between devices, on_device(): guide_half = lax.ppermute(guide_send, halves, [(0, 2), (2, 0)])  7.83 us
    ppermute x1, waiting for transfers between devices, on_device(): sibling = lax.ppermute(got, 'core', [(0, 1), (1, 0)])  1.96 us
  transfers between devices with their start and end apart: 14, of which 7 were waited for; matrix products, arithmetic and copies ran while one was open for 1% of the time, Pallas kernels for 16%

profile of v6, /device:TPU:24, one launch (start us, length us, event | category | flops | bytes accessed | tf_op | source)
XLA Modules:
  0.0 91.4 jit_solution(7442010577148427950)
XLA Ops:
  0.6 1.9 %pack.1 = bf16[8,272,128]{2,1,0:T(8,128)(2,1)} custom-call(bf16[1,32,2560]{2,1,0:T(8,128)(2,1)} %mq.1, bf16[1,32,2560]{2,1,0:T(8,128)(2,1)} %mk.1, bf16[1,32,2560]{2,1,0:T(8,128)(2,1)} %mv.1), custom_call_target="tpu_custom_call" | custom-call | tf_op jit(solution)/shard_map/pack/pallas_call | solution.py:432
  2.6 8.6 %all-to-all-start = ((bf16[8,272,128]{2,1,0:T(8,128)(2,1)}), bf16[8,272,128]{2,1,0:T(8,128)(2,1)S(1)}, u32[]{:S(2)}, u32[]{:S(2)}) async-start(bf16[8,272,128]{2,1,0:T(8,128)(2,1)} %pack.1), calls=%async_computation | async-start | bytes 1114112 | tf_op jit(solution)/shard_map/all_to_all | solution.py:472
  11.3 0.7 pack_guide.1
  12.0 1.3 %collective-permute-start = (bf16[3,128,128]{2,1,0:T(8,128)(2,1)S(1)}, bf16[3,128,128]{2,1,0:T(8,128)(2,1)S(1)}, u32[]{:S(2)}, u32[]{:S(2)}) collective-permute-start(bf16[3,128,128]{2,1,0:T(8,128)(2,1)S(1)} %get-tuple-element.20.guide_own), channel_id=1, source_target_pairs={{1,0},{3,2},{5,4},{7,6},{9,8},{11,10},{13,12},{15,14},{17,16},{19,... | collective-permute-start | bytes 294920 | tf_op jit(solution)/shard_map/ppermute | solution.py:469
  13.3 1.3 %collective-permute-start.2 = (bf16[3,128,128]{2,1,0:T(8,128)(2,1)S(1)}, bf16[3,128,128]{2,1,0:T(8,128)(2,1)S(1)}, u32[]{:S(2)}, u32[]{:S(2)}) collective-permute-start(bf16[3,128,128]{2,1,0:T(8,128)(2,1)S(1)} %get-tuple-element.21), channel_id=1, source_target_pairs={{1,2},{3,0},{5,6},{7,4},{9,10},{11,8},{13,14},{15,12},{17,18},{19,... | collective-permute-start | bytes 294920 | tf_op jit(solution)/shard_map/ppermute | solution.py:471
  14.6 7.8 %collective-permute-start.1 = (bf16[3,128,128]{2,1,0:T(8,128)(2,1)S(1)}, bf16[3,128,128]{2,1,0:T(8,128)(2,1)S(1)}, u32[]{:S(2)}, u32[]{:S(2)}) collective-permute-start(bf16[3,128,128]{2,1,0:T(8,128)(2,1)S(1)} %get-tuple-element.21), channel_id=1, source_target_pairs={{0,2},{2,0},{4,6},{6,4},{8,10},{10,8},{12,14},{14,12},{16,18},{18,... | collective-permute-start | bytes 294920 | tf_op jit(solution)/shard_map/ppermute | solution.py:470
  23.1 0.2 copy.15.guide_head
  23.3 0.3 copy.14.main_head
  23.6 0.7 copy-done
  24.4 1.1 %prepare.1 = (bf16[2,128,64]{2,1,0:T(8,128)(2,1)S(1)}, f32[8,128]{1,0:T(8,128)S(1)}, f32[128,128]{1,0:T(8,128)S(1)}, f32[8,128]{1,0:T(8,128)S(1)}) custom-call(s32[1]{0:T(128)S(6)} %copy.16.step, s32[3]{0:T(128)S(1)} %pad_add_fusion.place, bf16[50,2,2560]{2,1,0:T(2,128)(2,1)S(1)} %copy-done, bf16[50,2,1024]{2,1,0:T(2,128)(2,1)S(1)} %copy-done.1, ...), custom_call_target="tpu_custom_call" | custom-call | tf_op jit(solution)/shard_map/prepare/pallas_call | solution.py:446
  25.4 8.1 %collective-permute-done.2.guide_across = bf16[3,128,128]{2,1,0:T(8,128)(2,1)S(1)} collective-permute-done((bf16[3,128,128]{2,1,0:T(8,128)(2,1)S(1)}, bf16[3,128,128]{2,1,0:T(8,128)(2,1)S(1)}, u32[]{:S(2)}, u32[]{:S(2)}) %collective-permute-start.2) | collective-permute-done | bytes 98336 | tf_op jit(solution)/shard_map/ppermute | solution.py:471
  33.6 0.1 collective-permute-done.1.guide_half
  33.7 2.0 %collective-permute-done.3.sibling = bf16[8,272,128]{2,1,0:T(8,128)(2,1)S(1)} collective-permute-done((bf16[8,272,128]{2,1,0:T(8,128)(2,1)S(1)}, bf16[8,272,128]{2,1,0:T(8,128)(2,1)S(1)}, u32[]{:S(2)}, u32[]{:S(2)}) %collective-permute-start.3) | collective-permute-done | bytes 557088 | tf_op jit(solution)/shard_map/ppermute | solution.py:478
  35.6 0.6 unpack.1
  36.2 1.3 %collective-permute-start.6 = (bf16[4,512,128]{2,1,0:T(8,128)(2,1)S(1)}, bf16[4,512,128]{2,1,0:T(8,128)(2,1)S(1)}, u32[]{:S(2)}, u32[]{:S(2)}) collective-permute-start(bf16[4,512,128]{2,1,0:T(8,128)(2,1)S(1)} %get-tuple-element.33.refs_0_), channel_id=1, source_target_pairs={{0,8},{1,33},{4,12},{5,37},{8,0},{9,41},{12,4},{13,45},{16,24},{17... | collective-permute-start | bytes 1572872 | tf_op jit(solution)/shard_map/ppermute | solution.py:379
  37.6 2.2 %collective-permute-start.5 = (bf16[4,512,128]{2,1,0:T(8,128)(2,1)S(1)}, bf16[4,512,128]{2,1,0:T(8,128)(2,1)S(1)}, u32[]{:S(2)}, u32[]{:S(2)}) collective-permute-start(bf16[4,512,128]{2,1,0:T(8,128)(2,1)S(1)} %get-tuple-element.33.refs_0_), channel_id=1, source_target_pairs={{0,4},{1,17},{4,8},{5,21},{8,12},{9,25},{12,0},{13,29},{16,20},{17... | collective-permute-start | bytes 1572872 | tf_op jit(solution)/shard_map/ppermute | solution.py:379
  39.8 2.8 %collective-permute-start.7 = (bf16[1024,128]{1,0:T(8,128)(2,1)S(1)}, bf16[1024,128]{1,0:T(8,128)(2,1)S(1)}, u32[]{:S(2)}, u32[]{:S(2)}) collective-permute-start(bf16[1024,128]{1,0:T(8,128)(2,1)S(1)} %get-tuple-element.32.queries), channel_id=1, source_target_pairs={{0,48},{1,13},{4,52},{5,1},{8,56},{9,5},{12,60},{13,9},{16,0},{17,... | collective-permute-start | bytes 786440 | tf_op jit(solution)/shard_map/ppermute | solution.py:379
  42.5 9.0 %collective-permute-done.7.queries = bf16[1024,128]{1,0:T(8,128)(2,1)S(1)} collective-permute-done((bf16[1024,128]{1,0:T(8,128)(2,1)S(1)}, bf16[1024,128]{1,0:T(8,128)(2,1)S(1)}, u32[]{:S(2)}, u32[]{:S(2)}) %collective-permute-start.7) | collective-permute-done | bytes 262176 | tf_op jit(solution)/shard_map/ppermute | solution.py:379
  51.5 1.5 %collective-permute-start.11 = (bf16[1024,128]{1,0:T(8,128)(2,1)S(1)}, bf16[1024,128]{1,0:T(8,128)(2,1)S(1)}, u32[]{:S(2)}, u32[]{:S(2)}) collective-permute-start(bf16[1024,128]{1,0:T(8,128)(2,1)S(1)} %get-tuple-element.32.queries), channel_id=1, source_target_pairs={{0,32},{1,9},{4,36},{5,13},{8,40},{9,1},{12,44},{13,5},{16,48},{17... | collective-permute-start | bytes 786440 | tf_op jit(solution)/shard_map/ppermute | solution.py:379
  53.0 2.6 %collective-permute-done.4.refs_1_ = bf16[4,512,128]{2,1,0:T(8,128)(2,1)S(1)} collective-permute-done((bf16[4,512,128]{2,1,0:T(8,128)(2,1)S(1)}, bf16[4,512,128]{2,1,0:T(8,128)(2,1)S(1)}, u32[]{:S(2)}, u32[]{:S(2)}) %collective-permute-start.4) | collective-permute-done | bytes 524320 | tf_op jit(solution)/shard_map/ppermute | solution.py:379
  55.6 3.0 %attend.5 = bf16[1056,128]{1,0:T(8,128)(2,1)S(1)} custom-call(bf16[1024,128]{1,0:T(8,128)(2,1)S(1)} %collective-permute-done.7.queries, bf16[4,512,128]{2,1,0:T(8,128)(2,1)S(1)} %get-tuple-element.33.refs_0_, bf16[4,512,128]{2,1,0:T(8,128)(2,1)S(1)} %collective-permute-done.4.refs_1_, bf16[4,512,128]{2,1,0:T(8,128)(2,1)S(1)} %collective-permute-done.5.refs_2_, ...), custom_call_target="tpu_custom_call" | custom-call | flops 1073741824 | bytes 2097152 | tf_op jit(solution)/shard_map/attend/pallas_call | solution.py:387
  58.6 2.4 %collective-permute-start.8 = (bf16[1056,128]{1,0:T(8,128)(2,1)S(1)}, bf16[1056,128]{1,0:T(8,128)(2,1)S(1)}, u32[]{:S(2)}, u32[]{:S(2)}) collective-permute-start(bf16[1056,128]{1,0:T(8,128)(2,1)S(1)} %attend.5), channel_id=1, source_target_pairs={{0,16},{1,5},{4,20},{5,9},{8,24},{9,13},{12,28},{13,1},{16,32},{17... | collective-permute-start | bytes 811016 | tf_op jit(solution)/shard_map/ppermute | solution.py:379
  61.0 3.0 %attend.6 = bf16[1056,128]{1,0:T(8,128)(2,1)S(1)} custom-call(bf16[1024,128]{1,0:T(8,128)(2,1)S(1)} %collective-permute-done.9.queries, bf16[4,512,128]{2,1,0:T(8,128)(2,1)S(1)} %get-tuple-element.33.refs_0_, bf16[4,512,128]{2,1,0:T(8,128)(2,1)S(1)} %collective-permute-done.4.refs_1_, bf16[4,512,128]{2,1,0:T(8,128)(2,1)S(1)} %collective-permute-done.5.refs_2_, ...), custom_call_target="tpu_custom_call" | custom-call | flops 1073741824 | bytes 2097152 | tf_op jit(solution)/shard_map/attend/pallas_call | solution.py:387
  64.0 1.3 %collective-permute-start.10 = (bf16[1056,128]{1,0:T(8,128)(2,1)S(1)}, bf16[1056,128]{1,0:T(8,128)(2,1)S(1)}, u32[]{:S(2)}, u32[]{:S(2)}) collective-permute-start(bf16[1056,128]{1,0:T(8,128)(2,1)S(1)} %attend.6), channel_id=1, source_target_pairs={{0,48},{1,13},{4,52},{5,1},{8,56},{9,5},{12,60},{13,9},{16,0},{17,... | collective-permute-start | bytes 811016 | tf_op jit(solution)/shard_map/ppermute | solution.py:379
  65.3 3.0 %attend.7 = bf16[1056,128]{1,0:T(8,128)(2,1)S(1)} custom-call(bf16[1024,128]{1,0:T(8,128)(2,1)S(1)} %collective-permute-done.11.queries, bf16[4,512,128]{2,1,0:T(8,128)(2,1)S(1)} %get-tuple-element.33.refs_0_, bf16[4,512,128]{2,1,0:T(8,128)(2,1)S(1)} %collective-permute-done.4.refs_1_, bf16[4,512,128]{2,1,0:T(8,128)(2,1)S(1)} %collective-permute-done.5.refs_2_, ...), custom_call_target="tpu_custom_call" | custom-call | flops 1073741824 | bytes 2097152 | tf_op jit(solution)/shard_map/attend/pallas_call | solution.py:387
  68.3 2.0 %collective-permute-start.12 = (bf16[1056,128]{1,0:T(8,128)(2,1)S(1)}, bf16[1056,128]{1,0:T(8,128)(2,1)S(1)}, u32[]{:S(2)}, u32[]{:S(2)}) collective-permute-start(bf16[1056,128]{1,0:T(8,128)(2,1)S(1)} %attend.7), channel_id=1, source_target_pairs={{0,32},{1,9},{4,36},{5,13},{8,40},{9,1},{12,44},{13,5},{16,48},{17... | collective-permute-start | bytes 811016 | tf_op jit(solution)/shard_map/ppermute | solution.py:379
  70.3 3.0 %attend.4.refs_0_ = bf16[1056,128]{1,0:T(8,128)(2,1)S(1)} custom-call(bf16[1024,128]{1,0:T(8,128)(2,1)S(1)} %get-tuple-element.32.queries, bf16[4,512,128]{2,1,0:T(8,128)(2,1)S(1)} %get-tuple-element.33.refs_0_, bf16[4,512,128]{2,1,0:T(8,128)(2,1)S(1)} %collective-permute-done.4.refs_1_, bf16[4,512,128]{2,1,0:T(8,128)(2,1)S(1)} %collective-permute-done.5.refs_2_, ...), custom_call_target="tpu_custom_call" | custom-call | flops 1073741824 | bytes 2097152 | tf_op jit(solution)/shard_map/attend/pallas_call | solution.py:387
  73.3 0.7 merge.1
  74.0 2.3 %collective-permute-done.12.part = bf16[1056,128]{1,0:T(8,128)(2,1)S(1)} collective-permute-done((bf16[1056,128]{1,0:T(8,128)(2,1)S(1)}, bf16[1056,128]{1,0:T(8,128)(2,1)S(1)}, u32[]{:S(2)}, u32[]{:S(2)}) %collective-permute-start.12) | collective-permute-done | bytes 270368 | tf_op jit(solution)/shard_map/ppermute | solution.py:379
  76.4 1.5 %combine.1 = bf16[16,48,128]{2,1,0:T(8,128)(2,1)S(1)} custom-call(s32[3]{0:T(128)S(1)} %pad_add_fusion.place, bf16[2,128,64]{2,1,0:T(8,128)(2,1)S(1)} %get-tuple-element.26.weights, f32[8,128]{1,0:T(8,128)S(1)} %get-tuple-element.27.scales, f32[1024,128]{1,0:T(8,128)S(1)} %get-tuple-element.34.former, f32[8,128]{1,0:T(8,128)S(1)} %get-tuple-element.35.former_level, ...), custom_call_target="tpu_custom_call" | custom-call | tf_op jit(solution)/shard_map/combine/pallas_call | solution.py:499
  77.9 11.8 %all_to_all.10.got = bf16[16,48,128]{2,1,0:T(8,128)(2,1)S(1)} all-to-all(bf16[16,48,128]{2,1,0:T(8,128)(2,1)S(1)} %combine.1), channel_id=1, replica_groups=mesh['zl'=4,'x'=4,'y'=4,'zh'=2,'core'=2] {'core','zh','zl'}, dimensions={0} | all-to-all | bytes 393216 | tf_op jit(solution)/shard_map/all_to_all | solution.py:507
  89.7 1.7 %final.1 = (f32[1,32,64]{2,1,0:T(8,128)}, f32[1,32,64]{2,1,0:T(8,128)}) custom-call(s32[1]{0:T(128)S(6)} %copy.16.step, s32[3]{0:T(128)S(1)} %pad_add_fusion.place, bf16[16,48,128]{2,1,0:T(8,128)(2,1)S(1)} %all_to_all.10.got, f32[128,128]{1,0:T(8,128)S(1)} %get-tuple-element.36.means, f32[8,128]{1,0:T(8,128)S(1)} %get-tuple-element.37.shifts, ...), custom_call_target="tpu_custom_call" | custom-call | tf_op jit(solution)/shard_map/final/pallas_call | solution.py:508
  (27 shorter events, 0.3 us)
Async XLA Ops:
  2.6 8.7 %copy-start.2 = (bf16[1,128,256]{2,1,0:T(8,128)(2,1)S(1)}, bf16[1,128,256]{2,1,0:T(8,128)(2,1)}, u32[]{:S(2)}) copy-start(bf16[1,128,256]{2,1,0:T(8,128)(2,1)} %gq.1) | copy-start | bytes 196612
  2.6 8.7 %copy-start.3 = (bf16[1,128,256]{2,1,0:T(8,128)(2,1)S(1)}, bf16[1,128,256]{2,1,0:T(8,128)(2,1)}, u32[]{:S(2)}) copy-start(bf16[1,128,256]{2,1,0:T(8,128)(2,1)} %gk.1) | copy-start | bytes 196612
  2.6 8.7 %copy-start.4 = (bf16[1,128,256]{2,1,0:T(8,128)(2,1)S(1)}, bf16[1,128,256]{2,1,0:T(8,128)(2,1)}, u32[]{:S(2)}) copy-start(bf16[1,128,256]{2,1,0:T(8,128)(2,1)} %gv.1) | copy-start | bytes 196612
  2.6 20.5 %copy-start.7 = (bf16[1024,64]{0,1:T(8,128)(2,1)S(1)}, bf16[1024,64]{0,1:T(8,128)(2,1)}, u32[]{:S(2)}) copy-start(bf16[1024,64]{0,1:T(8,128)(2,1)} %param.23) | copy-start | bytes 393220
  2.6 31.0 %all-to-all-start = ((bf16[8,272,128]{2,1,0:T(8,128)(2,1)}), bf16[8,272,128]{2,1,0:T(8,128)(2,1)S(1)}, u32[]{:S(2)}, u32[]{:S(2)}) async-start(bf16[8,272,128]{2,1,0:T(8,128)(2,1)} %pack.1), calls=%async_computation | async-start | bytes 1114112 | tf_op jit(solution)/shard_map/all_to_all | solution.py:472
  11.2 12.0 %copy-start.6 = (bf16[2560,64]{0,1:T(8,128)(2,1)S(1)}, bf16[2560,64]{0,1:T(8,128)(2,1)}, u32[]{:S(2)}) copy-start(bf16[2560,64]{0,1:T(8,128)(2,1)} %param.22) | copy-start | bytes 983044
  12.0 13.4 %collective-permute-start = (bf16[3,128,128]{2,1,0:T(8,128)(2,1)S(1)}, bf16[3,128,128]{2,1,0:T(8,128)(2,1)S(1)}, u32[]{:S(2)}, u32[]{:S(2)}) collective-permute-start(bf16[3,128,128]{2,1,0:T(8,128)(2,1)S(1)} %get-tuple-element.20.guide_own), channel_id=1, source_target_pairs={{1,0},{3,2},{5,4},{7,6},{9,8},{11,10},{13,12},{15,14},{17,16},{19,... | collective-permute-start | bytes 294920 | tf_op jit(solution)/shard_map/ppermute | solution.py:469
  13.3 20.3 %collective-permute-start.2 = (bf16[3,128,128]{2,1,0:T(8,128)(2,1)S(1)}, bf16[3,128,128]{2,1,0:T(8,128)(2,1)S(1)}, u32[]{:S(2)}, u32[]{:S(2)}) collective-permute-start(bf16[3,128,128]{2,1,0:T(8,128)(2,1)S(1)} %get-tuple-element.21), channel_id=1, source_target_pairs={{1,2},{3,0},{5,6},{7,4},{9,10},{11,8},{13,14},{15,12},{17,18},{19,... | collective-permute-start | bytes 294920 | tf_op jit(solution)/shard_map/ppermute | solution.py:471
  14.6 19.1 %collective-permute-start.1 = (bf16[3,128,128]{2,1,0:T(8,128)(2,1)S(1)}, bf16[3,128,128]{2,1,0:T(8,128)(2,1)S(1)}, u32[]{:S(2)}, u32[]{:S(2)}) collective-permute-start(bf16[3,128,128]{2,1,0:T(8,128)(2,1)S(1)} %get-tuple-element.21), channel_id=1, source_target_pairs={{0,2},{2,0},{4,6},{6,4},{8,10},{10,8},{12,14},{14,12},{16,18},{18,... | collective-permute-start | bytes 294920 | tf_op jit(solution)/shard_map/ppermute | solution.py:470
  23.3 1.0 %copy-start = (bf16[50,2,2560]{2,1,0:T(2,128)(2,1)S(1)}, bf16[50,2,2560]{2,1,0:T(2,128)(2,1)}, u32[]{:S(2)}) copy-start(bf16[50,2,2560]{2,1,0:T(2,128)(2,1)} %main_mod.1) | copy-start | bytes 1536004
  23.3 1.1 %copy-start.1 = (bf16[50,2,1024]{2,1,0:T(2,128)(2,1)S(1)}, bf16[50,2,1024]{2,1,0:T(2,128)(2,1)}, u32[]{:S(2)}) copy-start(bf16[50,2,1024]{2,1,0:T(2,128)(2,1)} %guide_mod.1) | copy-start | bytes 614404
  33.7 2.0 %collective-permute-start.3 = (bf16[8,272,128]{2,1,0:T(8,128)(2,1)S(1)}, bf16[8,272,128]{2,1,0:T(8,128)(2,1)S(1)}, u32[]{:S(2)}, u32[]{:S(2)}) collective-permute-start(bf16[8,272,128]{2,1,0:T(8,128)(2,1)S(1)} %all-to-all-done.got), channel_id=1, source_target_pairs={{0,1},{1,0},{2,3},{3,2},{4,5},{5,4},{6,7},{7,6},{8,9},{9,8},{10,11... | collective-permute-start | bytes 1671176 | tf_op jit(solution)/shard_map/ppermute | solution.py:478
  36.2 16.7 %collective-permute-start.6 = (bf16[4,512,128]{2,1,0:T(8,128)(2,1)S(1)}, bf16[4,512,128]{2,1,0:T(8,128)(2,1)S(1)}, u32[]{:S(2)}, u32[]{:S(2)}) collective-permute-start(bf16[4,512,128]{2,1,0:T(8,128)(2,1)S(1)} %get-tuple-element.33.refs_0_), channel_id=1, source_target_pairs={{0,8},{1,33},{4,12},{5,37},{8,0},{9,41},{12,4},{13,45},{16,24},{17... | collective-permute-start | bytes 1572872 | tf_op jit(solution)/shard_map/ppermute | solution.py:379
  37.6 15.5 %collective-permute-start.5 = (bf16[4,512,128]{2,1,0:T(8,128)(2,1)S(1)}, bf16[4,512,128]{2,1,0:T(8,128)(2,1)S(1)}, u32[]{:S(2)}, u32[]{:S(2)}) collective-permute-start(bf16[4,512,128]{2,1,0:T(8,128)(2,1)S(1)} %get-tuple-element.33.refs_0_), channel_id=1, source_target_pairs={{0,4},{1,17},{4,8},{5,21},{8,12},{9,25},{12,0},{13,29},{16,20},{17... | collective-permute-start | bytes 1572872 | tf_op jit(solution)/shard_map/ppermute | solution.py:379
  39.7 15.8 %collective-permute-start.4 = (bf16[4,512,128]{2,1,0:T(8,128)(2,1)S(1)}, bf16[4,512,128]{2,1,0:T(8,128)(2,1)S(1)}, u32[]{:S(2)}, u32[]{:S(2)}) collective-permute-start(bf16[4,512,128]{2,1,0:T(8,128)(2,1)S(1)} %get-tuple-element.33.refs_0_), channel_id=1, source_target_pairs={{0,12},{1,49},{4,0},{5,53},{8,4},{9,57},{12,8},{13,61},{16,28},{17... | collective-permute-start | bytes 1572872 | tf_op jit(solution)/shard_map/ppermute | solution.py:379
  39.8 11.8 %collective-permute-start.7 = (bf16[1024,128]{1,0:T(8,128)(2,1)S(1)}, bf16[1024,128]{1,0:T(8,128)(2,1)S(1)}, u32[]{:S(2)}, u32[]{:S(2)}) collective-permute-start(bf16[1024,128]{1,0:T(8,128)(2,1)S(1)} %get-tuple-element.32.queries), channel_id=1, source_target_pairs={{0,48},{1,13},{4,52},{5,1},{8,56},{9,5},{12,60},{13,9},{16,0},{17,... | collective-permute-start | bytes 786440 | tf_op jit(solution)/shard_map/ppermute | solution.py:379
  42.5 18.5 %collective-permute-start.9 = (bf16[1024,128]{1,0:T(8,128)(2,1)S(1)}, bf16[1024,128]{1,0:T(8,128)(2,1)S(1)}, u32[]{:S(2)}, u32[]{:S(2)}) collective-permute-start(bf16[1024,128]{1,0:T(8,128)(2,1)S(1)} %get-tuple-element.32.queries), channel_id=1, source_target_pairs={{0,16},{1,5},{4,20},{5,9},{8,24},{9,13},{12,28},{13,1},{16,32},{17... | collective-permute-start | bytes 786440 | tf_op jit(solution)/shard_map/ppermute | solution.py:379
  51.5 13.8 %collective-permute-start.11 = (bf16[1024,128]{1,0:T(8,128)(2,1)S(1)}, bf16[1024,128]{1,0:T(8,128)(2,1)S(1)}, u32[]{:S(2)}, u32[]{:S(2)}) collective-permute-start(bf16[1024,128]{1,0:T(8,128)(2,1)S(1)} %get-tuple-element.32.queries), channel_id=1, source_target_pairs={{0,32},{1,9},{4,36},{5,13},{8,40},{9,1},{12,44},{13,5},{16,48},{17... | collective-permute-start | bytes 786440 | tf_op jit(solution)/shard_map/ppermute | solution.py:379
  58.6 14.7 %collective-permute-start.8 = (bf16[1056,128]{1,0:T(8,128)(2,1)S(1)}, bf16[1056,128]{1,0:T(8,128)(2,1)S(1)}, u32[]{:S(2)}, u32[]{:S(2)}) collective-permute-start(bf16[1056,128]{1,0:T(8,128)(2,1)S(1)} %attend.5), channel_id=1, source_target_pairs={{0,16},{1,5},{4,20},{5,9},{8,24},{9,13},{12,28},{13,1},{16,32},{17... | collective-permute-start | bytes 811016 | tf_op jit(solution)/shard_map/ppermute | solution.py:379
  64.0 9.4 %collective-permute-start.10 = (bf16[1056,128]{1,0:T(8,128)(2,1)S(1)}, bf16[1056,128]{1,0:T(8,128)(2,1)S(1)}, u32[]{:S(2)}, u32[]{:S(2)}) collective-permute-start(bf16[1056,128]{1,0:T(8,128)(2,1)S(1)} %attend.6), channel_id=1, source_target_pairs={{0,48},{1,13},{4,52},{5,1},{8,56},{9,5},{12,60},{13,9},{16,0},{17,... | collective-permute-start | bytes 811016 | tf_op jit(solution)/shard_map/ppermute | solution.py:379
  68.3 8.0 %collective-permute-start.12 = (bf16[1056,128]{1,0:T(8,128)(2,1)S(1)}, bf16[1056,128]{1,0:T(8,128)(2,1)S(1)}, u32[]{:S(2)}, u32[]{:S(2)}) collective-permute-start(bf16[1056,128]{1,0:T(8,128)(2,1)S(1)} %attend.7), channel_id=1, source_target_pairs={{0,32},{1,9},{4,36},{5,13},{8,40},{9,1},{12,44},{13,5},{16,48},{17... | collective-permute-start | bytes 811016 | tf_op jit(solution)/shard_map/ppermute | solution.py:379
  77.9 11.8 %copy-start.5 = (f32[1,32,64]{2,1,0:T(8,128)S(1)}, f32[1,32,64]{2,1,0:T(8,128)}, u32[]{:S(2)}) copy-start(f32[1,32,64]{2,1,0:T(8,128)} %latents.1) | copy-start | bytes 24580

commit v7 on v6

--- a/solution.py
+++ b/solution.py
@@ -211,7 +211,8 @@
         scales[1:2, :] = 1.0 + main_mod[0, :, shared][1:2].astype(f32)
 
     def rows_of(table, order):
-        shift, scale = table[0, 0:1, :].astype(f32), 1.0 + table[0, 1:2, :].astype(f32)
+        both = table[0].astype(f32)
+        shift, scale = both[0:1], 1.0 + both[1:2]
         owner = lax.broadcasted_iota(jnp.int32, scale.shape, 1) >> 7
         rows = [jnp.where(owner == head, scale, 0.0) for head in order] + [shift]
         rows += [jnp.zeros_like(shift)] * (-len(rows) % 8)
@@ -295,13 +296,17 @@
                 jnp.sum(jnp.where(on_diagonal, value[rows], 0.0), axis=0, keepdims=True)
                 for value in (mean, square)
             ]
-            stats.append(terms(jnp.concatenate(both, axis=0)))
-
+            both = jnp.concatenate(both, axis=0)
+            high = both.astype(bf16).astype(f32)
+            middle = (both - high).astype(bf16).astype(f32)
+            stats.append((jnp.concatenate([high, middle], axis=0), both - high - middle))
+
+    gap = jnp.zeros((2, HD), f32)
     for tile in range(blocks):
         other = blocks + tile
         rows = jnp.concatenate([flows[tile], flows[other]], axis=1)
         both = jnp.concatenate(
-            [stats[tile].astype(f32), stats[other].astype(f32), jnp.zeros((8, HD), f32)],
+            [stats[tile][0], stats[other][0], stats[tile][1], gap, stats[other][1], gap],
             axis=0,
         ).astype(bf16)
         for zl in range(ZL):
@@ -329,8 +334,9 @@
 
     table = []
     for source in range(CORE * Z):
-        block = got[source, ROWS : ROWS + 16, :].astype(f32)[:8]
-        table.append(block + jnp.concatenate([block[2:], block[:2]], axis=0))
+        block = got[source, ROWS : ROWS + 16, :].astype(f32)
+        high = block[:8]
+        table.append(high + jnp.concatenate([high[2:], high[:2]], axis=0) + block[8:])
     table = jnp.concatenate(table, axis=0)
     row = lax.broadcasted_iota(jnp.int32, (HD, HD), 0)
     kind, source = row & 7, row >> 3

time: 92.5 us -> 92.5 us (level)
  no operation moved by 1% of the time
where the time goes in v7:
time: 92.5 us; the launch traced here: 91.4 us
  starting transfers between devices  32.5 us (35%)
  waiting for transfers between devices  24.2 us (26%)
  Pallas kernels  20.2 us (22%)
  blocking collectives  11.8 us (13%)
  between operations  1.46 us (2%)
  local copies, waits for them, and re-layouts  1.27 us (1%)
    ppermute x9, waiting for transfers between devices, plane_shift(): return lax.ppermute(array, ('x', 'y', 'core'), pairs)  14 us
    ppermute x9, starting transfers between devices, plane_shift(): return lax.ppermute(array, ('x', 'y', 'core'), pairs)  13.5 us
    pallas_call x4, Pallas kernels, attend(): pl.pallas_call(attend_kernel, out_shape=shape(rows + STAT, HD), in_specs=...  12 us
    all_to_all x1, blocking collectives, on_device(): lax.all_to_all(send, ('core', 'zh', 'zl'), split_axis=0, concat_axis=0, t...  11.8 us
    all_to_all x1, starting transfers between devices, on_device(): lax.all_to_all(send, ('zh', 'zl'), split_axis=0, concat_axis=0, tiled=True)  8.61 us
    ppermute x1, waiting for transfers between devices, on_device(): guide_across = lax.ppermute(guide_send, halves, [(1, 2), (3, 0)])  8.11 us
    ppermute x1, starting transfers between devices, on_device(): guide_half = lax.ppermute(guide_send, halves, [(0, 2), (2, 0)])  7.83 us
    ppermute x1, waiting for transfers between devices, on_device(): sibling = lax.ppermute(got, 'core', [(0, 1), (1, 0)])  1.96 us
  transfers between devices with their start and end apart: 14, of which 7 were waited for; matrix products, arithmetic and copies ran while one was open for 1% of the time, Pallas kernels for 16%

profile of v7, /device:TPU:24, one launch (start us, length us, event | category | flops | bytes accessed | tf_op | source)
XLA Modules:
  0.0 91.4 jit_solution(13323300125431101794)
XLA Ops:
  0.6 1.9 %pack.1 = bf16[8,272,128]{2,1,0:T(8,128)(2,1)} custom-call(bf16[1,32,2560]{2,1,0:T(8,128)(2,1)} %mq.1, bf16[1,32,2560]{2,1,0:T(8,128)(2,1)} %mk.1, bf16[1,32,2560]{2,1,0:T(8,128)(2,1)} %mv.1), custom_call_target="tpu_custom_call" | custom-call | tf_op jit(solution)/shard_map/pack/pallas_call | solution.py:438
  2.6 8.6 %all-to-all-start = ((bf16[8,272,128]{2,1,0:T(8,128)(2,1)}), bf16[8,272,128]{2,1,0:T(8,128)(2,1)S(1)}, u32[]{:S(2)}, u32[]{:S(2)}) async-start(bf16[8,272,128]{2,1,0:T(8,128)(2,1)} %pack.1), calls=%async_computation | async-start | bytes 1114112 | tf_op jit(solution)/shard_map/all_to_all | solution.py:478
  11.3 0.7 pack_guide.1
  12.0 1.3 %collective-permute-start = (bf16[3,128,128]{2,1,0:T(8,128)(2,1)S(1)}, bf16[3,128,128]{2,1,0:T(8,128)(2,1)S(1)}, u32[]{:S(2)}, u32[]{:S(2)}) collective-permute-start(bf16[3,128,128]{2,1,0:T(8,128)(2,1)S(1)} %get-tuple-element.20.guide_own), channel_id=1, source_target_pairs={{1,0},{3,2},{5,4},{7,6},{9,8},{11,10},{13,12},{15,14},{17,16},{19,... | collective-permute-start | bytes 294920 | tf_op jit(solution)/shard_map/ppermute | solution.py:475
  13.3 1.3 %collective-permute-start.2 = (bf16[3,128,128]{2,1,0:T(8,128)(2,1)S(1)}, bf16[3,128,128]{2,1,0:T(8,128)(2,1)S(1)}, u32[]{:S(2)}, u32[]{:S(2)}) collective-permute-start(bf16[3,128,128]{2,1,0:T(8,128)(2,1)S(1)} %get-tuple-element.21), channel_id=1, source_target_pairs={{1,2},{3,0},{5,6},{7,4},{9,10},{11,8},{13,14},{15,12},{17,18},{19,... | collective-permute-start | bytes 294920 | tf_op jit(solution)/shard_map/ppermute | solution.py:477
  14.6 7.8 %collective-permute-start.1 = (bf16[3,128,128]{2,1,0:T(8,128)(2,1)S(1)}, bf16[3,128,128]{2,1,0:T(8,128)(2,1)S(1)}, u32[]{:S(2)}, u32[]{:S(2)}) collective-permute-start(bf16[3,128,128]{2,1,0:T(8,128)(2,1)S(1)} %get-tuple-element.21), channel_id=1, source_target_pairs={{0,2},{2,0},{4,6},{6,4},{8,10},{10,8},{12,14},{14,12},{16,18},{18,... | collective-permute-start | bytes 294920 | tf_op jit(solution)/shard_map/ppermute | solution.py:476
  23.1 0.2 copy.15.guide_head
  23.3 0.3 copy.14.main_head
  23.6 0.7 copy-done
  24.4 1.1 %prepare.1 = (bf16[2,128,64]{2,1,0:T(8,128)(2,1)S(1)}, f32[8,128]{1,0:T(8,128)S(1)}, f32[128,128]{1,0:T(8,128)S(1)}, f32[8,128]{1,0:T(8,128)S(1)}) custom-call(s32[1]{0:T(128)S(6)} %copy.16.step, s32[3]{0:T(128)S(1)} %pad_add_fusion.place, bf16[50,2,2560]{2,1,0:T(2,128)(2,1)S(1)} %copy-done, bf16[50,2,1024]{2,1,0:T(2,128)(2,1)S(1)} %copy-done.1, ...), custom_call_target="tpu_custom_call" | custom-call | tf_op jit(solution)/shard_map/prepare/pallas_call | solution.py:452
  25.4 8.1 %collective-permute-done.2.guide_across = bf16[3,128,128]{2,1,0:T(8,128)(2,1)S(1)} collective-permute-done((bf16[3,128,128]{2,1,0:T(8,128)(2,1)S(1)}, bf16[3,128,128]{2,1,0:T(8,128)(2,1)S(1)}, u32[]{:S(2)}, u32[]{:S(2)}) %collective-permute-start.2) | collective-permute-done | bytes 98336 | tf_op jit(solution)/shard_map/ppermute | solution.py:477
  33.6 0.1 collective-permute-done.1.guide_half
  33.7 2.0 %collective-permute-done.3.sibling = bf16[8,272,128]{2,1,0:T(8,128)(2,1)S(1)} collective-permute-done((bf16[8,272,128]{2,1,0:T(8,128)(2,1)S(1)}, bf16[8,272,128]{2,1,0:T(8,128)(2,1)S(1)}, u32[]{:S(2)}, u32[]{:S(2)}) %collective-permute-start.3) | collective-permute-done | bytes 557088 | tf_op jit(solution)/shard_map/ppermute | solution.py:484
  35.6 0.6 unpack.1
  36.2 1.3 %collective-permute-start.6 = (bf16[4,512,128]{2,1,0:T(8,128)(2,1)S(1)}, bf16[4,512,128]{2,1,0:T(8,128)(2,1)S(1)}, u32[]{:S(2)}, u32[]{:S(2)}) collective-permute-start(bf16[4,512,128]{2,1,0:T(8,128)(2,1)S(1)} %get-tuple-element.33.refs_0_), channel_id=1, source_target_pairs={{0,8},{1,33},{4,12},{5,37},{8,0},{9,41},{12,4},{13,45},{16,24},{17... | collective-permute-start | bytes 1572872 | tf_op jit(solution)/shard_map/ppermute | solution.py:385
  37.6 2.2 %collective-permute-start.5 = (bf16[4,512,128]{2,1,0:T(8,128)(2,1)S(1)}, bf16[4,512,128]{2,1,0:T(8,128)(2,1)S(1)}, u32[]{:S(2)}, u32[]{:S(2)}) collective-permute-start(bf16[4,512,128]{2,1,0:T(8,128)(2,1)S(1)} %get-tuple-element.33.refs_0_), channel_id=1, source_target_pairs={{0,4},{1,17},{4,8},{5,21},{8,12},{9,25},{12,0},{13,29},{16,20},{17... | collective-permute-start | bytes 1572872 | tf_op jit(solution)/shard_map/ppermute | solution.py:385
  39.8 2.8 %collective-permute-start.7 = (bf16[1024,128]{1,0:T(8,128)(2,1)S(1)}, bf16[1024,128]{1,0:T(8,128)(2,1)S(1)}, u32[]{:S(2)}, u32[]{:S(2)}) collective-permute-start(bf16[1024,128]{1,0:T(8,128)(2,1)S(1)} %get-tuple-element.32.queries), channel_id=1, source_target_pairs={{0,48},{1,13},{4,52},{5,1},{8,56},{9,5},{12,60},{13,9},{16,0},{17,... | collective-permute-start | bytes 786440 | tf_op jit(solution)/shard_map/ppermute | solution.py:385
  42.5 9.0 %collective-permute-done.7.queries = bf16[1024,128]{1,0:T(8,128)(2,1)S(1)} collective-permute-done((bf16[1024,128]{1,0:T(8,128)(2,1)S(1)}, bf16[1024,128]{1,0:T(8,128)(2,1)S(1)}, u32[]{:S(2)}, u32[]{:S(2)}) %collective-permute-start.7) | collective-permute-done | bytes 262176 | tf_op jit(solution)/shard_map/ppermute | solution.py:385
  51.5 1.5 %collective-permute-start.11 = (bf16[1024,128]{1,0:T(8,128)(2,1)S(1)}, bf16[1024,128]{1,0:T(8,128)(2,1)S(1)}, u32[]{:S(2)}, u32[]{:S(2)}) collective-permute-start(bf16[1024,128]{1,0:T(8,128)(2,1)S(1)} %get-tuple-element.32.queries), channel_id=1, source_target_pairs={{0,32},{1,9},{4,36},{5,13},{8,40},{9,1},{12,44},{13,5},{16,48},{17... | collective-permute-start | bytes 786440 | tf_op jit(solution)/shard_map/ppermute | solution.py:385
  53.0 2.6 %collective-permute-done.4.refs_1_ = bf16[4,512,128]{2,1,0:T(8,128)(2,1)S(1)} collective-permute-done((bf16[4,512,128]{2,1,0:T(8,128)(2,1)S(1)}, bf16[4,512,128]{2,1,0:T(8,128)(2,1)S(1)}, u32[]{:S(2)}, u32[]{:S(2)}) %collective-permute-start.4) | collective-permute-done | bytes 524320 | tf_op jit(solution)/shard_map/ppermute | solution.py:385
  55.6 3.0 %attend.5 = bf16[1056,128]{1,0:T(8,128)(2,1)S(1)} custom-call(bf16[1024,128]{1,0:T(8,128)(2,1)S(1)} %collective-permute-done.7.queries, bf16[4,512,128]{2,1,0:T(8,128)(2,1)S(1)} %get-tuple-element.33.refs_0_, bf16[4,512,128]{2,1,0:T(8,128)(2,1)S(1)} %collective-permute-done.4.refs_1_, bf16[4,512,128]{2,1,0:T(8,128)(2,1)S(1)} %collective-permute-done.5.refs_2_, ...), custom_call_target="tpu_custom_call" | custom-call | flops 1073741824 | bytes 2097152 | tf_op jit(solution)/shard_map/attend/pallas_call | solution.py:393
  58.6 2.4 %collective-permute-start.8 = (bf16[1056,128]{1,0:T(8,128)(2,1)S(1)}, bf16[1056,128]{1,0:T(8,128)(2,1)S(1)}, u32[]{:S(2)}, u32[]{:S(2)}) collective-permute-start(bf16[1056,128]{1,0:T(8,128)(2,1)S(1)} %attend.5), channel_id=1, source_target_pairs={{0,16},{1,5},{4,20},{5,9},{8,24},{9,13},{12,28},{13,1},{16,32},{17... | collective-permute-start | bytes 811016 | tf_op jit(solution)/shard_map/ppermute | solution.py:385
  61.0 3.0 %attend.6 = bf16[1056,128]{1,0:T(8,128)(2,1)S(1)} custom-call(bf16[1024,128]{1,0:T(8,128)(2,1)S(1)} %collective-permute-done.9.queries, bf16[4,512,128]{2,1,0:T(8,128)(2,1)S(1)} %get-tuple-element.33.refs_0_, bf16[4,512,128]{2,1,0:T(8,128)(2,1)S(1)} %collective-permute-done.4.refs_1_, bf16[4,512,128]{2,1,0:T(8,128)(2,1)S(1)} %collective-permute-done.5.refs_2_, ...), custom_call_target="tpu_custom_call" | custom-call | flops 1073741824 | bytes 2097152 | tf_op jit(solution)/shard_map/attend/pallas_call | solution.py:393
  64.0 1.3 %collective-permute-start.10 = (bf16[1056,128]{1,0:T(8,128)(2,1)S(1)}, bf16[1056,128]{1,0:T(8,128)(2,1)S(1)}, u32[]{:S(2)}, u32[]{:S(2)}) collective-permute-start(bf16[1056,128]{1,0:T(8,128)(2,1)S(1)} %attend.6), channel_id=1, source_target_pairs={{0,48},{1,13},{4,52},{5,1},{8,56},{9,5},{12,60},{13,9},{16,0},{17,... | collective-permute-start | bytes 811016 | tf_op jit(solution)/shard_map/ppermute | solution.py:385
  65.3 3.0 %attend.7 = bf16[1056,128]{1,0:T(8,128)(2,1)S(1)} custom-call(bf16[1024,128]{1,0:T(8,128)(2,1)S(1)} %collective-permute-done.11.queries, bf16[4,512,128]{2,1,0:T(8,128)(2,1)S(1)} %get-tuple-element.33.refs_0_, bf16[4,512,128]{2,1,0:T(8,128)(2,1)S(1)} %collective-permute-done.4.refs_1_, bf16[4,512,128]{2,1,0:T(8,128)(2,1)S(1)} %collective-permute-done.5.refs_2_, ...), custom_call_target="tpu_custom_call" | custom-call | flops 1073741824 | bytes 2097152 | tf_op jit(solution)/shard_map/attend/pallas_call | solution.py:393
  68.3 2.0 %collective-permute-start.12 = (bf16[1056,128]{1,0:T(8,128)(2,1)S(1)}, bf16[1056,128]{1,0:T(8,128)(2,1)S(1)}, u32[]{:S(2)}, u32[]{:S(2)}) collective-permute-start(bf16[1056,128]{1,0:T(8,128)(2,1)S(1)} %attend.7), channel_id=1, source_target_pairs={{0,32},{1,9},{4,36},{5,13},{8,40},{9,1},{12,44},{13,5},{16,48},{17... | collective-permute-start | bytes 811016 | tf_op jit(solution)/shard_map/ppermute | solution.py:385
  70.3 3.0 %attend.4.refs_0_ = bf16[1056,128]{1,0:T(8,128)(2,1)S(1)} custom-call(bf16[1024,128]{1,0:T(8,128)(2,1)S(1)} %get-tuple-element.32.queries, bf16[4,512,128]{2,1,0:T(8,128)(2,1)S(1)} %get-tuple-element.33.refs_0_, bf16[4,512,128]{2,1,0:T(8,128)(2,1)S(1)} %collective-permute-done.4.refs_1_, bf16[4,512,128]{2,1,0:T(8,128)(2,1)S(1)} %collective-permute-done.5.refs_2_, ...), custom_call_target="tpu_custom_call" | custom-call | flops 1073741824 | bytes 2097152 | tf_op jit(solution)/shard_map/attend/pallas_call | solution.py:393
  73.3 0.7 merge.1
  74.0 2.3 %collective-permute-done.12.part = bf16[1056,128]{1,0:T(8,128)(2,1)S(1)} collective-permute-done((bf16[1056,128]{1,0:T(8,128)(2,1)S(1)}, bf16[1056,128]{1,0:T(8,128)(2,1)S(1)}, u32[]{:S(2)}, u32[]{:S(2)}) %collective-permute-start.12) | collective-permute-done | bytes 270368 | tf_op jit(solution)/shard_map/ppermute | solution.py:385
  76.4 1.5 %combine.1 = bf16[16,48,128]{2,1,0:T(8,128)(2,1)S(1)} custom-call(s32[3]{0:T(128)S(1)} %pad_add_fusion.place, bf16[2,128,64]{2,1,0:T(8,128)(2,1)S(1)} %get-tuple-element.26.weights, f32[8,128]{1,0:T(8,128)S(1)} %get-tuple-element.27.scales, f32[1024,128]{1,0:T(8,128)S(1)} %get-tuple-element.34.former, f32[8,128]{1,0:T(8,128)S(1)} %get-tuple-element.35.former_level, ...), custom_call_target="tpu_custom_call" | custom-call | tf_op jit(solution)/shard_map/combine/pallas_call | solution.py:505
  77.9 11.8 %all_to_all.10.got = bf16[16,48,128]{2,1,0:T(8,128)(2,1)S(1)} all-to-all(bf16[16,48,128]{2,1,0:T(8,128)(2,1)S(1)} %combine.1), channel_id=1, replica_groups=mesh['zl'=4,'x'=4,'y'=4,'zh'=2,'core'=2] {'core','zh','zl'}, dimensions={0} | all-to-all | bytes 393216 | tf_op jit(solution)/shard_map/all_to_all | solution.py:513
  89.7 1.7 %final.1 = (f32[1,32,64]{2,1,0:T(8,128)}, f32[1,32,64]{2,1,0:T(8,128)}) custom-call(s32[1]{0:T(128)S(6)} %copy.16.step, s32[3]{0:T(128)S(1)} %pad_add_fusion.place, bf16[16,48,128]{2,1,0:T(8,128)(2,1)S(1)} %all_to_all.10.got, f32[128,128]{1,0:T(8,128)S(1)} %get-tuple-element.36.means, f32[8,128]{1,0:T(8,128)S(1)} %get-tuple-element.37.shifts, ...), custom_call_target="tpu_custom_call" | custom-call | tf_op jit(solution)/shard_map/final/pallas_call | solution.py:514
  (27 shorter events, 0.3 us)
Async XLA Ops:
  2.6 8.7 %copy-start.2 = (bf16[1,128,256]{2,1,0:T(8,128)(2,1)S(1)}, bf16[1,128,256]{2,1,0:T(8,128)(2,1)}, u32[]{:S(2)}) copy-start(bf16[1,128,256]{2,1,0:T(8,128)(2,1)} %gq.1) | copy-start | bytes 196612
  2.6 8.7 %copy-start.3 = (bf16[1,128,256]{2,1,0:T(8,128)(2,1)S(1)}, bf16[1,128,256]{2,1,0:T(8,128)(2,1)}, u32[]{:S(2)}) copy-start(bf16[1,128,256]{2,1,0:T(8,128)(2,1)} %gk.1) | copy-start | bytes 196612
  2.6 8.7 %copy-start.4 = (bf16[1,128,256]{2,1,0:T(8,128)(2,1)S(1)}, bf16[1,128,256]{2,1,0:T(8,128)(2,1)}, u32[]{:S(2)}) copy-start(bf16[1,128,256]{2,1,0:T(8,128)(2,1)} %gv.1) | copy-start | bytes 196612
  2.6 20.5 %copy-start.7 = (bf16[1024,64]{0,1:T(8,128)(2,1)S(1)}, bf16[1024,64]{0,1:T(8,128)(2,1)}, u32[]{:S(2)}) copy-start(bf16[1024,64]{0,1:T(8,128)(2,1)} %param.23) | copy-start | bytes 393220
  2.6 31.0 %all-to-all-start = ((bf16[8,272,128]{2,1,0:T(8,128)(2,1)}), bf16[8,272,128]{2,1,0:T(8,128)(2,1)S(1)}, u32[]{:S(2)}, u32[]{:S(2)}) async-start(bf16[8,272,128]{2,1,0:T(8,128)(2,1)} %pack.1), calls=%async_computation | async-start | bytes 1114112 | tf_op jit(solution)/shard_map/all_to_all | solution.py:478
  11.2 12.0 %copy-start.6 = (bf16[2560,64]{0,1:T(8,128)(2,1)S(1)}, bf16[2560,64]{0,1:T(8,128)(2,1)}, u32[]{:S(2)}) copy-start(bf16[2560,64]{0,1:T(8,128)(2,1)} %param.22) | copy-start | bytes 983044
  12.0 13.4 %collective-permute-start = (bf16[3,128,128]{2,1,0:T(8,128)(2,1)S(1)}, bf16[3,128,128]{2,1,0:T(8,128)(2,1)S(1)}, u32[]{:S(2)}, u32[]{:S(2)}) collective-permute-start(bf16[3,128,128]{2,1,0:T(8,128)(2,1)S(1)} %get-tuple-element.20.guide_own), channel_id=1, source_target_pairs={{1,0},{3,2},{5,4},{7,6},{9,8},{11,10},{13,12},{15,14},{17,16},{19,... | collective-permute-start | bytes 294920 | tf_op jit(solution)/shard_map/ppermute | solution.py:475
  13.3 20.3 %collective-permute-start.2 = (bf16[3,128,128]{2,1,0:T(8,128)(2,1)S(1)}, bf16[3,128,128]{2,1,0:T(8,128)(2,1)S(1)}, u32[]{:S(2)}, u32[]{:S(2)}) collective-permute-start(bf16[3,128,128]{2,1,0:T(8,128)(2,1)S(1)} %get-tuple-element.21), channel_id=1, source_target_pairs={{1,2},{3,0},{5,6},{7,4},{9,10},{11,8},{13,14},{15,12},{17,18},{19,... | collective-permute-start | bytes 294920 | tf_op jit(solution)/shard_map/ppermute | solution.py:477
  14.6 19.1 %collective-permute-start.1 = (bf16[3,128,128]{2,1,0:T(8,128)(2,1)S(1)}, bf16[3,128,128]{2,1,0:T(8,128)(2,1)S(1)}, u32[]{:S(2)}, u32[]{:S(2)}) collective-permute-start(bf16[3,128,128]{2,1,0:T(8,128)(2,1)S(1)} %get-tuple-element.21), channel_id=1, source_target_pairs={{0,2},{2,0},{4,6},{6,4},{8,10},{10,8},{12,14},{14,12},{16,18},{18,... | collective-permute-start | bytes 294920 | tf_op jit(solution)/shard_map/ppermute | solution.py:476
  23.3 1.0 %copy-start = (bf16[50,2,2560]{2,1,0:T(2,128)(2,1)S(1)}, bf16[50,2,2560]{2,1,0:T(2,128)(2,1)}, u32[]{:S(2)}) copy-start(bf16[50,2,2560]{2,1,0:T(2,128)(2,1)} %main_mod.1) | copy-start | bytes 1536004
  23.3 1.1 %copy-start.1 = (bf16[50,2,1024]{2,1,0:T(2,128)(2,1)S(1)}, bf16[50,2,1024]{2,1,0:T(2,128)(2,1)}, u32[]{:S(2)}) copy-start(bf16[50,2,1024]{2,1,0:T(2,128)(2,1)} %guide_mod.1) | copy-start | bytes 614404
  33.7 2.0 %collective-permute-start.3 = (bf16[8,272,128]{2,1,0:T(8,128)(2,1)S(1)}, bf16[8,272,128]{2,1,0:T(8,128)(2,1)S(1)}, u32[]{:S(2)}, u32[]{:S(2)}) collective-permute-start(bf16[8,272,128]{2,1,0:T(8,128)(2,1)S(1)} %all-to-all-done.got), channel_id=1, source_target_pairs={{0,1},{1,0},{2,3},{3,2},{4,5},{5,4},{6,7},{7,6},{8,9},{9,8},{10,11... | collective-permute-start | bytes 1671176 | tf_op jit(solution)/shard_map/ppermute | solution.py:484
  36.2 16.7 %collective-permute-start.6 = (bf16[4,512,128]{2,1,0:T(8,128)(2,1)S(1)}, bf16[4,512,128]{2,1,0:T(8,128)(2,1)S(1)}, u32[]{:S(2)}, u32[]{:S(2)}) collective-permute-start(bf16[4,512,128]{2,1,0:T(8,128)(2,1)S(1)} %get-tuple-element.33.refs_0_), channel_id=1, source_target_pairs={{0,8},{1,33},{4,12},{5,37},{8,0},{9,41},{12,4},{13,45},{16,24},{17... | collective-permute-start | bytes 1572872 | tf_op jit(solution)/shard_map/ppermute | solution.py:385
  37.6 15.5 %collective-permute-start.5 = (bf16[4,512,128]{2,1,0:T(8,128)(2,1)S(1)}, bf16[4,512,128]{2,1,0:T(8,128)(2,1)S(1)}, u32[]{:S(2)}, u32[]{:S(2)}) collective-permute-start(bf16[4,512,128]{2,1,0:T(8,128)(2,1)S(1)} %get-tuple-element.33.refs_0_), channel_id=1, source_target_pairs={{0,4},{1,17},{4,8},{5,21},{8,12},{9,25},{12,0},{13,29},{16,20},{17... | collective-permute-start | bytes 1572872 | tf_op jit(solution)/shard_map/ppermute | solution.py:385
  39.7 15.8 %collective-permute-start.4 = (bf16[4,512,128]{2,1,0:T(8,128)(2,1)S(1)}, bf16[4,512,128]{2,1,0:T(8,128)(2,1)S(1)}, u32[]{:S(2)}, u32[]{:S(2)}) collective-permute-start(bf16[4,512,128]{2,1,0:T(8,128)(2,1)S(1)} %get-tuple-element.33.refs_0_), channel_id=1, source_target_pairs={{0,12},{1,49},{4,0},{5,53},{8,4},{9,57},{12,8},{13,61},{16,28},{17... | collective-permute-start | bytes 1572872 | tf_op jit(solution)/shard_map/ppermute | solution.py:385
  39.8 11.8 %collective-permute-start.7 = (bf16[1024,128]{1,0:T(8,128)(2,1)S(1)}, bf16[1024,128]{1,0:T(8,128)(2,1)S(1)}, u32[]{:S(2)}, u32[]{:S(2)}) collective-permute-start(bf16[1024,128]{1,0:T(8,128)(2,1)S(1)} %get-tuple-element.32.queries), channel_id=1, source_target_pairs={{0,48},{1,13},{4,52},{5,1},{8,56},{9,5},{12,60},{13,9},{16,0},{17,... | collective-permute-start | bytes 786440 | tf_op jit(solution)/shard_map/ppermute | solution.py:385
  42.5 18.5 %collective-permute-start.9 = (bf16[1024,128]{1,0:T(8,128)(2,1)S(1)}, bf16[1024,128]{1,0:T(8,128)(2,1)S(1)}, u32[]{:S(2)}, u32[]{:S(2)}) collective-permute-start(bf16[1024,128]{1,0:T(8,128)(2,1)S(1)} %get-tuple-element.32.queries), channel_id=1, source_target_pairs={{0,16},{1,5},{4,20},{5,9},{8,24},{9,13},{12,28},{13,1},{16,32},{17... | collective-permute-start | bytes 786440 | tf_op jit(solution)/shard_map/ppermute | solution.py:385
  51.5 13.8 %collective-permute-start.11 = (bf16[1024,128]{1,0:T(8,128)(2,1)S(1)}, bf16[1024,128]{1,0:T(8,128)(2,1)S(1)}, u32[]{:S(2)}, u32[]{:S(2)}) collective-permute-start(bf16[1024,128]{1,0:T(8,128)(2,1)S(1)} %get-tuple-element.32.queries), channel_id=1, source_target_pairs={{0,32},{1,9},{4,36},{5,13},{8,40},{9,1},{12,44},{13,5},{16,48},{17... | collective-permute-start | bytes 786440 | tf_op jit(solution)/shard_map/ppermute | solution.py:385
  58.6 14.7 %collective-permute-start.8 = (bf16[1056,128]{1,0:T(8,128)(2,1)S(1)}, bf16[1056,128]{1,0:T(8,128)(2,1)S(1)}, u32[]{:S(2)}, u32[]{:S(2)}) collective-permute-start(bf16[1056,128]{1,0:T(8,128)(2,1)S(1)} %attend.5), channel_id=1, source_target_pairs={{0,16},{1,5},{4,20},{5,9},{8,24},{9,13},{12,28},{13,1},{16,32},{17... | collective-permute-start | bytes 811016 | tf_op jit(solution)/shard_map/ppermute | solution.py:385
  64.0 9.4 %collective-permute-start.10 = (bf16[1056,128]{1,0:T(8,128)(2,1)S(1)}, bf16[1056,128]{1,0:T(8,128)(2,1)S(1)}, u32[]{:S(2)}, u32[]{:S(2)}) collective-permute-start(bf16[1056,128]{1,0:T(8,128)(2,1)S(1)} %attend.6), channel_id=1, source_target_pairs={{0,48},{1,13},{4,52},{5,1},{8,56},{9,5},{12,60},{13,9},{16,0},{17,... | collective-permute-start | bytes 811016 | tf_op jit(solution)/shard_map/ppermute | solution.py:385
  68.3 8.0 %collective-permute-start.12 = (bf16[1056,128]{1,0:T(8,128)(2,1)S(1)}, bf16[1056,128]{1,0:T(8,128)(2,1)S(1)}, u32[]{:S(2)}, u32[]{:S(2)}) collective-permute-start(bf16[1056,128]{1,0:T(8,128)(2,1)S(1)} %attend.7), channel_id=1, source_target_pairs={{0,32},{1,9},{4,36},{5,13},{8,40},{9,1},{12,44},{13,5},{16,48},{17... | collective-permute-start | bytes 811016 | tf_op jit(solution)/shard_map/ppermute | solution.py:385
  77.9 11.8 %copy-start.5 = (f32[1,32,64]{2,1,0:T(8,128)S(1)}, f32[1,32,64]{2,1,0:T(8,128)}, u32[]{:S(2)}) copy-start(f32[1,32,64]{2,1,0:T(8,128)} %latents.1) | copy-start | bytes 24580

commit v8 on v7

--- a/solution.py
+++ b/solution.py
@@ -288,7 +288,8 @@
         mean = jnp.mean(attended.astype(f32), axis=1, keepdims=True)
         centered = attended.astype(f32) - mean
         square = jnp.sum(centered * centered, axis=1, keepdims=True)
-        flow = term_dot(centered * scales[head : head + 1, :], weights[head]).astype(bf16)
+        scaled = (centered * scales[head : head + 1, :]).astype(bf16)
+        flow = jnp.dot(scaled, weights[head], preferred_element_type=f32).astype(bf16)
         for tile in range(blocks):
             rows = slice(tile * HD, (tile + 1) * HD)
             flows.append(flow[rows])

time: 92.5 us -> 92.4 us (level)
  no operation moved by 1% of the time
where the time goes in v8:
time: 92.4 us; the launch traced here: 91.3 us
  starting transfers between devices  32.5 us (35%)
  waiting for transfers between devices  24.2 us (26%)
  Pallas kernels  20.1 us (22%)
  blocking collectives  11.8 us (13%)
  between operations  1.46 us (2%)
  local copies, waits for them, and re-layouts  1.27 us (1%)
    ppermute x9, waiting for transfers between devices, plane_shift(): return lax.ppermute(array, ('x', 'y', 'core'), pairs)  14 us
    ppermute x9, starting transfers between devices, plane_shift(): return lax.ppermute(array, ('x', 'y', 'core'), pairs)  13.5 us
    pallas_call x4, Pallas kernels, attend(): pl.pallas_call(attend_kernel, out_shape=shape(rows + STAT, HD), in_specs=...  12 us
    all_to_all x1, blocking collectives, on_device(): lax.all_to_all(send, ('core', 'zh', 'zl'), split_axis=0, concat_axis=0, t...  11.8 us
    all_to_all x1, starting transfers between devices, on_device(): lax.all_to_all(send, ('zh', 'zl'), split_axis=0, concat_axis=0, tiled=True)  8.61 us
    ppermute x1, waiting for transfers between devices, on_device(): guide_across = lax.ppermute(guide_send, halves, [(1, 2), (3, 0)])  8.11 us
    ppermute x1, starting transfers between devices, on_device(): guide_half = lax.ppermute(guide_send, halves, [(0, 2), (2, 0)])  7.83 us
    ppermute x1, waiting for transfers between devices, on_device(): sibling = lax.ppermute(got, 'core', [(0, 1), (1, 0)])  1.96 us
  transfers between devices with their start and end apart: 14, of which 7 were waited for; matrix products, arithmetic and copies ran while one was open for 1% of the time, Pallas kernels for 16%

profile of v8, /device:TPU:24, one launch (start us, length us, event | category | flops | bytes accessed | tf_op | source)
XLA Modules:
  0.0 91.3 jit_solution(16991973063922223278)
XLA Ops:
  0.6 1.9 %pack.1 = bf16[8,272,128]{2,1,0:T(8,128)(2,1)} custom-call(bf16[1,32,2560]{2,1,0:T(8,128)(2,1)} %mq.1, bf16[1,32,2560]{2,1,0:T(8,128)(2,1)} %mk.1, bf16[1,32,2560]{2,1,0:T(8,128)(2,1)} %mv.1), custom_call_target="tpu_custom_call" | custom-call | tf_op jit(solution)/shard_map/pack/pallas_call | solution.py:439
  2.6 8.6 %all-to-all-start = ((bf16[8,272,128]{2,1,0:T(8,128)(2,1)}), bf16[8,272,128]{2,1,0:T(8,128)(2,1)S(1)}, u32[]{:S(2)}, u32[]{:S(2)}) async-start(bf16[8,272,128]{2,1,0:T(8,128)(2,1)} %pack.1), calls=%async_computation | async-start | bytes 1114112 | tf_op jit(solution)/shard_map/all_to_all | solution.py:479
  11.3 0.7 pack_guide.1
  12.0 1.3 %collective-permute-start = (bf16[3,128,128]{2,1,0:T(8,128)(2,1)S(1)}, bf16[3,128,128]{2,1,0:T(8,128)(2,1)S(1)}, u32[]{:S(2)}, u32[]{:S(2)}) collective-permute-start(bf16[3,128,128]{2,1,0:T(8,128)(2,1)S(1)} %get-tuple-element.20.guide_own), channel_id=1, source_target_pairs={{1,0},{3,2},{5,4},{7,6},{9,8},{11,10},{13,12},{15,14},{17,16},{19,... | collective-permute-start | bytes 294920 | tf_op jit(solution)/shard_map/ppermute | solution.py:476
  13.3 1.3 %collective-permute-start.2 = (bf16[3,128,128]{2,1,0:T(8,128)(2,1)S(1)}, bf16[3,128,128]{2,1,0:T(8,128)(2,1)S(1)}, u32[]{:S(2)}, u32[]{:S(2)}) collective-permute-start(bf16[3,128,128]{2,1,0:T(8,128)(2,1)S(1)} %get-tuple-element.21), channel_id=1, source_target_pairs={{1,2},{3,0},{5,6},{7,4},{9,10},{11,8},{13,14},{15,12},{17,18},{19,... | collective-permute-start | bytes 294920 | tf_op jit(solution)/shard_map/ppermute | solution.py:478
  14.6 7.8 %collective-permute-start.1 = (bf16[3,128,128]{2,1,0:T(8,128)(2,1)S(1)}, bf16[3,128,128]{2,1,0:T(8,128)(2,1)S(1)}, u32[]{:S(2)}, u32[]{:S(2)}) collective-permute-start(bf16[3,128,128]{2,1,0:T(8,128)(2,1)S(1)} %get-tuple-element.21), channel_id=1, source_target_pairs={{0,2},{2,0},{4,6},{6,4},{8,10},{10,8},{12,14},{14,12},{16,18},{18,... | collective-permute-start | bytes 294920 | tf_op jit(solution)/shard_map/ppermute | solution.py:477
  23.1 0.2 copy.15.guide_head
  23.3 0.3 copy.14.main_head
  23.6 0.7 copy-done
  24.4 1.1 %prepare.1 = (bf16[2,128,64]{2,1,0:T(8,128)(2,1)S(1)}, f32[8,128]{1,0:T(8,128)S(1)}, f32[128,128]{1,0:T(8,128)S(1)}, f32[8,128]{1,0:T(8,128)S(1)}) custom-call(s32[1]{0:T(128)S(6)} %copy.16.step, s32[3]{0:T(128)S(1)} %pad_add_fusion.place, bf16[50,2,2560]{2,1,0:T(2,128)(2,1)S(1)} %copy-done, bf16[50,2,1024]{2,1,0:T(2,128)(2,1)S(1)} %copy-done.1, ...), custom_call_target="tpu_custom_call" | custom-call | tf_op jit(solution)/shard_map/prepare/pallas_call | solution.py:453
  25.4 8.1 %collective-permute-done.2.guide_across = bf16[3,128,128]{2,1,0:T(8,128)(2,1)S(1)} collective-permute-done((bf16[3,128,128]{2,1,0:T(8,128)(2,1)S(1)}, bf16[3,128,128]{2,1,0:T(8,128)(2,1)S(1)}, u32[]{:S(2)}, u32[]{:S(2)}) %collective-permute-start.2) | collective-permute-done | bytes 98336 | tf_op jit(solution)/shard_map/ppermute | solution.py:478
  33.6 0.1 collective-permute-done.1.guide_half
  33.7 2.0 %collective-permute-done.3.sibling = bf16[8,272,128]{2,1,0:T(8,128)(2,1)S(1)} collective-permute-done((bf16[8,272,128]{2,1,0:T(8,128)(2,1)S(1)}, bf16[8,272,128]{2,1,0:T(8,128)(2,1)S(1)}, u32[]{:S(2)}, u32[]{:S(2)}) %collective-permute-start.3) | collective-permute-done | bytes 557088 | tf_op jit(solution)/shard_map/ppermute | solution.py:485
  35.6 0.6 unpack.1
  36.2 1.3 %collective-permute-start.6 = (bf16[4,512,128]{2,1,0:T(8,128)(2,1)S(1)}, bf16[4,512,128]{2,1,0:T(8,128)(2,1)S(1)}, u32[]{:S(2)}, u32[]{:S(2)}) collective-permute-start(bf16[4,512,128]{2,1,0:T(8,128)(2,1)S(1)} %get-tuple-element.33.refs_0_), channel_id=1, source_target_pairs={{0,8},{1,33},{4,12},{5,37},{8,0},{9,41},{12,4},{13,45},{16,24},{17... | collective-permute-start | bytes 1572872 | tf_op jit(solution)/shard_map/ppermute | solution.py:386
  37.6 2.2 %collective-permute-start.5 = (bf16[4,512,128]{2,1,0:T(8,128)(2,1)S(1)}, bf16[4,512,128]{2,1,0:T(8,128)(2,1)S(1)}, u32[]{:S(2)}, u32[]{:S(2)}) collective-permute-start(bf16[4,512,128]{2,1,0:T(8,128)(2,1)S(1)} %get-tuple-element.33.refs_0_), channel_id=1, source_target_pairs={{0,4},{1,17},{4,8},{5,21},{8,12},{9,25},{12,0},{13,29},{16,20},{17... | collective-permute-start | bytes 1572872 | tf_op jit(solution)/shard_map/ppermute | solution.py:386
  39.8 2.8 %collective-permute-start.7 = (bf16[1024,128]{1,0:T(8,128)(2,1)S(1)}, bf16[1024,128]{1,0:T(8,128)(2,1)S(1)}, u32[]{:S(2)}, u32[]{:S(2)}) collective-permute-start(bf16[1024,128]{1,0:T(8,128)(2,1)S(1)} %get-tuple-element.32.queries), channel_id=1, source_target_pairs={{0,48},{1,13},{4,52},{5,1},{8,56},{9,5},{12,60},{13,9},{16,0},{17,... | collective-permute-start | bytes 786440 | tf_op jit(solution)/shard_map/ppermute | solution.py:386
  42.5 9.0 %collective-permute-done.7.queries = bf16[1024,128]{1,0:T(8,128)(2,1)S(1)} collective-permute-done((bf16[1024,128]{1,0:T(8,128)(2,1)S(1)}, bf16[1024,128]{1,0:T(8,128)(2,1)S(1)}, u32[]{:S(2)}, u32[]{:S(2)}) %collective-permute-start.7) | collective-permute-done | bytes 262176 | tf_op jit(solution)/shard_map/ppermute | solution.py:386
  51.5 1.5 %collective-permute-start.11 = (bf16[1024,128]{1,0:T(8,128)(2,1)S(1)}, bf16[1024,128]{1,0:T(8,128)(2,1)S(1)}, u32[]{:S(2)}, u32[]{:S(2)}) collective-permute-start(bf16[1024,128]{1,0:T(8,128)(2,1)S(1)} %get-tuple-element.32.queries), channel_id=1, source_target_pairs={{0,32},{1,9},{4,36},{5,13},{8,40},{9,1},{12,44},{13,5},{16,48},{17... | collective-permute-start | bytes 786440 | tf_op jit(solution)/shard_map/ppermute | solution.py:386
  53.0 2.6 %collective-permute-done.4.refs_1_ = bf16[4,512,128]{2,1,0:T(8,128)(2,1)S(1)} collective-permute-done((bf16[4,512,128]{2,1,0:T(8,128)(2,1)S(1)}, bf16[4,512,128]{2,1,0:T(8,128)(2,1)S(1)}, u32[]{:S(2)}, u32[]{:S(2)}) %collective-permute-start.4) | collective-permute-done | bytes 524320 | tf_op jit(solution)/shard_map/ppermute | solution.py:386
  55.6 3.0 %attend.5 = bf16[1056,128]{1,0:T(8,128)(2,1)S(1)} custom-call(bf16[1024,128]{1,0:T(8,128)(2,1)S(1)} %collective-permute-done.7.queries, bf16[4,512,128]{2,1,0:T(8,128)(2,1)S(1)} %get-tuple-element.33.refs_0_, bf16[4,512,128]{2,1,0:T(8,128)(2,1)S(1)} %collective-permute-done.4.refs_1_, bf16[4,512,128]{2,1,0:T(8,128)(2,1)S(1)} %collective-permute-done.5.refs_2_, ...), custom_call_target="tpu_custom_call" | custom-call | flops 1073741824 | bytes 2097152 | tf_op jit(solution)/shard_map/attend/pallas_call | solution.py:394
  58.6 2.4 %collective-permute-start.8 = (bf16[1056,128]{1,0:T(8,128)(2,1)S(1)}, bf16[1056,128]{1,0:T(8,128)(2,1)S(1)}, u32[]{:S(2)}, u32[]{:S(2)}) collective-permute-start(bf16[1056,128]{1,0:T(8,128)(2,1)S(1)} %attend.5), channel_id=1, source_target_pairs={{0,16},{1,5},{4,20},{5,9},{8,24},{9,13},{12,28},{13,1},{16,32},{17... | collective-permute-start | bytes 811016 | tf_op jit(solution)/shard_map/ppermute | solution.py:386
  61.0 3.0 %attend.6 = bf16[1056,128]{1,0:T(8,128)(2,1)S(1)} custom-call(bf16[1024,128]{1,0:T(8,128)(2,1)S(1)} %collective-permute-done.9.queries, bf16[4,512,128]{2,1,0:T(8,128)(2,1)S(1)} %get-tuple-element.33.refs_0_, bf16[4,512,128]{2,1,0:T(8,128)(2,1)S(1)} %collective-permute-done.4.refs_1_, bf16[4,512,128]{2,1,0:T(8,128)(2,1)S(1)} %collective-permute-done.5.refs_2_, ...), custom_call_target="tpu_custom_call" | custom-call | flops 1073741824 | bytes 2097152 | tf_op jit(solution)/shard_map/attend/pallas_call | solution.py:394
  64.0 1.3 %collective-permute-start.10 = (bf16[1056,128]{1,0:T(8,128)(2,1)S(1)}, bf16[1056,128]{1,0:T(8,128)(2,1)S(1)}, u32[]{:S(2)}, u32[]{:S(2)}) collective-permute-start(bf16[1056,128]{1,0:T(8,128)(2,1)S(1)} %attend.6), channel_id=1, source_target_pairs={{0,48},{1,13},{4,52},{5,1},{8,56},{9,5},{12,60},{13,9},{16,0},{17,... | collective-permute-start | bytes 811016 | tf_op jit(solution)/shard_map/ppermute | solution.py:386
  65.3 3.0 %attend.7 = bf16[1056,128]{1,0:T(8,128)(2,1)S(1)} custom-call(bf16[1024,128]{1,0:T(8,128)(2,1)S(1)} %collective-permute-done.11.queries, bf16[4,512,128]{2,1,0:T(8,128)(2,1)S(1)} %get-tuple-element.33.refs_0_, bf16[4,512,128]{2,1,0:T(8,128)(2,1)S(1)} %collective-permute-done.4.refs_1_, bf16[4,512,128]{2,1,0:T(8,128)(2,1)S(1)} %collective-permute-done.5.refs_2_, ...), custom_call_target="tpu_custom_call" | custom-call | flops 1073741824 | bytes 2097152 | tf_op jit(solution)/shard_map/attend/pallas_call | solution.py:394
  68.3 2.0 %collective-permute-start.12 = (bf16[1056,128]{1,0:T(8,128)(2,1)S(1)}, bf16[1056,128]{1,0:T(8,128)(2,1)S(1)}, u32[]{:S(2)}, u32[]{:S(2)}) collective-permute-start(bf16[1056,128]{1,0:T(8,128)(2,1)S(1)} %attend.7), channel_id=1, source_target_pairs={{0,32},{1,9},{4,36},{5,13},{8,40},{9,1},{12,44},{13,5},{16,48},{17... | collective-permute-start | bytes 811016 | tf_op jit(solution)/shard_map/ppermute | solution.py:386
  70.3 3.0 %attend.4.refs_0_ = bf16[1056,128]{1,0:T(8,128)(2,1)S(1)} custom-call(bf16[1024,128]{1,0:T(8,128)(2,1)S(1)} %get-tuple-element.32.queries, bf16[4,512,128]{2,1,0:T(8,128)(2,1)S(1)} %get-tuple-element.33.refs_0_, bf16[4,512,128]{2,1,0:T(8,128)(2,1)S(1)} %collective-permute-done.4.refs_1_, bf16[4,512,128]{2,1,0:T(8,128)(2,1)S(1)} %collective-permute-done.5.refs_2_, ...), custom_call_target="tpu_custom_call" | custom-call | flops 1073741824 | bytes 2097152 | tf_op jit(solution)/shard_map/attend/pallas_call | solution.py:394
  73.3 0.7 merge.1
  74.0 2.3 %collective-permute-done.12.part = bf16[1056,128]{1,0:T(8,128)(2,1)S(1)} collective-permute-done((bf16[1056,128]{1,0:T(8,128)(2,1)S(1)}, bf16[1056,128]{1,0:T(8,128)(2,1)S(1)}, u32[]{:S(2)}, u32[]{:S(2)}) %collective-permute-start.12) | collective-permute-done | bytes 270368 | tf_op jit(solution)/shard_map/ppermute | solution.py:386
  76.4 1.4 %combine.1 = bf16[16,48,128]{2,1,0:T(8,128)(2,1)S(1)} custom-call(s32[3]{0:T(128)S(1)} %pad_add_fusion.place, bf16[2,128,64]{2,1,0:T(8,128)(2,1)S(1)} %get-tuple-element.26.weights, f32[8,128]{1,0:T(8,128)S(1)} %get-tuple-element.27.scales, f32[1024,128]{1,0:T(8,128)S(1)} %get-tuple-element.34.former, f32[8,128]{1,0:T(8,128)S(1)} %get-tuple-element.35.former_level, ...), custom_call_target="tpu_custom_call" | custom-call | tf_op jit(solution)/shard_map/combine/pallas_call | solution.py:506
  77.8 11.8 %all_to_all.10.got = bf16[16,48,128]{2,1,0:T(8,128)(2,1)S(1)} all-to-all(bf16[16,48,128]{2,1,0:T(8,128)(2,1)S(1)} %combine.1), channel_id=1, replica_groups=mesh['zl'=4,'x'=4,'y'=4,'zh'=2,'core'=2] {'core','zh','zl'}, dimensions={0} | all-to-all | bytes 393216 | tf_op jit(solution)/shard_map/all_to_all | solution.py:514
  89.6 1.7 %final.1 = (f32[1,32,64]{2,1,0:T(8,128)}, f32[1,32,64]{2,1,0:T(8,128)}) custom-call(s32[1]{0:T(128)S(6)} %copy.16.step, s32[3]{0:T(128)S(1)} %pad_add_fusion.place, bf16[16,48,128]{2,1,0:T(8,128)(2,1)S(1)} %all_to_all.10.got, f32[128,128]{1,0:T(8,128)S(1)} %get-tuple-element.36.means, f32[8,128]{1,0:T(8,128)S(1)} %get-tuple-element.37.shifts, ...), custom_call_target="tpu_custom_call" | custom-call | tf_op jit(solution)/shard_map/final/pallas_call | solution.py:515
  (27 shorter events, 0.3 us)
Async XLA Ops:
  2.6 8.7 %copy-start.2 = (bf16[1,128,256]{2,1,0:T(8,128)(2,1)S(1)}, bf16[1,128,256]{2,1,0:T(8,128)(2,1)}, u32[]{:S(2)}) copy-start(bf16[1,128,256]{2,1,0:T(8,128)(2,1)} %gq.1) | copy-start | bytes 196612
  2.6 8.7 %copy-start.3 = (bf16[1,128,256]{2,1,0:T(8,128)(2,1)S(1)}, bf16[1,128,256]{2,1,0:T(8,128)(2,1)}, u32[]{:S(2)}) copy-start(bf16[1,128,256]{2,1,0:T(8,128)(2,1)} %gk.1) | copy-start | bytes 196612
  2.6 8.7 %copy-start.4 = (bf16[1,128,256]{2,1,0:T(8,128)(2,1)S(1)}, bf16[1,128,256]{2,1,0:T(8,128)(2,1)}, u32[]{:S(2)}) copy-start(bf16[1,128,256]{2,1,0:T(8,128)(2,1)} %gv.1) | copy-start | bytes 196612
  2.6 20.5 %copy-start.7 = (bf16[1024,64]{0,1:T(8,128)(2,1)S(1)}, bf16[1024,64]{0,1:T(8,128)(2,1)}, u32[]{:S(2)}) copy-start(bf16[1024,64]{0,1:T(8,128)(2,1)} %param.23) | copy-start | bytes 393220
  2.6 31.0 %all-to-all-start = ((bf16[8,272,128]{2,1,0:T(8,128)(2,1)}), bf16[8,272,128]{2,1,0:T(8,128)(2,1)S(1)}, u32[]{:S(2)}, u32[]{:S(2)}) async-start(bf16[8,272,128]{2,1,0:T(8,128)(2,1)} %pack.1), calls=%async_computation | async-start | bytes 1114112 | tf_op jit(solution)/shard_map/all_to_all | solution.py:479
  11.2 12.0 %copy-start.6 = (bf16[2560,64]{0,1:T(8,128)(2,1)S(1)}, bf16[2560,64]{0,1:T(8,128)(2,1)}, u32[]{:S(2)}) copy-start(bf16[2560,64]{0,1:T(8,128)(2,1)} %param.22) | copy-start | bytes 983044
  12.0 13.4 %collective-permute-start = (bf16[3,128,128]{2,1,0:T(8,128)(2,1)S(1)}, bf16[3,128,128]{2,1,0:T(8,128)(2,1)S(1)}, u32[]{:S(2)}, u32[]{:S(2)}) collective-permute-start(bf16[3,128,128]{2,1,0:T(8,128)(2,1)S(1)} %get-tuple-element.20.guide_own), channel_id=1, source_target_pairs={{1,0},{3,2},{5,4},{7,6},{9,8},{11,10},{13,12},{15,14},{17,16},{19,... | collective-permute-start | bytes 294920 | tf_op jit(solution)/shard_map/ppermute | solution.py:476
  13.3 20.3 %collective-permute-start.2 = (bf16[3,128,128]{2,1,0:T(8,128)(2,1)S(1)}, bf16[3,128,128]{2,1,0:T(8,128)(2,1)S(1)}, u32[]{:S(2)}, u32[]{:S(2)}) collective-permute-start(bf16[3,128,128]{2,1,0:T(8,128)(2,1)S(1)} %get-tuple-element.21), channel_id=1, source_target_pairs={{1,2},{3,0},{5,6},{7,4},{9,10},{11,8},{13,14},{15,12},{17,18},{19,... | collective-permute-start | bytes 294920 | tf_op jit(solution)/shard_map/ppermute | solution.py:478
  14.6 19.1 %collective-permute-start.1 = (bf16[3,128,128]{2,1,0:T(8,128)(2,1)S(1)}, bf16[3,128,128]{2,1,0:T(8,128)(2,1)S(1)}, u32[]{:S(2)}, u32[]{:S(2)}) collective-permute-start(bf16[3,128,128]{2,1,0:T(8,128)(2,1)S(1)} %get-tuple-element.21), channel_id=1, source_target_pairs={{0,2},{2,0},{4,6},{6,4},{8,10},{10,8},{12,14},{14,12},{16,18},{18,... | collective-permute-start | bytes 294920 | tf_op jit(solution)/shard_map/ppermute | solution.py:477
  23.3 1.0 %copy-start = (bf16[50,2,2560]{2,1,0:T(2,128)(2,1)S(1)}, bf16[50,2,2560]{2,1,0:T(2,128)(2,1)}, u32[]{:S(2)}) copy-start(bf16[50,2,2560]{2,1,0:T(2,128)(2,1)} %main_mod.1) | copy-start | bytes 1536004
  23.3 1.1 %copy-start.1 = (bf16[50,2,1024]{2,1,0:T(2,128)(2,1)S(1)}, bf16[50,2,1024]{2,1,0:T(2,128)(2,1)}, u32[]{:S(2)}) copy-start(bf16[50,2,1024]{2,1,0:T(2,128)(2,1)} %guide_mod.1) | copy-start | bytes 614404
  33.7 2.0 %collective-permute-start.3 = (bf16[8,272,128]{2,1,0:T(8,128)(2,1)S(1)}, bf16[8,272,128]{2,1,0:T(8,128)(2,1)S(1)}, u32[]{:S(2)}, u32[]{:S(2)}) collective-permute-start(bf16[8,272,128]{2,1,0:T(8,128)(2,1)S(1)} %all-to-all-done.got), channel_id=1, source_target_pairs={{0,1},{1,0},{2,3},{3,2},{4,5},{5,4},{6,7},{7,6},{8,9},{9,8},{10,11... | collective-permute-start | bytes 1671176 | tf_op jit(solution)/shard_map/ppermute | solution.py:485
  36.2 16.7 %collective-permute-start.6 = (bf16[4,512,128]{2,1,0:T(8,128)(2,1)S(1)}, bf16[4,512,128]{2,1,0:T(8,128)(2,1)S(1)}, u32[]{:S(2)}, u32[]{:S(2)}) collective-permute-start(bf16[4,512,128]{2,1,0:T(8,128)(2,1)S(1)} %get-tuple-element.33.refs_0_), channel_id=1, source_target_pairs={{0,8},{1,33},{4,12},{5,37},{8,0},{9,41},{12,4},{13,45},{16,24},{17... | collective-permute-start | bytes 1572872 | tf_op jit(solution)/shard_map/ppermute | solution.py:386
  37.6 15.5 %collective-permute-start.5 = (bf16[4,512,128]{2,1,0:T(8,128)(2,1)S(1)}, bf16[4,512,128]{2,1,0:T(8,128)(2,1)S(1)}, u32[]{:S(2)}, u32[]{:S(2)}) collective-permute-start(bf16[4,512,128]{2,1,0:T(8,128)(2,1)S(1)} %get-tuple-element.33.refs_0_), channel_id=1, source_target_pairs={{0,4},{1,17},{4,8},{5,21},{8,12},{9,25},{12,0},{13,29},{16,20},{17... | collective-permute-start | bytes 1572872 | tf_op jit(solution)/shard_map/ppermute | solution.py:386
  39.7 15.8 %collective-permute-start.4 = (bf16[4,512,128]{2,1,0:T(8,128)(2,1)S(1)}, bf16[4,512,128]{2,1,0:T(8,128)(2,1)S(1)}, u32[]{:S(2)}, u32[]{:S(2)}) collective-permute-start(bf16[4,512,128]{2,1,0:T(8,128)(2,1)S(1)} %get-tuple-element.33.refs_0_), channel_id=1, source_target_pairs={{0,12},{1,49},{4,0},{5,53},{8,4},{9,57},{12,8},{13,61},{16,28},{17... | collective-permute-start | bytes 1572872 | tf_op jit(solution)/shard_map/ppermute | solution.py:386
  39.8 11.8 %collective-permute-start.7 = (bf16[1024,128]{1,0:T(8,128)(2,1)S(1)}, bf16[1024,128]{1,0:T(8,128)(2,1)S(1)}, u32[]{:S(2)}, u32[]{:S(2)}) collective-permute-start(bf16[1024,128]{1,0:T(8,128)(2,1)S(1)} %get-tuple-element.32.queries), channel_id=1, source_target_pairs={{0,48},{1,13},{4,52},{5,1},{8,56},{9,5},{12,60},{13,9},{16,0},{17,... | collective-permute-start | bytes 786440 | tf_op jit(solution)/shard_map/ppermute | solution.py:386
  42.5 18.5 %collective-permute-start.9 = (bf16[1024,128]{1,0:T(8,128)(2,1)S(1)}, bf16[1024,128]{1,0:T(8,128)(2,1)S(1)}, u32[]{:S(2)}, u32[]{:S(2)}) collective-permute-start(bf16[1024,128]{1,0:T(8,128)(2,1)S(1)} %get-tuple-element.32.queries), channel_id=1, source_target_pairs={{0,16},{1,5},{4,20},{5,9},{8,24},{9,13},{12,28},{13,1},{16,32},{17... | collective-permute-start | bytes 786440 | tf_op jit(solution)/shard_map/ppermute | solution.py:386
  51.5 13.8 %collective-permute-start.11 = (bf16[1024,128]{1,0:T(8,128)(2,1)S(1)}, bf16[1024,128]{1,0:T(8,128)(2,1)S(1)}, u32[]{:S(2)}, u32[]{:S(2)}) collective-permute-start(bf16[1024,128]{1,0:T(8,128)(2,1)S(1)} %get-tuple-element.32.queries), channel_id=1, source_target_pairs={{0,32},{1,9},{4,36},{5,13},{8,40},{9,1},{12,44},{13,5},{16,48},{17... | collective-permute-start | bytes 786440 | tf_op jit(solution)/shard_map/ppermute | solution.py:386
  58.6 14.7 %collective-permute-start.8 = (bf16[1056,128]{1,0:T(8,128)(2,1)S(1)}, bf16[1056,128]{1,0:T(8,128)(2,1)S(1)}, u32[]{:S(2)}, u32[]{:S(2)}) collective-permute-start(bf16[1056,128]{1,0:T(8,128)(2,1)S(1)} %attend.5), channel_id=1, source_target_pairs={{0,16},{1,5},{4,20},{5,9},{8,24},{9,13},{12,28},{13,1},{16,32},{17... | collective-permute-start | bytes 811016 | tf_op jit(solution)/shard_map/ppermute | solution.py:386
  64.0 9.4 %collective-permute-start.10 = (bf16[1056,128]{1,0:T(8,128)(2,1)S(1)}, bf16[1056,128]{1,0:T(8,128)(2,1)S(1)}, u32[]{:S(2)}, u32[]{:S(2)}) collective-permute-start(bf16[1056,128]{1,0:T(8,128)(2,1)S(1)} %attend.6), channel_id=1, source_target_pairs={{0,48},{1,13},{4,52},{5,1},{8,56},{9,5},{12,60},{13,9},{16,0},{17,... | collective-permute-start | bytes 811016 | tf_op jit(solution)/shard_map/ppermute | solution.py:386
  68.3 8.0 %collective-permute-start.12 = (bf16[1056,128]{1,0:T(8,128)(2,1)S(1)}, bf16[1056,128]{1,0:T(8,128)(2,1)S(1)}, u32[]{:S(2)}, u32[]{:S(2)}) collective-permute-start(bf16[1056,128]{1,0:T(8,128)(2,1)S(1)} %attend.7), channel_id=1, source_target_pairs={{0,32},{1,9},{4,36},{5,13},{8,40},{9,1},{12,44},{13,5},{16,48},{17... | collective-permute-start | bytes 811016 | tf_op jit(solution)/shard_map/ppermute | solution.py:386
  77.8 11.8 %copy-start.5 = (f32[1,32,64]{2,1,0:T(8,128)S(1)}, f32[1,32,64]{2,1,0:T(8,128)}, u32[]{:S(2)}) copy-start(f32[1,32,64]{2,1,0:T(8,128)} %latents.1) | copy-start | bytes 24580

commit v9 on v7

--- a/solution.py
+++ b/solution.py
@@ -361,9 +361,10 @@
     lane = lax.broadcasted_iota(jnp.int32, (ROWS, HD), 1)
     shrink = jnp.where(lane < C, mine[:, 2:3], mine[:, 3:4])
     high = means[...].astype(bf16)
-    moved = term_dot(mine, high) + jnp.dot(
-        mine.astype(bf16), (means[...] - high.astype(f32)).astype(bf16), preferred_element_type=f32
-    )
+    low = (means[...] - high.astype(f32)).astype(bf16)
+    both = jnp.concatenate([high, low], axis=1)
+    moved = jnp.dot(terms(mine), both, preferred_element_type=f32)
+    moved = moved[:ROWS, :HD] + moved[ROWS:, :HD] + moved[:ROWS, HD:]
     flow = shrink * (total + moved) + shifts[0:1, :]
     main_flow, guide_flow = flow[:, :C], flow[:, C:]
     result = guide_flow + guidance * (main_flow - guide_flow)

time: 92.5 us -> 92.5 us (level)
  no operation moved by 1% of the time
where the time goes in v9:
time: 92.5 us; the launch traced here: 91.4 us
  starting transfers between devices  32.5 us (35%)
  waiting for transfers between devices  24.2 us (26%)
  Pallas kernels  20.2 us (22%)
  blocking collectives  11.8 us (13%)
  between operations  1.46 us (2%)
  local copies, waits for them, and re-layouts  1.27 us (1%)
    ppermute x9, waiting for transfers between devices, plane_shift(): return lax.ppermute(array, ('x', 'y', 'core'), pairs)  14 us
    ppermute x9, starting transfers between devices, plane_shift(): return lax.ppermute(array, ('x', 'y', 'core'), pairs)  13.5 us
    pallas_call x4, Pallas kernels, attend(): pl.pallas_call(attend_kernel, out_shape=shape(rows + STAT, HD), in_specs=...  12 us
    all_to_all x1, blocking collectives, on_device(): lax.all_to_all(send, ('core', 'zh', 'zl'), split_axis=0, concat_axis=0, t...  11.8 us
    all_to_all x1, starting transfers between devices, on_device(): lax.all_to_all(send, ('zh', 'zl'), split_axis=0, concat_axis=0, tiled=True)  8.61 us
    ppermute x1, waiting for transfers between devices, on_device(): guide_across = lax.ppermute(guide_send, halves, [(1, 2), (3, 0)])  8.11 us
    ppermute x1, starting transfers between devices, on_device(): guide_half = lax.ppermute(guide_send, halves, [(0, 2), (2, 0)])  7.83 us
    ppermute x1, waiting for transfers between devices, on_device(): sibling = lax.ppermute(got, 'core', [(0, 1), (1, 0)])  1.96 us
  transfers between devices with their start and end apart: 14, of which 7 were waited for; matrix products, arithmetic and copies ran while one was open for 1% of the time, Pallas kernels for 16%

profile of v9, /device:TPU:24, one launch (start us, length us, event | category | flops | bytes accessed | tf_op | source)
XLA Modules:
  0.0 91.4 jit_solution(4181652539497714579)
XLA Ops:
  0.6 1.9 %pack.1 = bf16[8,272,128]{2,1,0:T(8,128)(2,1)} custom-call(bf16[1,32,2560]{2,1,0:T(8,128)(2,1)} %mq.1, bf16[1,32,2560]{2,1,0:T(8,128)(2,1)} %mk.1, bf16[1,32,2560]{2,1,0:T(8,128)(2,1)} %mv.1), custom_call_target="tpu_custom_call" | custom-call | tf_op jit(solution)/shard_map/pack/pallas_call | solution.py:439
  2.6 8.6 %all-to-all-start = ((bf16[8,272,128]{2,1,0:T(8,128)(2,1)}), bf16[8,272,128]{2,1,0:T(8,128)(2,1)S(1)}, u32[]{:S(2)}, u32[]{:S(2)}) async-start(bf16[8,272,128]{2,1,0:T(8,128)(2,1)} %pack.1), calls=%async_computation | async-start | bytes 1114112 | tf_op jit(solution)/shard_map/all_to_all | solution.py:479
  11.3 0.7 pack_guide.1
  12.0 1.3 %collective-permute-start = (bf16[3,128,128]{2,1,0:T(8,128)(2,1)S(1)}, bf16[3,128,128]{2,1,0:T(8,128)(2,1)S(1)}, u32[]{:S(2)}, u32[]{:S(2)}) collective-permute-start(bf16[3,128,128]{2,1,0:T(8,128)(2,1)S(1)} %get-tuple-element.20.guide_own), channel_id=1, source_target_pairs={{1,0},{3,2},{5,4},{7,6},{9,8},{11,10},{13,12},{15,14},{17,16},{19,... | collective-permute-start | bytes 294920 | tf_op jit(solution)/shard_map/ppermute | solution.py:476
  13.3 1.3 %collective-permute-start.2 = (bf16[3,128,128]{2,1,0:T(8,128)(2,1)S(1)}, bf16[3,128,128]{2,1,0:T(8,128)(2,1)S(1)}, u32[]{:S(2)}, u32[]{:S(2)}) collective-permute-start(bf16[3,128,128]{2,1,0:T(8,128)(2,1)S(1)} %get-tuple-element.21), channel_id=1, source_target_pairs={{1,2},{3,0},{5,6},{7,4},{9,10},{11,8},{13,14},{15,12},{17,18},{19,... | collective-permute-start | bytes 294920 | tf_op jit(solution)/shard_map/ppermute | solution.py:478
  14.6 7.8 %collective-permute-start.1 = (bf16[3,128,128]{2,1,0:T(8,128)(2,1)S(1)}, bf16[3,128,128]{2,1,0:T(8,128)(2,1)S(1)}, u32[]{:S(2)}, u32[]{:S(2)}) collective-permute-start(bf16[3,128,128]{2,1,0:T(8,128)(2,1)S(1)} %get-tuple-element.21), channel_id=1, source_target_pairs={{0,2},{2,0},{4,6},{6,4},{8,10},{10,8},{12,14},{14,12},{16,18},{18,... | collective-permute-start | bytes 294920 | tf_op jit(solution)/shard_map/ppermute | solution.py:477
  23.1 0.2 copy.15.guide_head
  23.3 0.3 copy.14.main_head
  23.6 0.7 copy-done
  24.4 1.1 %prepare.1 = (bf16[2,128,64]{2,1,0:T(8,128)(2,1)S(1)}, f32[8,128]{1,0:T(8,128)S(1)}, f32[128,128]{1,0:T(8,128)S(1)}, f32[8,128]{1,0:T(8,128)S(1)}) custom-call(s32[1]{0:T(128)S(6)} %copy.16.step, s32[3]{0:T(128)S(1)} %pad_add_fusion.place, bf16[50,2,2560]{2,1,0:T(2,128)(2,1)S(1)} %copy-done, bf16[50,2,1024]{2,1,0:T(2,128)(2,1)S(1)} %copy-done.1, ...), custom_call_target="tpu_custom_call" | custom-call | tf_op jit(solution)/shard_map/prepare/pallas_call | solution.py:453
  25.4 8.1 %collective-permute-done.2.guide_across = bf16[3,128,128]{2,1,0:T(8,128)(2,1)S(1)} collective-permute-done((bf16[3,128,128]{2,1,0:T(8,128)(2,1)S(1)}, bf16[3,128,128]{2,1,0:T(8,128)(2,1)S(1)}, u32[]{:S(2)}, u32[]{:S(2)}) %collective-permute-start.2) | collective-permute-done | bytes 98336 | tf_op jit(solution)/shard_map/ppermute | solution.py:478
  33.6 0.1 collective-permute-done.1.guide_half
  33.7 2.0 %collective-permute-done.3.sibling = bf16[8,272,128]{2,1,0:T(8,128)(2,1)S(1)} collective-permute-done((bf16[8,272,128]{2,1,0:T(8,128)(2,1)S(1)}, bf16[8,272,128]{2,1,0:T(8,128)(2,1)S(1)}, u32[]{:S(2)}, u32[]{:S(2)}) %collective-permute-start.3) | collective-permute-done | bytes 557088 | tf_op jit(solution)/shard_map/ppermute | solution.py:485
  35.6 0.6 unpack.1
  36.2 1.3 %collective-permute-start.6 = (bf16[4,512,128]{2,1,0:T(8,128)(2,1)S(1)}, bf16[4,512,128]{2,1,0:T(8,128)(2,1)S(1)}, u32[]{:S(2)}, u32[]{:S(2)}) collective-permute-start(bf16[4,512,128]{2,1,0:T(8,128)(2,1)S(1)} %get-tuple-element.33.refs_0_), channel_id=1, source_target_pairs={{0,8},{1,33},{4,12},{5,37},{8,0},{9,41},{12,4},{13,45},{16,24},{17... | collective-permute-start | bytes 1572872 | tf_op jit(solution)/shard_map/ppermute | solution.py:386
  37.6 2.2 %collective-permute-start.5 = (bf16[4,512,128]{2,1,0:T(8,128)(2,1)S(1)}, bf16[4,512,128]{2,1,0:T(8,128)(2,1)S(1)}, u32[]{:S(2)}, u32[]{:S(2)}) collective-permute-start(bf16[4,512,128]{2,1,0:T(8,128)(2,1)S(1)} %get-tuple-element.33.refs_0_), channel_id=1, source_target_pairs={{0,4},{1,17},{4,8},{5,21},{8,12},{9,25},{12,0},{13,29},{16,20},{17... | collective-permute-start | bytes 1572872 | tf_op jit(solution)/shard_map/ppermute | solution.py:386
  39.8 2.8 %collective-permute-start.7 = (bf16[1024,128]{1,0:T(8,128)(2,1)S(1)}, bf16[1024,128]{1,0:T(8,128)(2,1)S(1)}, u32[]{:S(2)}, u32[]{:S(2)}) collective-permute-start(bf16[1024,128]{1,0:T(8,128)(2,1)S(1)} %get-tuple-element.32.queries), channel_id=1, source_target_pairs={{0,48},{1,13},{4,52},{5,1},{8,56},{9,5},{12,60},{13,9},{16,0},{17,... | collective-permute-start | bytes 786440 | tf_op jit(solution)/shard_map/ppermute | solution.py:386
  42.5 9.0 %collective-permute-done.7.queries = bf16[1024,128]{1,0:T(8,128)(2,1)S(1)} collective-permute-done((bf16[1024,128]{1,0:T(8,128)(2,1)S(1)}, bf16[1024,128]{1,0:T(8,128)(2,1)S(1)}, u32[]{:S(2)}, u32[]{:S(2)}) %collective-permute-start.7) | collective-permute-done | bytes 262176 | tf_op jit(solution)/shard_map/ppermute | solution.py:386
  51.5 1.5 %collective-permute-start.11 = (bf16[1024,128]{1,0:T(8,128)(2,1)S(1)}, bf16[1024,128]{1,0:T(8,128)(2,1)S(1)}, u32[]{:S(2)}, u32[]{:S(2)}) collective-permute-start(bf16[1024,128]{1,0:T(8,128)(2,1)S(1)} %get-tuple-element.32.queries), channel_id=1, source_target_pairs={{0,32},{1,9},{4,36},{5,13},{8,40},{9,1},{12,44},{13,5},{16,48},{17... | collective-permute-start | bytes 786440 | tf_op jit(solution)/shard_map/ppermute | solution.py:386
  53.0 2.6 %collective-permute-done.4.refs_1_ = bf16[4,512,128]{2,1,0:T(8,128)(2,1)S(1)} collective-permute-done((bf16[4,512,128]{2,1,0:T(8,128)(2,1)S(1)}, bf16[4,512,128]{2,1,0:T(8,128)(2,1)S(1)}, u32[]{:S(2)}, u32[]{:S(2)}) %collective-permute-start.4) | collective-permute-done | bytes 524320 | tf_op jit(solution)/shard_map/ppermute | solution.py:386
  55.6 3.0 %attend.5 = bf16[1056,128]{1,0:T(8,128)(2,1)S(1)} custom-call(bf16[1024,128]{1,0:T(8,128)(2,1)S(1)} %collective-permute-done.7.queries, bf16[4,512,128]{2,1,0:T(8,128)(2,1)S(1)} %get-tuple-element.33.refs_0_, bf16[4,512,128]{2,1,0:T(8,128)(2,1)S(1)} %collective-permute-done.4.refs_1_, bf16[4,512,128]{2,1,0:T(8,128)(2,1)S(1)} %collective-permute-done.5.refs_2_, ...), custom_call_target="tpu_custom_call" | custom-call | flops 1073741824 | bytes 2097152 | tf_op jit(solution)/shard_map/attend/pallas_call | solution.py:394
  58.6 2.4 %collective-permute-start.8 = (bf16[1056,128]{1,0:T(8,128)(2,1)S(1)}, bf16[1056,128]{1,0:T(8,128)(2,1)S(1)}, u32[]{:S(2)}, u32[]{:S(2)}) collective-permute-start(bf16[1056,128]{1,0:T(8,128)(2,1)S(1)} %attend.5), channel_id=1, source_target_pairs={{0,16},{1,5},{4,20},{5,9},{8,24},{9,13},{12,28},{13,1},{16,32},{17... | collective-permute-start | bytes 811016 | tf_op jit(solution)/shard_map/ppermute | solution.py:386
  61.0 3.0 %attend.6 = bf16[1056,128]{1,0:T(8,128)(2,1)S(1)} custom-call(bf16[1024,128]{1,0:T(8,128)(2,1)S(1)} %collective-permute-done.9.queries, bf16[4,512,128]{2,1,0:T(8,128)(2,1)S(1)} %get-tuple-element.33.refs_0_, bf16[4,512,128]{2,1,0:T(8,128)(2,1)S(1)} %collective-permute-done.4.refs_1_, bf16[4,512,128]{2,1,0:T(8,128)(2,1)S(1)} %collective-permute-done.5.refs_2_, ...), custom_call_target="tpu_custom_call" | custom-call | flops 1073741824 | bytes 2097152 | tf_op jit(solution)/shard_map/attend/pallas_call | solution.py:394
  64.0 1.3 %collective-permute-start.10 = (bf16[1056,128]{1,0:T(8,128)(2,1)S(1)}, bf16[1056,128]{1,0:T(8,128)(2,1)S(1)}, u32[]{:S(2)}, u32[]{:S(2)}) collective-permute-start(bf16[1056,128]{1,0:T(8,128)(2,1)S(1)} %attend.6), channel_id=1, source_target_pairs={{0,48},{1,13},{4,52},{5,1},{8,56},{9,5},{12,60},{13,9},{16,0},{17,... | collective-permute-start | bytes 811016 | tf_op jit(solution)/shard_map/ppermute | solution.py:386
  65.3 3.0 %attend.7 = bf16[1056,128]{1,0:T(8,128)(2,1)S(1)} custom-call(bf16[1024,128]{1,0:T(8,128)(2,1)S(1)} %collective-permute-done.11.queries, bf16[4,512,128]{2,1,0:T(8,128)(2,1)S(1)} %get-tuple-element.33.refs_0_, bf16[4,512,128]{2,1,0:T(8,128)(2,1)S(1)} %collective-permute-done.4.refs_1_, bf16[4,512,128]{2,1,0:T(8,128)(2,1)S(1)} %collective-permute-done.5.refs_2_, ...), custom_call_target="tpu_custom_call" | custom-call | flops 1073741824 | bytes 2097152 | tf_op jit(solution)/shard_map/attend/pallas_call | solution.py:394
  68.3 2.0 %collective-permute-start.12 = (bf16[1056,128]{1,0:T(8,128)(2,1)S(1)}, bf16[1056,128]{1,0:T(8,128)(2,1)S(1)}, u32[]{:S(2)}, u32[]{:S(2)}) collective-permute-start(bf16[1056,128]{1,0:T(8,128)(2,1)S(1)} %attend.7), channel_id=1, source_target_pairs={{0,32},{1,9},{4,36},{5,13},{8,40},{9,1},{12,44},{13,5},{16,48},{17... | collective-permute-start | bytes 811016 | tf_op jit(solution)/shard_map/ppermute | solution.py:386
  70.3 3.0 %attend.4.refs_0_ = bf16[1056,128]{1,0:T(8,128)(2,1)S(1)} custom-call(bf16[1024,128]{1,0:T(8,128)(2,1)S(1)} %get-tuple-element.32.queries, bf16[4,512,128]{2,1,0:T(8,128)(2,1)S(1)} %get-tuple-element.33.refs_0_, bf16[4,512,128]{2,1,0:T(8,128)(2,1)S(1)} %collective-permute-done.4.refs_1_, bf16[4,512,128]{2,1,0:T(8,128)(2,1)S(1)} %collective-permute-done.5.refs_2_, ...), custom_call_target="tpu_custom_call" | custom-call | flops 1073741824 | bytes 2097152 | tf_op jit(solution)/shard_map/attend/pallas_call | solution.py:394
  73.3 0.7 merge.1
  74.0 2.3 %collective-permute-done.12.part = bf16[1056,128]{1,0:T(8,128)(2,1)S(1)} collective-permute-done((bf16[1056,128]{1,0:T(8,128)(2,1)S(1)}, bf16[1056,128]{1,0:T(8,128)(2,1)S(1)}, u32[]{:S(2)}, u32[]{:S(2)}) %collective-permute-start.12) | collective-permute-done | bytes 270368 | tf_op jit(solution)/shard_map/ppermute | solution.py:386
  76.4 1.5 %combine.1 = bf16[16,48,128]{2,1,0:T(8,128)(2,1)S(1)} custom-call(s32[3]{0:T(128)S(1)} %pad_add_fusion.place, bf16[2,128,64]{2,1,0:T(8,128)(2,1)S(1)} %get-tuple-element.26.weights, f32[8,128]{1,0:T(8,128)S(1)} %get-tuple-element.27.scales, f32[1024,128]{1,0:T(8,128)S(1)} %get-tuple-element.34.former, f32[8,128]{1,0:T(8,128)S(1)} %get-tuple-element.35.former_level, ...), custom_call_target="tpu_custom_call" | custom-call | tf_op jit(solution)/shard_map/combine/pallas_call | solution.py:506
  77.9 11.8 %all_to_all.10.got = bf16[16,48,128]{2,1,0:T(8,128)(2,1)S(1)} all-to-all(bf16[16,48,128]{2,1,0:T(8,128)(2,1)S(1)} %combine.1), channel_id=1, replica_groups=mesh['zl'=4,'x'=4,'y'=4,'zh'=2,'core'=2] {'core','zh','zl'}, dimensions={0} | all-to-all | bytes 393216 | tf_op jit(solution)/shard_map/all_to_all | solution.py:514
  89.7 1.7 %final.1 = (f32[1,32,64]{2,1,0:T(8,128)}, f32[1,32,64]{2,1,0:T(8,128)}) custom-call(s32[1]{0:T(128)S(6)} %copy.16.step, s32[3]{0:T(128)S(1)} %pad_add_fusion.place, bf16[16,48,128]{2,1,0:T(8,128)(2,1)S(1)} %all_to_all.10.got, f32[128,128]{1,0:T(8,128)S(1)} %get-tuple-element.36.means, f32[8,128]{1,0:T(8,128)S(1)} %get-tuple-element.37.shifts, ...), custom_call_target="tpu_custom_call" | custom-call | tf_op jit(solution)/shard_map/final/pallas_call | solution.py:515
  (27 shorter events, 0.3 us)
Async XLA Ops:
  2.6 8.7 %copy-start.2 = (bf16[1,128,256]{2,1,0:T(8,128)(2,1)S(1)}, bf16[1,128,256]{2,1,0:T(8,128)(2,1)}, u32[]{:S(2)}) copy-start(bf16[1,128,256]{2,1,0:T(8,128)(2,1)} %gq.1) | copy-start | bytes 196612
  2.6 8.7 %copy-start.3 = (bf16[1,128,256]{2,1,0:T(8,128)(2,1)S(1)}, bf16[1,128,256]{2,1,0:T(8,128)(2,1)}, u32[]{:S(2)}) copy-start(bf16[1,128,256]{2,1,0:T(8,128)(2,1)} %gk.1) | copy-start | bytes 196612
  2.6 8.7 %copy-start.4 = (bf16[1,128,256]{2,1,0:T(8,128)(2,1)S(1)}, bf16[1,128,256]{2,1,0:T(8,128)(2,1)}, u32[]{:S(2)}) copy-start(bf16[1,128,256]{2,1,0:T(8,128)(2,1)} %gv.1) | copy-start | bytes 196612
  2.6 20.5 %copy-start.7 = (bf16[1024,64]{0,1:T(8,128)(2,1)S(1)}, bf16[1024,64]{0,1:T(8,128)(2,1)}, u32[]{:S(2)}) copy-start(bf16[1024,64]{0,1:T(8,128)(2,1)} %param.23) | copy-start | bytes 393220
  2.6 31.0 %all-to-all-start = ((bf16[8,272,128]{2,1,0:T(8,128)(2,1)}), bf16[8,272,128]{2,1,0:T(8,128)(2,1)S(1)}, u32[]{:S(2)}, u32[]{:S(2)}) async-start(bf16[8,272,128]{2,1,0:T(8,128)(2,1)} %pack.1), calls=%async_computation | async-start | bytes 1114112 | tf_op jit(solution)/shard_map/all_to_all | solution.py:479
  11.2 12.0 %copy-start.6 = (bf16[2560,64]{0,1:T(8,128)(2,1)S(1)}, bf16[2560,64]{0,1:T(8,128)(2,1)}, u32[]{:S(2)}) copy-start(bf16[2560,64]{0,1:T(8,128)(2,1)} %param.22) | copy-start | bytes 983044
  12.0 13.4 %collective-permute-start = (bf16[3,128,128]{2,1,0:T(8,128)(2,1)S(1)}, bf16[3,128,128]{2,1,0:T(8,128)(2,1)S(1)}, u32[]{:S(2)}, u32[]{:S(2)}) collective-permute-start(bf16[3,128,128]{2,1,0:T(8,128)(2,1)S(1)} %get-tuple-element.20.guide_own), channel_id=1, source_target_pairs={{1,0},{3,2},{5,4},{7,6},{9,8},{11,10},{13,12},{15,14},{17,16},{19,... | collective-permute-start | bytes 294920 | tf_op jit(solution)/shard_map/ppermute | solution.py:476
  13.3 20.3 %collective-permute-start.2 = (bf16[3,128,128]{2,1,0:T(8,128)(2,1)S(1)}, bf16[3,128,128]{2,1,0:T(8,128)(2,1)S(1)}, u32[]{:S(2)}, u32[]{:S(2)}) collective-permute-start(bf16[3,128,128]{2,1,0:T(8,128)(2,1)S(1)} %get-tuple-element.21), channel_id=1, source_target_pairs={{1,2},{3,0},{5,6},{7,4},{9,10},{11,8},{13,14},{15,12},{17,18},{19,... | collective-permute-start | bytes 294920 | tf_op jit(solution)/shard_map/ppermute | solution.py:478
  14.6 19.1 %collective-permute-start.1 = (bf16[3,128,128]{2,1,0:T(8,128)(2,1)S(1)}, bf16[3,128,128]{2,1,0:T(8,128)(2,1)S(1)}, u32[]{:S(2)}, u32[]{:S(2)}) collective-permute-start(bf16[3,128,128]{2,1,0:T(8,128)(2,1)S(1)} %get-tuple-element.21), channel_id=1, source_target_pairs={{0,2},{2,0},{4,6},{6,4},{8,10},{10,8},{12,14},{14,12},{16,18},{18,... | collective-permute-start | bytes 294920 | tf_op jit(solution)/shard_map/ppermute | solution.py:477
  23.3 1.0 %copy-start = (bf16[50,2,2560]{2,1,0:T(2,128)(2,1)S(1)}, bf16[50,2,2560]{2,1,0:T(2,128)(2,1)}, u32[]{:S(2)}) copy-start(bf16[50,2,2560]{2,1,0:T(2,128)(2,1)} %main_mod.1) | copy-start | bytes 1536004
  23.3 1.1 %copy-start.1 = (bf16[50,2,1024]{2,1,0:T(2,128)(2,1)S(1)}, bf16[50,2,1024]{2,1,0:T(2,128)(2,1)}, u32[]{:S(2)}) copy-start(bf16[50,2,1024]{2,1,0:T(2,128)(2,1)} %guide_mod.1) | copy-start | bytes 614404
  33.7 2.0 %collective-permute-start.3 = (bf16[8,272,128]{2,1,0:T(8,128)(2,1)S(1)}, bf16[8,272,128]{2,1,0:T(8,128)(2,1)S(1)}, u32[]{:S(2)}, u32[]{:S(2)}) collective-permute-start(bf16[8,272,128]{2,1,0:T(8,128)(2,1)S(1)} %all-to-all-done.got), channel_id=1, source_target_pairs={{0,1},{1,0},{2,3},{3,2},{4,5},{5,4},{6,7},{7,6},{8,9},{9,8},{10,11... | collective-permute-start | bytes 1671176 | tf_op jit(solution)/shard_map/ppermute | solution.py:485
  36.2 16.7 %collective-permute-start.6 = (bf16[4,512,128]{2,1,0:T(8,128)(2,1)S(1)}, bf16[4,512,128]{2,1,0:T(8,128)(2,1)S(1)}, u32[]{:S(2)}, u32[]{:S(2)}) collective-permute-start(bf16[4,512,128]{2,1,0:T(8,128)(2,1)S(1)} %get-tuple-element.33.refs_0_), channel_id=1, source_target_pairs={{0,8},{1,33},{4,12},{5,37},{8,0},{9,41},{12,4},{13,45},{16,24},{17... | collective-permute-start | bytes 1572872 | tf_op jit(solution)/shard_map/ppermute | solution.py:386
  37.6 15.5 %collective-permute-start.5 = (bf16[4,512,128]{2,1,0:T(8,128)(2,1)S(1)}, bf16[4,512,128]{2,1,0:T(8,128)(2,1)S(1)}, u32[]{:S(2)}, u32[]{:S(2)}) collective-permute-start(bf16[4,512,128]{2,1,0:T(8,128)(2,1)S(1)} %get-tuple-element.33.refs_0_), channel_id=1, source_target_pairs={{0,4},{1,17},{4,8},{5,21},{8,12},{9,25},{12,0},{13,29},{16,20},{17... | collective-permute-start | bytes 1572872 | tf_op jit(solution)/shard_map/ppermute | solution.py:386
  39.7 15.8 %collective-permute-start.4 = (bf16[4,512,128]{2,1,0:T(8,128)(2,1)S(1)}, bf16[4,512,128]{2,1,0:T(8,128)(2,1)S(1)}, u32[]{:S(2)}, u32[]{:S(2)}) collective-permute-start(bf16[4,512,128]{2,1,0:T(8,128)(2,1)S(1)} %get-tuple-element.33.refs_0_), channel_id=1, source_target_pairs={{0,12},{1,49},{4,0},{5,53},{8,4},{9,57},{12,8},{13,61},{16,28},{17... | collective-permute-start | bytes 1572872 | tf_op jit(solution)/shard_map/ppermute | solution.py:386
  39.8 11.8 %collective-permute-start.7 = (bf16[1024,128]{1,0:T(8,128)(2,1)S(1)}, bf16[1024,128]{1,0:T(8,128)(2,1)S(1)}, u32[]{:S(2)}, u32[]{:S(2)}) collective-permute-start(bf16[1024,128]{1,0:T(8,128)(2,1)S(1)} %get-tuple-element.32.queries), channel_id=1, source_target_pairs={{0,48},{1,13},{4,52},{5,1},{8,56},{9,5},{12,60},{13,9},{16,0},{17,... | collective-permute-start | bytes 786440 | tf_op jit(solution)/shard_map/ppermute | solution.py:386
  42.5 18.5 %collective-permute-start.9 = (bf16[1024,128]{1,0:T(8,128)(2,1)S(1)}, bf16[1024,128]{1,0:T(8,128)(2,1)S(1)}, u32[]{:S(2)}, u32[]{:S(2)}) collective-permute-start(bf16[1024,128]{1,0:T(8,128)(2,1)S(1)} %get-tuple-element.32.queries), channel_id=1, source_target_pairs={{0,16},{1,5},{4,20},{5,9},{8,24},{9,13},{12,28},{13,1},{16,32},{17... | collective-permute-start | bytes 786440 | tf_op jit(solution)/shard_map/ppermute | solution.py:386
  51.5 13.8 %collective-permute-start.11 = (bf16[1024,128]{1,0:T(8,128)(2,1)S(1)}, bf16[1024,128]{1,0:T(8,128)(2,1)S(1)}, u32[]{:S(2)}, u32[]{:S(2)}) collective-permute-start(bf16[1024,128]{1,0:T(8,128)(2,1)S(1)} %get-tuple-element.32.queries), channel_id=1, source_target_pairs={{0,32},{1,9},{4,36},{5,13},{8,40},{9,1},{12,44},{13,5},{16,48},{17... | collective-permute-start | bytes 786440 | tf_op jit(solution)/shard_map/ppermute | solution.py:386
  58.6 14.7 %collective-permute-start.8 = (bf16[1056,128]{1,0:T(8,128)(2,1)S(1)}, bf16[1056,128]{1,0:T(8,128)(2,1)S(1)}, u32[]{:S(2)}, u32[]{:S(2)}) collective-permute-start(bf16[1056,128]{1,0:T(8,128)(2,1)S(1)} %attend.5), channel_id=1, source_target_pairs={{0,16},{1,5},{4,20},{5,9},{8,24},{9,13},{12,28},{13,1},{16,32},{17... | collective-permute-start | bytes 811016 | tf_op jit(solution)/shard_map/ppermute | solution.py:386
  64.0 9.4 %collective-permute-start.10 = (bf16[1056,128]{1,0:T(8,128)(2,1)S(1)}, bf16[1056,128]{1,0:T(8,128)(2,1)S(1)}, u32[]{:S(2)}, u32[]{:S(2)}) collective-permute-start(bf16[1056,128]{1,0:T(8,128)(2,1)S(1)} %attend.6), channel_id=1, source_target_pairs={{0,48},{1,13},{4,52},{5,1},{8,56},{9,5},{12,60},{13,9},{16,0},{17,... | collective-permute-start | bytes 811016 | tf_op jit(solution)/shard_map/ppermute | solution.py:386
  68.3 8.0 %collective-permute-start.12 = (bf16[1056,128]{1,0:T(8,128)(2,1)S(1)}, bf16[1056,128]{1,0:T(8,128)(2,1)S(1)}, u32[]{:S(2)}, u32[]{:S(2)}) collective-permute-start(bf16[1056,128]{1,0:T(8,128)(2,1)S(1)} %attend.7), channel_id=1, source_target_pairs={{0,32},{1,9},{4,36},{5,13},{8,40},{9,1},{12,44},{13,5},{16,48},{17... | collective-permute-start | bytes 811016 | tf_op jit(solution)/shard_map/ppermute | solution.py:386
  77.9 11.8 %copy-start.5 = (f32[1,32,64]{2,1,0:T(8,128)S(1)}, f32[1,32,64]{2,1,0:T(8,128)}, u32[]{:S(2)}) copy-start(f32[1,32,64]{2,1,0:T(8,128)} %latents.1) | copy-start | bytes 24580
